TPU v7x, 32 devices: a whole 2x2x4 slice. The times are simulated.
32 devices in a mesh: item: 4 (over y, x), seq: 8 (over z, core).
Axes of the slice: x: 2, y: 2, z: 4, core: 2. Of those that a mesh axis runs over, the one named last changes fastest.
Arguments:
- tokens: bfloat16 [4, 1024, 768], P('item', 'seq'), may hold values from -6 to 6
- rand_blocks: int32 [16, 4, 12, 3], P(None, 'item'), may hold values from 0 to 15, all different within a row; in each aligned block of 12 rows (0 to 11, 12 to 23, ..., all dimensions but the last counted through in order) at most 3 rows name the same one
- w_query: bfloat16 [768, 768], replicated, may hold values from -0.21875 to 0.21875
- w_key: bfloat16 [768, 768], replicated, may hold values from -0.21875 to 0.21875
- w_value: bfloat16 [768, 768], replicated, may hold values from -0.21875 to 0.21875
- w_out: bfloat16 [768, 768], replicated, may hold values from -0.875 to 0.875
- w_up: bfloat16 [768, 3072], replicated, may hold values from -0.21875 to 0.21875
- w_down: bfloat16 [3072, 768], replicated, may hold values from -0.109375 to 0.109375
- bias_query: float32 [768], replicated, may hold values from -3 to 3
- bias_value: float32 [768], replicated, may hold values from -3 to 3
- bias_out: float32 [768], replicated, may hold values from -3 to 3
- bias_up: float32 [3072], replicated, may hold values from -3 to 3
- bias_down: float32 [768], replicated, may hold values from -3 to 3
- attn_gain: float32 [768], replicated, may hold values from 0.5 to 1.5
- attn_shift: float32 [768], replicated, may hold values from -2 to 2
- ffn_gain: float32 [768], replicated, may hold values from 0.5 to 1.5
- ffn_shift: float32 [768], replicated, may hold values from -2 to 2
- cotangent: bfloat16 [4, 1024, 768], P('item', 'seq'), may hold values from -6 to 6
Outputs:
- layer_out: bfloat16 [4, 1024, 768], P('item', 'seq')
- grad_tokens: bfloat16 [4, 1024, 768], P('item', 'seq')
- grad_w_query: float32 [768, 768], replicated
- grad_w_key: float32 [768, 768], replicated
- grad_w_value: float32 [768, 768], replicated
- grad_w_out: float32 [768, 768], replicated
- grad_w_up: float32 [768, 3072], replicated
- grad_w_down: float32 [3072, 768], replicated
- grad_bias_query: float32 [768], replicated
- grad_bias_value: float32 [768], replicated
- grad_bias_out: float32 [768], replicated
- grad_bias_up: float32 [3072], replicated
- grad_bias_down: float32 [768], replicated
- grad_attn_gain: float32 [768], replicated
- grad_attn_shift: float32 [768], replicated
- grad_ffn_gain: float32 [768], replicated
- grad_ffn_shift: float32 [768], replicated
Inputs may be any that keep to these rules, and one draw needn't show every extreme that they name: Each row rand_blocks[j, t, h, :] names 3 different key blocks. Among the rows of one query block of the 1 sequence of one index of item (all heads together), no key block is named more than 3 times, and in some such group one key block is named exactly 3 times.
All inputs are finite; a program needn't handle non-finite values.
Results may differ from a plain program's by a relative error of at most 0.015.
Values may be sent and summed in bfloat16 or wider, within the bound.
No kernel may reach another device: no remote copies, remote signals or barrier semaphores. Data moves between devices by JAX's collectives and lax.ppermute only.
A program may use at most 448 MiB of HBM per device.

v0:
```python
import jax
import jax.numpy as jnp
from jax import lax
from jax.sharding import PartitionSpec as P

HEADS = 12
HD = 64
BLOCK = 64
RAND = 3


epsilon = 1e-05


def from_root(shard, axis, root):
    mine = lax.axis_index(axis) == root
    return lax.psum(jnp.where(mine, shard, jnp.zeros_like(shard)), axis)


def extended(block, sides, width):
    for axis, dim in sides:
        count = lax.axis_size(axis)
        forward = [(i, i + 1) for i in range(count - 1)]
        backward = [(target, source) for source, target in forward]
        low = lax.ppermute(
            lax.slice_in_dim(block, block.shape[dim] - width, None, axis=dim), axis, forward
        )
        high = lax.ppermute(lax.slice_in_dim(block, 0, width, axis=dim), axis, backward)
        block = jnp.concatenate([low, block, high], axis=dim)
    return block


def joined(shard, axis, join):
    gathered = jax.tree.map(
        lambda a, kind: lax.all_gather(a.astype(kind), axis),
        shard,
        (jnp.bfloat16, jnp.bfloat16, jnp.bfloat16),
    )

    def take(source):
        return jax.tree.map(
            lambda a, own: lax.dynamic_index_in_dim(a, source, 0, False).astype(own.dtype),
            gathered,
            shard,
        )

    return lax.fori_loop(
        1, lax.axis_size(axis), lambda source, state: join(state, take(source)), take(0)
    )


def entering(shard, axis, combine, identity, reverse):
    count, position = (lax.axis_size(axis), lax.axis_index(axis))
    everything = jax.tree.map(
        lambda part, kind: lax.all_gather(part.astype(kind), axis),
        shard,
        jax.tree.map(lambda a: jnp.bfloat16 if a.dtype == jnp.float32 else a.dtype, shard),
    )
    start = jax.tree.map(
        lambda part, zero: jnp.broadcast_to(jnp.asarray(zero, part.dtype), part.shape),
        shard,
        identity,
    )

    def step(k, before):
        at = count - 1 - k if reverse else k
        reached = at > position if reverse else at < position
        new = combine(
            before, jax.tree.map(lambda part, own: part[at].astype(own.dtype), everything, shard)
        )
        return jax.tree.map(lambda a, b: jnp.where(reached, a, b), new, before)

    return lax.fori_loop(0, count, step, start)


def layer_norm(values, norm_gain, norm_bias):
    center = values - jnp.mean(values, axis=-1, keepdims=True)
    spread = jnp.mean(center * center, axis=-1, keepdims=True)
    return center * lax.rsqrt(spread + epsilon) * norm_gain + norm_bias


def gelu_exact(values):
    return jax.nn.gelu(values, approximate=False)


def dense_rows(left, right):
    return jnp.dot(left, right, preferred_element_type=jnp.float32)


def dense_left(left, right):
    return lax.dot_general(
        left, right, (((0,), (0,)), ((), ())), preferred_element_type=jnp.float32
    )


def dense_back(left, right):
    return lax.dot_general(
        left, right, (((1,), (1,)), ((), ())), preferred_element_type=jnp.float32
    )


def mixed_sum(form, left, right):
    return jnp.einsum(form, left, right, preferred_element_type=jnp.float32)


def exact_sum(form, left, right):
    return jnp.einsum(
        form, left, right, precision=lax.Precision.HIGHEST, preferred_element_type=jnp.float32
    )


def from_ends(first_part, last_part):
    head_part = from_root(first_part, "seq", 0)
    tail_part = from_root(last_part, "seq", lax.axis_size("seq") - 1)
    return (head_part, tail_part)


def merge_rows(left_part, right_part):
    left_peak, left_total, left_sum = left_part
    right_peak, right_total, right_sum = right_part
    new_peak = jnp.maximum(left_peak, right_peak)
    left_scale = jnp.exp(left_peak - new_peak)
    right_scale = jnp.exp(right_peak - new_peak)
    return (
        new_peak,
        left_total * left_scale + right_total * right_scale,
        left_sum * left_scale[..., None] + right_sum * right_scale[..., None],
    )


def add_pair(earlier_sum, later_sum):
    return (earlier_sum[0] + later_sum[0], earlier_sum[1] + later_sum[1])


def per_device(
    tokens,
    rand_blocks,
    w_query,
    w_key,
    w_value,
    w_out,
    w_up,
    w_down,
    bias_query,
    bias_value,
    bias_out,
    bias_up,
    bias_down,
    attn_gain,
    attn_shift,
    ffn_gain,
    ffn_shift,
    cotangent,
):
    seq_here, local_len, model_width = tokens.shape
    blocks_all = rand_blocks.shape[0]
    devices = lax.axis_size("seq")
    position = lax.axis_index("seq")
    per_dev = blocks_all // devices
    slot_cap = max(2, seq_here * HEADS * RAND * 4 // (3 * blocks_all))
    pair_width = 2 * HD
    lane_count = seq_here * HEADS * RAND
    slot_size = BLOCK * pair_width
    rows_here = seq_here * local_len
    score_scale = HD ** (-0.5)

    def to_heads(values):
        return values.reshape(seq_here, per_dev, BLOCK, HEADS, -1).transpose(0, 1, 3, 2, 4)

    def from_heads(values):
        return values.transpose(0, 1, 3, 2, 4).reshape(rows_here, -1)

    inputs = tokens.reshape(rows_here, model_width).astype(jnp.float32)
    normed = layer_norm(inputs, attn_gain, attn_shift).astype(jnp.bfloat16)
    queries = (dense_rows(normed, w_query) + bias_query).astype(jnp.bfloat16)
    key_rows = dense_rows(normed, w_key).astype(jnp.bfloat16)
    value_rows = (dense_rows(normed, w_value) + bias_value).astype(jnp.bfloat16)
    kv_tokens = jnp.stack(
        [
            key_rows.reshape(seq_here, local_len, HEADS, HD),
            value_rows.reshape(seq_here, local_len, HEADS, HD),
        ],
        axis=3,
    ).reshape(seq_here, local_len, 2 * model_width)
    padded = extended(kv_tokens, (("seq", 1),), BLOCK)
    pad_blocks = padded.reshape(seq_here, per_dev + 2, BLOCK, HEADS, pair_width)
    window = jnp.stack(
        [pad_blocks[:, 0:per_dev], pad_blocks[:, 1 : per_dev + 1], pad_blocks[:, 2 : per_dev + 2]],
        axis=2,
    )
    window = window.transpose(0, 1, 4, 2, 3, 5).reshape(
        seq_here, per_dev, HEADS, 3 * BLOCK, pair_width
    )
    packed = jnp.concatenate([queries.reshape(seq_here, local_len, model_width), kv_tokens], axis=2)
    head_pack, tail_pack = from_ends(packed[:, :BLOCK], packed[:, local_len - BLOCK :])
    global_pack = jnp.stack([head_pack, tail_pack], axis=1)
    global_query = (
        global_pack[..., :model_width]
        .reshape(seq_here, 2, BLOCK, HEADS, HD)
        .transpose(0, 3, 1, 2, 4)
        .reshape(seq_here, HEADS, 2 * BLOCK, HD)
    )
    global_kv = (
        global_pack[..., model_width:]
        .reshape(seq_here, 2, BLOCK, HEADS, pair_width)
        .transpose(0, 3, 1, 2, 4)
        .reshape(seq_here, HEADS, 2 * BLOCK, pair_width)
    )
    flat_req = rand_blocks.reshape(blocks_all, lane_count)
    block_ids = jnp.arange(blocks_all, dtype=jnp.int32)
    live_rows = (block_ids != 0) & (block_ids != blocks_all - 1)
    own_blocks = position * per_dev + jnp.arange(per_dev, dtype=jnp.int32)
    matches = (
        (flat_req[:, :, None] == own_blocks[None, None, :]) & live_rows[:, None, None]
    ).astype(jnp.int32)
    order_rank = jnp.cumsum(matches, axis=1) - matches
    slot_ids = jnp.arange(slot_cap, dtype=jnp.int32)
    chosen = matches[..., None] * (order_rank[..., None] == slot_ids).astype(jnp.int32)
    lane_ids = jnp.arange(lane_count, dtype=jnp.int32)
    source_rows = lane_ids // (HEADS * RAND) * (per_dev * HEADS) + lane_ids // RAND % HEADS
    slot_live = jnp.sum(chosen, axis=1)
    slot_rows = (
        jnp.sum(chosen * source_rows[None, :, None, None], axis=1)
        + (jnp.arange(per_dev, dtype=jnp.int32) * HEADS)[None, :, None]
    )
    kv_heads = (
        kv_tokens.reshape(seq_here, per_dev, BLOCK, HEADS, pair_width)
        .transpose(0, 1, 3, 2, 4)
        .reshape(seq_here * per_dev * HEADS, slot_size)
    )
    served = jnp.take(kv_heads, slot_rows.reshape(-1), axis=0) * slot_live.reshape(-1, 1).astype(
        jnp.bfloat16
    )
    served = served.reshape(devices, per_dev, per_dev, slot_cap, slot_size)
    replies = lax.all_to_all(served, "seq", split_axis=0, concat_axis=0, tiled=True)
    fetched = replies.transpose(1, 0, 2, 3, 4).reshape(per_dev * blocks_all * slot_cap, slot_size)
    my_blocks = lax.dynamic_slice_in_dim(flat_req, position * per_dev, per_dev, 0)
    same_key = (my_blocks[:, :, None] == my_blocks[:, None, :]) & (
        lane_ids[None, None, :] < lane_ids[None, :, None]
    )
    my_ranks = jnp.sum(same_key.astype(jnp.int32), axis=2)
    pick_rows = (
        jnp.arange(per_dev, dtype=jnp.int32)[:, None] * blocks_all + my_blocks
    ) * slot_cap + my_ranks
    rand_kv = jnp.take(fetched, pick_rows.reshape(-1), axis=0).reshape(
        per_dev, seq_here, HEADS, RAND, BLOCK, pair_width
    )
    rand_kv = rand_kv.transpose(1, 0, 2, 3, 4, 5).reshape(
        seq_here, per_dev, HEADS, RAND * BLOCK, pair_width
    )
    global_kv_all = jnp.broadcast_to(
        global_kv[:, None], (seq_here, per_dev, HEADS, 2 * BLOCK, pair_width)
    )
    keys_all = jnp.concatenate([window, global_kv_all, rand_kv], axis=3)
    list_keys = keys_all[..., :HD]
    list_values = keys_all[..., HD:]
    query_heads = to_heads(queries)
    scores = mixed_sum("sjhqd,sjhkd->sjhqk", query_heads, list_keys) * score_scale
    row_peak = jnp.max(scores, axis=-1, keepdims=True)
    weights = jnp.exp(scores - row_peak)
    row_total = jnp.sum(weights, axis=-1, keepdims=True)
    near_out = (
        mixed_sum("sjhqk,sjhkd->sjhqd", weights.astype(jnp.bfloat16), list_values) / row_total
    )
    local_heads = kv_tokens.reshape(seq_here, per_dev, BLOCK, HEADS, pair_width).transpose(
        0, 3, 1, 2, 4
    )
    local_keys = local_heads[..., :HD]
    local_values = local_heads[..., HD:]
    global_scores = mixed_sum("shqd,shjkd->shqjk", global_query, local_keys) * score_scale
    block_peak = jnp.max(global_scores, axis=-1, keepdims=True)
    global_weights = jnp.exp(global_scores - block_peak)
    local_top = jnp.max(block_peak, axis=3, keepdims=True)
    factor = jnp.exp(block_peak - local_top)
    local_total = jnp.sum(factor * jnp.sum(global_weights, axis=-1, keepdims=True), axis=(3, 4))
    local_sum = jnp.sum(
        factor * mixed_sum("shqjk,shjkd->shqjd", global_weights.astype(jnp.bfloat16), local_values),
        axis=3,
    )
    global_top, global_total, global_sum = joined(
        (local_top[..., 0, 0], local_total, local_sum), "seq", merge_rows
    )
    global_ctx = global_sum / global_total[..., None]
    global_lse = global_top + jnp.log(global_total)
    block_here = jnp.arange(per_dev, dtype=jnp.int32)
    head_mask = ((position == 0) & (block_here == 0))[None, :, None, None, None]
    tail_mask = ((position == devices - 1) & (block_here == per_dev - 1))[None, :, None, None, None]
    context = jnp.where(head_mask, global_ctx[:, None, :, :BLOCK], near_out)
    context = jnp.where(tail_mask, global_ctx[:, None, :, BLOCK:], context)
    context_rows = from_heads(context).astype(jnp.bfloat16)
    middle = inputs + (dense_rows(context_rows, w_out) + bias_out)
    normed_two = layer_norm(middle, ffn_gain, ffn_shift).astype(jnp.bfloat16)
    hidden = dense_rows(normed_two, w_up) + bias_up
    active = gelu_exact(hidden).astype(jnp.bfloat16)
    layer_out = (
        (middle + dense_rows(active, w_down) + bias_down)
        .astype(jnp.bfloat16)
        .reshape(seq_here, local_len, model_width)
    )
    cot_rows = cotangent.reshape(rows_here, model_width)
    cot_float = cot_rows.astype(jnp.float32)
    grad_w_down = dense_left(active, cot_rows)
    grad_bias_down = jnp.sum(cot_float, axis=0)
    d_active = dense_back(cot_rows, w_down)
    gelu_pull = jax.vjp(gelu_exact, hidden)[1]
    d_hidden = gelu_pull(d_active)[0].astype(jnp.bfloat16)
    grad_w_up = dense_left(normed_two, d_hidden)
    grad_bias_up = jnp.sum(d_hidden.astype(jnp.float32), axis=0)
    norm_pull_two = jax.vjp(layer_norm, middle, ffn_gain, ffn_shift)[1]
    d_middle_norm, grad_ffn_gain, grad_ffn_shift = norm_pull_two(dense_back(d_hidden, w_up))
    d_middle = cot_float + d_middle_norm
    d_attended = d_middle.astype(jnp.bfloat16)
    grad_w_out = dense_left(context_rows, d_attended)
    grad_bias_out = jnp.sum(d_attended.astype(jnp.float32), axis=0)
    d_context = dense_back(d_attended, w_out).astype(jnp.bfloat16)
    d_tokens = d_context.reshape(seq_here, local_len, model_width)
    head_grad, tail_grad = from_ends(d_tokens[:, :BLOCK], d_tokens[:, local_len - BLOCK :])
    d_heads = jnp.where(head_mask | tail_mask, jnp.zeros((), jnp.bfloat16), to_heads(d_context))
    d_float = d_heads.astype(jnp.float32)
    row_delta = jnp.sum(d_float * near_out, axis=-1, keepdims=True)
    scores = mixed_sum("sjhqd,sjhkd->sjhqk", query_heads, list_keys) * score_scale
    weights = jnp.exp(scores - row_peak)
    d_weights = mixed_sum("sjhqd,sjhkd->sjhqk", d_heads, list_values)
    d_scores = (weights / row_total * (d_weights - row_delta)).astype(jnp.bfloat16)
    d_query = mixed_sum("sjhqk,sjhkd->sjhqd", d_scores, list_keys) * score_scale
    d_list_keys = mixed_sum("sjhqk,sjhqd->sjhkd", d_scores, query_heads) * score_scale
    d_list_values = exact_sum(
        "sjhqk,sjhqd->sjhkd", weights.astype(jnp.bfloat16).astype(jnp.float32), d_float / row_total
    )
    d_kv = jnp.concatenate([d_list_keys, d_list_values], axis=-1)
    d_window = d_kv[:, :, :, : 3 * BLOCK].reshape(seq_here, per_dev, HEADS, 3, BLOCK, pair_width)
    keep_dims = ((0, 0), (0, 0), (0, 0))
    spread_sum = jnp.pad(d_window[:, :, :, 0], ((0, 0), (0, 2)) + keep_dims)
    spread_sum = spread_sum + jnp.pad(d_window[:, :, :, 1], ((0, 0), (1, 1)) + keep_dims)
    spread_sum = spread_sum + jnp.pad(d_window[:, :, :, 2], ((0, 0), (2, 0)) + keep_dims)
    own_grad = spread_sum[:, 1 : per_dev + 1]
    rim_grad = jnp.concatenate(
        [spread_sum[:, 0:1], spread_sum[:, per_dev + 1 : per_dev + 2]], axis=1
    )
    rim_grad = rim_grad.transpose(0, 1, 3, 2, 4).reshape(seq_here, 2 * BLOCK, 2 * model_width)
    back_rim = extended(rim_grad.astype(jnp.bfloat16), (("seq", 1),), BLOCK).astype(rim_grad.dtype)
    from_left = (
        back_rim[:, :BLOCK].reshape(seq_here, BLOCK, HEADS, pair_width).transpose(0, 2, 1, 3)
    )
    from_right = (
        back_rim[:, 3 * BLOCK :].reshape(seq_here, BLOCK, HEADS, pair_width).transpose(0, 2, 1, 3)
    )
    own_grad = own_grad.at[:, 0].add(from_left).at[:, per_dev - 1].add(from_right)
    global_part = jnp.sum(d_kv[:, :, :, 3 * BLOCK : 5 * BLOCK], axis=1)
    rand_part = d_kv[:, :, :, 5 * BLOCK :].reshape(seq_here, per_dev, HEADS, RAND, slot_size)
    rand_part = rand_part.transpose(1, 0, 2, 3, 4).reshape(per_dev * lane_count, slot_size)
    slot_grads = (
        jnp.zeros((per_dev * blocks_all * slot_cap, slot_size), jnp.float32)
        .at[pick_rows.reshape(-1)]
        .add(rand_part)
    )
    slot_grads = slot_grads.reshape(per_dev, devices, per_dev, slot_cap, slot_size).transpose(
        1, 0, 2, 3, 4
    )
    returned = lax.all_to_all(
        slot_grads.astype(jnp.bfloat16), "seq", split_axis=0, concat_axis=0, tiled=True
    ).astype(slot_grads.dtype)
    dump_row = seq_here * per_dev * HEADS
    targets = jnp.where(slot_live > 0, slot_rows, dump_row).reshape(-1)
    collected = (
        jnp.zeros((dump_row + 1, slot_size), jnp.float32)
        .at[targets]
        .add(returned.reshape(-1, slot_size))
    )
    own_grad = own_grad + collected[:dump_row].reshape(seq_here, per_dev, HEADS, BLOCK, pair_width)
    global_grad = (
        jnp.stack([head_grad, tail_grad], axis=1)
        .reshape(seq_here, 2, BLOCK, HEADS, HD)
        .transpose(0, 3, 1, 2, 4)
        .reshape(seq_here, HEADS, 2 * BLOCK, HD)
    )
    global_float = global_grad.astype(jnp.float32)
    global_delta = jnp.sum(global_float * global_ctx, axis=-1)
    global_scores = mixed_sum("shqd,shjkd->shqjk", global_query, local_keys) * score_scale
    global_weights = jnp.exp(global_scores - block_peak)
    coefficient = jnp.exp(block_peak - global_lse[..., None, None])
    global_probs = global_weights * coefficient
    global_dweights = mixed_sum("shqd,shjkd->shqjk", global_grad, local_values)
    global_dscores = (global_probs * (global_dweights - global_delta[..., None, None])).astype(
        jnp.bfloat16
    )
    d_global_query = mixed_sum("shqjk,shjkd->shqd", global_dscores, local_keys) * score_scale
    d_local_keys = mixed_sum("shqjk,shqd->shjkd", global_dscores, global_query) * score_scale
    d_local_values = exact_sum(
        "shqjk,shqd->shjkd",
        global_weights.astype(jnp.bfloat16).astype(jnp.float32) * coefficient,
        global_float,
    )
    own_grad = own_grad + jnp.concatenate([d_local_keys, d_local_values], axis=-1).transpose(
        0, 2, 1, 3, 4
    )
    head_terms = (d_global_query[:, :, :BLOCK], global_part[:, :, :BLOCK])
    tail_terms = (d_global_query[:, :, BLOCK:], global_part[:, :, BLOCK:])
    zero_terms = (jnp.zeros_like(head_terms[0]), jnp.zeros_like(head_terms[1]))
    head_rest = entering(head_terms, "seq", add_pair, zero_terms, True)
    tail_rest = entering(tail_terms, "seq", add_pair, zero_terms, False)
    head_full = add_pair(head_rest, head_terms)
    tail_full = add_pair(tail_rest, tail_terms)
    d_query = (
        d_query
        + jnp.where(head_mask, head_full[0][:, None], 0.0)
        + jnp.where(tail_mask, tail_full[0][:, None], 0.0)
    )
    own_grad = (
        own_grad
        + jnp.where(head_mask, head_full[1][:, None], 0.0)
        + jnp.where(tail_mask, tail_full[1][:, None], 0.0)
    )
    d_query_rows = from_heads(d_query).astype(jnp.bfloat16)
    kv_grad = own_grad.transpose(0, 1, 3, 2, 4).reshape(rows_here, HEADS, pair_width)
    d_key_rows = kv_grad[..., :HD].reshape(rows_here, model_width).astype(jnp.bfloat16)
    d_value_rows = kv_grad[..., HD:].reshape(rows_here, model_width).astype(jnp.bfloat16)
    grad_w_query = dense_left(normed, d_query_rows)
    grad_bias_query = jnp.sum(d_query_rows.astype(jnp.float32), axis=0)
    grad_w_key = dense_left(normed, d_key_rows)
    grad_w_value = dense_left(normed, d_value_rows)
    grad_bias_value = jnp.sum(d_value_rows.astype(jnp.float32), axis=0)
    d_normed = (
        dense_back(d_query_rows, w_query)
        + dense_back(d_key_rows, w_key)
        + dense_back(d_value_rows, w_value)
    )
    norm_pull_one = jax.vjp(layer_norm, inputs, attn_gain, attn_shift)[1]
    d_inputs_norm, grad_attn_gain, grad_attn_shift = norm_pull_one(d_normed)
    grad_tokens = (
        (d_middle + d_inputs_norm).astype(jnp.bfloat16).reshape(seq_here, local_len, model_width)
    )
    grad_list = [
        grad_w_query,
        grad_w_key,
        grad_w_value,
        grad_w_out,
        grad_w_up,
        grad_w_down,
        grad_bias_query,
        grad_bias_value,
        grad_bias_out,
        grad_bias_up,
        grad_bias_down,
        grad_attn_gain,
        grad_attn_shift,
        grad_ffn_gain,
        grad_ffn_shift,
    ]
    flattened = jnp.concatenate([member.reshape(-1) for member in grad_list])
    item_count = lax.axis_size("item")
    length_all = flattened.shape[0]
    stride_all = 128 * item_count * devices
    padded_len = (length_all + stride_all - 1) // stride_all * stride_all
    lead_pad = padded_len - length_all
    grad_grid = jnp.pad(flattened, (lead_pad, 0)).reshape(-1, 128)
    shared_rows = lax.psum_scatter(grad_grid, ("item", "seq"), scatter_dimension=0, tiled=True)
    summed = (
        lax.all_gather(shared_rows.astype(jnp.bfloat16), ("item", "seq"), axis=0, tiled=True)
        .astype(shared_rows.dtype)
        .reshape(-1)
    )
    results = []
    offset = lead_pad
    for member in grad_list:
        results.append(summed[offset : offset + member.size].reshape(member.shape))
        offset = offset + member.size
    return (
        layer_out,
        grad_tokens,
        results[0],
        results[1],
        results[2],
        results[3],
        results[4],
        results[5],
        results[6],
        results[7],
        results[8],
        results[9],
        results[10],
        results[11],
        results[12],
        results[13],
        results[14],
    )


def solution(mesh):
    placed = (
        P("item", "seq", None),
        P(None, "item", None, None),
        P(),
        P(),
        P(),
        P(),
        P(),
        P(),
        P(),
        P(),
        P(),
        P(),
        P(),
        P(),
        P(),
        P(),
        P(),
        P("item", "seq", None),
    )
    return jax.shard_map(
        per_device,
        mesh=mesh,
        in_specs=placed,
        out_specs=(
            P("item", "seq", None),
            P("item", "seq", None),
            P(),
            P(),
            P(),
            P(),
            P(),
            P(),
            P(),
            P(),
            P(),
            P(),
            P(),
            P(),
            P(),
            P(),
            P(),
        ),
        check_vma=False,
    )
```

profile of v0, /device:TPU:0, one launch (start us, length us, event | category | flops | bytes accessed | tf_op | source)
XLA Modules:
  0.0 1066.8 jit_solution(6723519332472985679)
XLA Ops:
  17.0 4.1 gather.13
  27.3 6.3 all-to-all-start
  36.0 3.8 collective-permute-start
  47.8 69.1 %all-reduce.13.cloned.1.call-done = (bf16[1,1,64,2304]{2,3,1,0:T(8,128)(2,1)}, bf16[1,1,64,2304]{2,3,1,0:T(8,128)(2,1)}) async-done(((bf16[1,1,64,2304]{2,3,1,0:T(8,128)(2,1)}, bf16[1,1,64,2304]{2,3,1,0:T(8,128)(2,1)}), (bf16[1,1,64,2304]{2,3,1,0:T(8,128)(2,1)}, bf16[1,1,64,2304]{2,3,1,0:T(8,128)(2,1)})) %all-reduce.13.cloned.1.call-update) | async-done | bytes 589840 | tf_op jit(solution)/shard_map/psum | solution.py:17
  131.2 14.1 %all-gather.7 = bf16[8,12,128]{2,1,0:T(8,128)(2,1)S(1)} all-gather(bf16[1,12,128]{2,1,0:T(8,128)(2,1)S(1)} %convert_bitcast_fusion.4), channel_id=2, replica_groups=mesh['item'=4,'seq'=8] {'seq'}, dimensions={0}, use_global_device_ids=true | all-gather | bytes 27648 | tf_op jit(solution)/shard_map/all_gather | solution.py:35
  145.2 14.0 %all-gather.8 = bf16[8,12,128]{2,1,0:T(8,128)(2,1)S(1)} all-gather(bf16[1,12,128]{2,1,0:T(8,128)(2,1)S(1)} %bitcast.475), channel_id=3, replica_groups=mesh['item'=4,'seq'=8] {'seq'}, dimensions={0}, use_global_device_ids=true | all-gather | bytes 27648 | tf_op jit(solution)/shard_map/all_gather | solution.py:35
  159.9 4.1 copy.314
  184.1 23.8 %while.55 = (s32[]{:T(128)}, f32[1,12,128]{2,1,0:T(8,128)S(1)}, f32[1,12,128]{2,1,0:T(8,128)S(1)}, f32[1,12,128,64]{3,2,1,0:T(8,128)S(1)}, bf16[8,1,12,128]{3,2,...) while((s32[]{:T(128)}, f32[1,12,128]{2,1,0:T(8,128)S(1)}, ...), condition=%wide.region_10.11_spmd, body=%wide.region_9.10_spmd.sunk | while | flops 408581 | bytes 1852571 | solution.py:47
  215.4 8.2 multiply_convert_fusion.1
  234.7 5.7 convolution_bitcast_fusion.1
  245.5 4.2 multiply_convert_fusion
  258.7 6.6 pad_maximum_fusion
  265.3 3.4 copy.337
  278.6 3.7 collective-permute-start.2
  282.4 3.4 copy.345
  285.7 3.4 reshape.1244
  289.1 6.2 scatter_custom_fusion
  298.6 4.1 convert_element_type.532
  302.6 4.6 copy.346
  307.3 4.4 all-to-all-start.1
  314.7 3.3 reshape.1201
  320.7 5.9 copy.381
  326.6 5.2 fusion.90
  331.8 10.8 %reshape.1203 = f32[2359296]{0:T(1024)} reshape(f32[3072,768]{1,0:T(8,128)} %fusion.90) | data formatting | bytes 18874368 | tf_op jit(solution)/shard_map/reshape | solution.py:450
  352.2 32.6 %all-gather.3 = bf16[8,12,64,64]{3,2,1,0:T(8,128)(2,1)} all-gather(bf16[1,12,64,64]{3,2,1,0:T(8,128)(2,1)S(1)} %copy.326), channel_id=5, replica_groups=mesh['item'=4,'seq'=8] {'seq'}, dimensions={0}, use_global_device_ids=true | all-gather | bytes 884736 | tf_op jit(solution)/shard_map/all_gather | solution.py:55
  385.8 20.7 %all-gather.5 = bf16[8,12,64,64]{3,2,1,0:T(8,128)(2,1)} all-gather(bf16[1,12,64,64]{3,2,1,0:T(8,128)(2,1)S(1)} %copy.332), channel_id=7, replica_groups=mesh['item'=4,'seq'=8] {'seq'}, dimensions={0}, use_global_device_ids=true | all-gather | bytes 884736 | tf_op jit(solution)/shard_map/all_gather | solution.py:55
  414.1 18.6 %while.56 = (s32[]{:T(128)}, f32[1,12,64,64]{3,2,1,0:T(8,128)S(1)}, f32[1,12,64,128]{3,2,1,0:T(8,128)S(1)}, s32[]{:T(128)}, bf16[8,1,12,64,64]{4,3,2,1,0:T(8,128...) while((s32[]{:T(128)}, f32[1,12,64,64]{3,2,1,0:T(8,128)S(1)}, ...), condition=%wide.region_27.28_spmd.clone, body=%wide.region_26.27_spmd.clone.sunk | while | flops 589832 | bytes 1474745 | solution.py:73
  432.8 18.4 %while.57 = (s32[]{:T(128)}, f32[1,12,64,64]{3,2,1,0:T(8,128)S(1)}, f32[1,12,64,128]{3,2,1,0:T(8,128)S(1)}, s32[]{:T(128)}, bf16[8,1,12,64,64]{4,3,2,1,0:T(8,128...) while((s32[]{:T(128)}, f32[1,12,64,64]{3,2,1,0:T(8,128)S(1)}, ...), condition=%wide.region_29.30_spmd.clone, body=%wide.region_28.29_spmd.clone.sunk | while | flops 589828 | bytes 1474683 | solution.py:73
  463.7 4.2 copy.348
  467.9 5.2 reshape.1252
  473.1 6.7 scatter_custom_fusion.1
  494.7 3.2 constant_dynamic-update-slice_fusion.4
  504.5 3.4 constant_dynamic-update-slice_fusion.18
  512.0 9.7 constant_dynamic-update-slice_fusion.15
  521.8 3.8 constant_dynamic-update-slice_fusion.14
  537.2 20.8 %pad_bitcast_fusion = f32[55392,128]{1,0:T(8,128)} fusion(f32[7087104]{0:T(1024)} %constant_dynamic-update-slice_fusion.5), kind=kLoop, calls=%fused_computation.19 | loop fusion | bytes 56709120 | tf_op jit(solution)/shard_map/reshape | solution.py:456
  558.0 305.8 %fusion = f32[1744,128]{1,0:T(8,128)S(1)} fusion(f32[55392,128]{1,0:T(8,128)} %pad_bitcast_fusion), kind=kCustom, calls=%all-reduce-scatter | all-reduce-scatter fusion | flops 7143425 | bytes 29253632
  866.2 3.4 concatenate.45
  871.5 3.8 fusion.38
  875.4 103.6 %all-gather.21.cloned.1.call-done = bf16[32,1731,128]{2,1,0:T(8,128)(2,1)} async-done(((bf16[1,1731,128]{2,1,0:T(8,128)(2,1)}), bf16[32,1731,128]{2,1,0:T(8,128)(2,1)}) %all-gather.21.cloned.1.call-update) | async-done | bytes 14180368 | tf_op jit(solution)/shard_map/all_gather | solution.py:459
  978.9 22.9 %reshape.1278 = f32[55392,128]{1,0:T(8,128)} reshape(bf16[32,1731,128]{2,1,0:T(8,128)(2,1)} %all-gather.21.cloned.1.call-done) | data formatting | bytes 42541056 | tf_op jit(solution)/shard_map/convert_element_type | solution.py:460
  1001.9 6.9 fusion.128
  1008.8 14.2 %fusion.127 = (f32[18432,128]{1,0:T(8,128)}, f32[18432,128]{1,0:T(8,128)}) fusion(f32[55392,128]{1,0:T(8,128)} %reshape.1278), kind=kLoop, calls=%fused_computation.308 | loop fusion | bytes 37748736 | tf_op jit(solution)/shard_map/slice | solution.py:466
  1025.7 3.4 reshape.1205
  1029.0 3.4 reshape.1206
  1032.4 3.4 reshape.1207
  1037.4 10.9 %reshape.1209 = f32[768,3072]{1,0:T(8,128)} reshape(f32[18432,128]{1,0:T(8,128)} %get-tuple-element.688) | data formatting | bytes 18874368 | tf_op jit(solution)/shard_map/reshape | solution.py:466
  1048.3 11.3 %reshape.1210 = f32[3072,768]{1,0:T(8,128)} reshape(f32[18432,128]{1,0:T(8,128)} %get-tuple-element.687) | data formatting | bytes 18874368 | tf_op jit(solution)/shard_map/reshape | solution.py:466
  (500 shorter events, 248.0 us)
Async XLA Ops:
  10.4 29.4 %copy-start.65 = (f32[128]{0:T(128)}, f32[128]{0:T(128)S(1)}, u32[]{:S(2)}) copy-start(f32[128]{0:T(128)S(1)} %broadcast_multiply_fusion.1) | copy-start | bytes 1540
  10.7 29.1 %copy-start.70 = (f32[128]{0:T(128)}, f32[128]{0:T(128)S(1)}, u32[]{:S(2)}) copy-start(f32[128]{0:T(128)S(1)} %fusion.108) | copy-start | bytes 1540
  12.9 107.5 %copy-start.10 = (bf16[1,2,64,12,128]{4,2,1,3,0:T(8,128)(2,1)}, bf16[1,2,64,12,128]{4,2,1,3,0:T(8,128)(2,1)S(1)}, u32[]{:S(2)}) copy-start(bf16[1,2,64,12,128]{4,2,1,3,0:T(8,128)(2,1)S(1)} %reshape_reshape.4) | copy-start | bytes 1179652
  27.3 132.6 %all-to-all-start = ((bf16[8,2,2,3,8192]{4,2,3,1,0:T(2,128)(2,1)}), bf16[8,2,2,3,8192]{4,2,3,1,0:T(2,128)(2,1)}, u32[]{:S(2)}, u32[]{:S(2)}) async-start(bf16[8,2,2,3,8192]{4,2,3,1,0:T(2,128)(2,1)} %copy.313), calls=%async_computation | async-start | bytes 3145728 | tf_op jit(solution)/shard_map/all_to_all | solution.py:235
  33.6 6.2 copy-start.87
  33.6 83.3 %all-reduce.13.cloned.1.call-start = ((), (), s32[]{:S(2)}) async-start(), calls=%async_computation.7 | async-start | bytes 2359296 | tf_op jit(solution)/shard_map/psum | solution.py:17
  34.7 87.2 %collective-permute-start.1 = (bf16[1,64,1536]{1,2,0:T(8,128)(2,1)}, bf16[1,64,1536]{1,2,0:T(8,128)(2,1)}, u32[]{:S(2)}, u32[]{:S(2)}) collective-permute-start(bf16[1,64,1536]{1,2,0:T(8,128)(2,1)} %get-tuple-element.722), channel_id=1, source_target_pairs={{1,0},{2,1},{3,2},{4,3},{5,4},{6,5},{7,6},{9,8},{10,9},{11,10},{12... | collective-permute-start | bytes 589832 | tf_op jit(solution)/shard_map/ppermute | solution.py:28
  36.0 85.9 %collective-permute-start = (bf16[1,64,1536]{1,2,0:T(8,128)(2,1)}, bf16[1,64,1536]{1,2,0:T(8,128)(2,1)}, u32[]{:S(2)}, u32[]{:S(2)}) collective-permute-start(bf16[1,64,1536]{1,2,0:T(8,128)(2,1)} %get-tuple-element.721), channel_id=1, source_target_pairs={{0,1},{1,2},{2,3},{3,4},{4,5},{5,6},{6,7},{8,9},{9,10},{10,11},{11... | collective-permute-start | bytes 589832 | tf_op jit(solution)/shard_map/ppermute | solution.py:25
  42.9 140.0 %all-gather.15.cloned.1.call-start = ((), (), s32[]{:S(2)}) async-start(), calls=%async_computation.2 | async-start | bytes 1769472 | tf_op jit(solution)/shard_map/all_gather | solution.py:35
  47.2 72.1 %copy-start.85 = (s32[72]{0:T(128)}, s32[72]{0:T(128)S(1)}, u32[]{:S(2)}) copy-start(s32[72]{0:T(128)S(1)} %fusion.106) | copy-start | bytes 868
  121.6 221.6 %all-reduce.11.cloned.1.call-start = ((), (), s32[]{:S(2)}) async-start(), calls=%async_computation.6 | async-start | bytes 1048576 | tf_op jit(solution)/shard_map/psum | solution.py:17
  145.2 14.0 %copy-start.52 = (bf16[8,12,128]{2,1,0:T(8,128)(2,1)}, bf16[8,12,128]{2,1,0:T(8,128)(2,1)S(1)}, u32[]{:S(2)}) copy-start(bf16[8,12,128]{2,1,0:T(8,128)(2,1)S(1)} %all-gather.7) | copy-start | bytes 73732
  213.2 10.4 slice-start.5
  213.2 12.9 %slice-start.3 = ((s8[4718592]{0:T(1024)(128)(4,1)}), s8[4194304]{0:T(1024)(128)(4,1)S(1)}, s32[]{:S(2)}) async-start(s8[4718592]{0:T(1024)(128)(4,1)} %bitcast.440), calls=%async_computation.11 | async-start | bytes 8388608
  215.1 13.3 %copy-start.72 = (f32[128]{0:T(128)}, f32[128]{0:T(128)S(1)}, u32[]{:S(2)}) copy-start(f32[128]{0:T(128)S(1)} %broadcast_multiply_fusion) | copy-start | bytes 1540
  215.4 13.1 %copy-start.75 = (f32[128]{0:T(128)}, f32[128]{0:T(128)S(1)}, u32[]{:S(2)}) copy-start(f32[128]{0:T(128)S(1)} %fusion.109) | copy-start | bytes 1540
  215.4 8.2 slice-start.6
  215.4 8.2 copy-start.33
  215.4 10.7 %slice-start.4 = ((s8[4718592]{0:T(1024)(128)(4,1)}), s8[524288]{0:T(1024)(128)(4,1)S(1)}, s32[]{:S(2)}) async-start(s8[4718592]{0:T(1024)(128)(4,1)} %bitcast.440), calls=%async_computation.12 | async-start | bytes 1048576
  234.7 5.7 copy-start.27
  234.7 5.7 copy-start.31
  234.7 5.7 copy-start.78
  245.5 4.2 copy-start.23
  256.7 157.4 %all-gather.17.cloned.1.call-start = ((), (), s32[]{:S(2)}) async-start(), calls=%async_computation.3 | async-start | bytes 1769472 | tf_op jit(solution)/shard_map/all_gather | solution.py:55
  277.3 131.9 %collective-permute-start.3 = (bf16[1,64,1536]{2,1,0:T(8,128)(2,1)}, bf16[1,64,1536]{2,1,0:T(8,128)(2,1)}, u32[]{:S(2)}, u32[]{:S(2)}) collective-permute-start(bf16[1,64,1536]{2,1,0:T(8,128)(2,1)} %get-tuple-element.716), channel_id=1, source_target_pairs={{1,0},{2,1},{3,2},{4,3},{5,4},{6,5},{7,6},{9,8},{10,9},{11,10},{12... | collective-permute-start | bytes 589832 | tf_op jit(solution)/shard_map/ppermute | solution.py:28
  278.6 130.7 %collective-permute-start.2 = (bf16[1,64,1536]{2,1,0:T(8,128)(2,1)}, bf16[1,64,1536]{2,1,0:T(8,128)(2,1)}, u32[]{:S(2)}, u32[]{:S(2)}) collective-permute-start(bf16[1,64,1536]{2,1,0:T(8,128)(2,1)} %get-tuple-element.715), channel_id=1, source_target_pairs={{0,1},{1,2},{2,3},{3,4},{4,5},{5,6},{6,7},{8,9},{9,10},{10,11},{11... | collective-permute-start | bytes 589832 | tf_op jit(solution)/shard_map/ppermute | solution.py:25
  307.3 4.7 copy-start.39
  307.3 154.1 %all-to-all-start.1 = ((bf16[8,2,2,3,8192]{4,2,3,1,0:T(2,128)(2,1)}), bf16[8,2,2,3,8192]{4,2,3,1,0:T(2,128)(2,1)}, u32[]{:S(2)}, u32[]{:S(2)}) async-start(bf16[8,2,2,3,8192]{4,2,3,1,0:T(2,128)(2,1)} %copy.346), calls=%async_computation.1 | async-start | bytes 3145728 | tf_op jit(solution)/shard_map/all_to_all | solution.py:360
  311.7 121.1 %all-gather.19.cloned.1.call-start = ((), (), s32[]{:S(2)}) async-start(), calls=%async_computation.4 | async-start | bytes 1769472 | tf_op jit(solution)/shard_map/all_gather | solution.py:55
  320.7 6.0 copy-start.20
  320.7 5.9 copy-start.34
  331.8 10.8 %copy-start.48 = (f32[12,128,2]{1,2,0:T(2,128)S(1)}, f32[12,128,2]{1,2,0:T(2,128)}, u32[]{:S(2)}) copy-start(f32[12,128,2]{1,2,0:T(2,128)} %copy-done.47) | copy-start | bytes 36868
  343.2 635.7 %all-gather.21.cloned.1.call-start = ((), (), s32[]{:S(2)}) async-start(), calls=%async_computation.5 | async-start | bytes 14665728 | tf_op jit(solution)/shard_map/all_gather | solution.py:459
  352.2 54.4 %copy-start.37 = (bf16[12,128,64,1]{1,2,0,3:T(8,128)(2,1)S(1)}, bf16[12,128,64,1]{1,2,0,3:T(8,128)(2,1)}, u32[]{:S(2)}) copy-start(bf16[12,128,64,1]{1,2,0,3:T(8,128)(2,1)} %copy-done.36) | copy-start | bytes 589828
  385.8 21.9 %copy-start.50 = (f32[12,128,2]{1,2,0:T(2,128)S(1)}, f32[12,128,2]{1,2,0:T(2,128)}, u32[]{:S(2)}) copy-start(f32[12,128,2]{1,2,0:T(2,128)} %copy-done.47) | copy-start | bytes 36868
  385.8 21.9 %copy-start.59 = (f32[12,128,2]{1,2,0:T(2,128)S(1)}, f32[12,128,2]{1,2,0:T(2,128)}, u32[]{:S(2)}) copy-start(f32[12,128,2]{1,2,0:T(2,128)} %subtract_exponential_fusion.3) | copy-start | bytes 36868
  414.1 18.7 %copy-start.6 = (f32[1,12,64,64]{3,2,1,0:T(8,128)S(1)}, f32[1,12,64,64]{3,2,1,0:T(8,128)}, u32[]{:S(2)}) copy-start(f32[1,12,64,64]{3,2,1,0:T(8,128)} %custom-call.2) | copy-start | bytes 589828
  414.1 18.7 %copy-start.7 = (f32[1,12,64,128]{3,2,1,0:T(8,128)S(1)}, f32[1,12,64,128]{3,2,1,0:T(8,128)}, u32[]{:S(2)}) copy-start(f32[1,12,64,128]{3,2,1,0:T(8,128)} %custom-call.3) | copy-start | bytes 1179652
  510.4 11.3 %slice-start = ((s8[9437184]{0:T(1024)(128)(4,1)}), s8[4194304]{0:T(1024)(128)(4,1)S(1)}, s32[]{:S(2)}) async-start(s8[9437184]{0:T(1024)(128)(4,1)} %bitcast.426), calls=%async_computation.8 | async-start | bytes 8388608
  512.0 9.7 slice-start.1
  512.0 9.7 slice-start.2
  521.7 6.4 copy-start.69
  521.7 7.7 copy-start.74
  521.7 12.9 %copy-start.68 = (f32[768]{0:T(1024)S(1)}, f32[768]{0:T(1024)}, u32[]{:S(2)}) copy-start(f32[768]{0:T(1024)} %get-tuple-element.614) | copy-start | bytes 9220
  521.7 14.2 %copy-start.67 = (f32[768]{0:T(1024)S(1)}, f32[768]{0:T(1024)}, u32[]{:S(2)}) copy-start(f32[768]{0:T(1024)} %get-tuple-element.620) | copy-start | bytes 9220
  863.8 7.7 copy-start.21
  863.8 7.7 copy-start.79
  863.9 2.4 collective-permute-start.4
  (60 other events, 124.6 us)
Sparse Core Ops, SparseCore 0:
  43.0 73.8 all-reduce.12
  121.8 24.2 all-gather.14
  256.8 55.1 all-reduce.10
  314.2 44.0 all-gather.16
  359.8 29.6 all-gather.18
  871.6 107.2 all-gather.20
where the time goes:
time: 1080 us; the launch traced here: 1070 us
  blocking collectives  387 us (36%)
  local copies, waits for them, and re-layouts  293 us (27%)
  waiting for transfers between devices  174 us (16%)
  other arithmetic  111 us (10%)
  matrix products  61.5 us (6%)
  starting transfers between devices  22.9 us (2%)
  between operations  16.2 us (2%)
    unnamed x1, blocking collectives  306 us
    all_gather x1, waiting for transfers between devices, per_device(): lax.all_gather(shared_rows.astype(jnp.bfloat16), ('item', 'seq'), axis=0,...  104 us
    psum x2, waiting for transfers between devices, from_root(): return lax.psum(jnp.where(mine, shard, jnp.zeros_like(shard)), axis)  69.1 us
    unnamed x219, local copies, waits for them, and re-layouts  61.9 us
    all_gather x2, blocking collectives, entering(): lax.all_gather(part.astype(kind), axis)  53.3 us
    select_n x32, other arithmetic, step(): return jax.tree.map(lambda a, b: jnp.where(reached, a, b), new, before)  36.3 us
    reshape x6, local copies, waits for them, and re-layouts, per_device(): results.append(summed[offset:offset + member.size].reshape(member.shape))  33.8 us
    all_gather x2, blocking collectives, joined(): lax.all_gather(a.astype(kind), axis)  28.1 us
  transfers between devices with their start and end apart: 13, of which 3 were waited for; matrix products, arithmetic and copies ran while one was open for 17% of the time, Pallas kernels for 0%

commit v1 on v0

--- a/solution.py
+++ b/solution.py
@@ -1,6 +1,10 @@
+import functools
+
 import jax
 import jax.numpy as jnp
 from jax import lax
+from jax.experimental import pallas as pl
+from jax.experimental.pallas import tpu as pltpu
 from jax.sharding import PartitionSpec as P
 
 HEADS = 12
@@ -132,7 +136,7 @@
     return (earlier_sum[0] + later_sum[0], earlier_sum[1] + later_sum[1])
 
 
-def per_device(
+def general_device(
     tokens,
     rand_blocks,
     w_query,
@@ -486,6 +490,1210 @@
     )
 
 
+LANES = 128
+GROUP = 4
+FAR = -1e30
+BF = jnp.bfloat16
+F32 = jnp.float32
+VMEM_ASK = 56 * 1024 * 1024
+
+
+def over_z(value, step):
+    count = lax.axis_size("seq")
+    return lax.ppermute(value, "seq", [(i, i ^ (2 * step)) for i in range(count)])
+
+
+def over_core(value):
+    count = lax.axis_size("seq")
+    return lax.ppermute(value, "seq", [(i, i ^ 1) for i in range(count)])
+
+
+def over_item(value, step):
+    count = lax.axis_size("item")
+    return lax.ppermute(value, "item", [(i, i ^ step) for i in range(count)])
+
+
+def in_order(parts, place):
+    low = (place & 1) == 1
+    high = (place & 2) == 2
+    p0, p1, p2, p3 = parts
+    p0, p1, p2, p3 = (
+        jnp.where(low, p1, p0),
+        jnp.where(low, p0, p1),
+        jnp.where(low, p3, p2),
+        jnp.where(low, p2, p3),
+    )
+    return [
+        jnp.where(high, p2, p0),
+        jnp.where(high, p3, p1),
+        jnp.where(high, p0, p2),
+        jnp.where(high, p1, p3),
+    ]
+
+
+def params(**more):
+    return pltpu.CompilerParams(vmem_limit_bytes=VMEM_ASK, **more)
+
+
+def vmem(count):
+    return [pl.BlockSpec(memory_space=pltpu.VMEM)] * count
+
+
+def cost(flops, moved, special=0):
+    return pl.CostEstimate(flops=flops, bytes_accessed=moved, transcendentals=special)
+
+
+LIGHT = cost(10**6, 10**5)
+
+
+def dot_nn(left, right):
+    return lax.dot_general(left, right, (((1,), (0,)), ((), ())), preferred_element_type=F32)
+
+
+def dot_tn(left, right):
+    return lax.dot_general(left, right, (((0,), (0,)), ((), ())), preferred_element_type=F32)
+
+
+def dot_nt(left, right):
+    return lax.dot_general(left, right, (((1,), (1,)), ((), ())), preferred_element_type=F32)
+
+
+def attend_kernel(heads, *refs):
+    own, other, mult_ref = refs[:4], refs[4:8], refs[8]
+    ctx_refs, out_ref, lse_ref = refs[9:13], refs[13], refs[14]
+    width = heads * HD
+    for h in range(heads):
+        low = h * HD
+        query = jnp.concatenate([r[low : low + HD, :] for r in own], axis=1)
+        key = jnp.concatenate(
+            [r[width + low : width + low + HD, :] for r in own]
+            + [r[low : low + HD, :] for r in other],
+            axis=1,
+        )
+        value = jnp.concatenate(
+            [r[2 * width + low : 2 * width + low + HD, :] for r in own]
+            + [r[width + low : width + low + HD, :] for r in other],
+            axis=1,
+        )
+        rows, lanes = key.shape[1], query.shape[1]
+        scores = dot_tn(key, query) * (HD**-0.5)
+        scores = scores.reshape(rows // BLOCK, BLOCK, lanes)
+        mult = mult_ref[h][:, None, :]
+        scores = jnp.where(mult > 0.0, scores, FAR)
+        peak = jnp.max(jnp.max(scores, axis=0), axis=0, keepdims=True)
+        weights = jnp.exp(scores - peak[None]) * mult
+        total = jnp.sum(jnp.sum(weights, axis=0), axis=0, keepdims=True)
+        packed = weights.astype(BF).reshape(rows, lanes)
+        out = dot_nn(value, packed) / total
+        out_ref[low : low + HD, :] = out
+        lse_ref[h] = peak + jnp.log(total)
+        rounded = out.astype(BF)
+        for k in range(4):
+            ctx_refs[k][low : low + HD, :] = rounded[:, k * LANES : (k + 1) * LANES]
+
+
+def attend_back_kernel(heads, *refs):
+    own, other, mult_ref, out_ref, lse_ref = refs[:4], refs[4:8], refs[8], refs[9], refs[10]
+    grad_refs = refs[11:14]
+    dq_ref, dkv_ref, far_ref = refs[14:17]
+    width = heads * HD
+    for h in range(heads):
+        low = h * HD
+        query = jnp.concatenate([r[low : low + HD, :] for r in own], axis=1)
+        key = jnp.concatenate(
+            [r[width + low : width + low + HD, :] for r in own]
+            + [r[low : low + HD, :] for r in other],
+            axis=1,
+        )
+        value = jnp.concatenate(
+            [r[2 * width + low : 2 * width + low + HD, :] for r in own]
+            + [r[width + low : width + low + HD, :] for r in other],
+            axis=1,
+        )
+        grad = jnp.concatenate(
+            [r[low : low + HD, :] for r in grad_refs]
+            + [grad_refs[2][width + low : width + low + HD, :]],
+            axis=1,
+        )
+        rows, lanes = key.shape[1], query.shape[1]
+        scale = HD**-0.5
+        scores = dot_tn(key, query) * scale
+        scores = scores.reshape(rows // BLOCK, BLOCK, lanes)
+        mult = mult_ref[h][:, None, :]
+        scores = jnp.where(mult > 0.0, scores, FAR)
+        probs = jnp.exp(scores - lse_ref[h][None]) * mult
+        delta = jnp.sum(grad.astype(F32) * out_ref[low : low + HD, :], axis=0, keepdims=True)
+        d_probs = dot_tn(value, grad).reshape(rows // BLOCK, BLOCK, lanes)
+        d_scores = (probs * (d_probs - delta[None])).astype(BF).reshape(rows, lanes)
+        packed = probs.astype(BF).reshape(rows, lanes)
+        dq_ref[low : low + HD, :] = (dot_nn(key, d_scores) * scale).astype(BF)
+        d_key = dot_nt(query, d_scores) * scale
+        d_value = dot_nt(grad, packed)
+        half = rows // 2
+        dkv_ref[low : low + HD, :] = d_key[:, :half]
+        dkv_ref[width + low : width + low + HD, :] = d_value[:, :half]
+        far_ref[low : low + HD, :] = d_key[:, half:].astype(BF)
+        far_ref[width + low : width + low + HD, :] = d_value[:, half:].astype(BF)
+
+
+def norm_parts(values):
+    center = values - jnp.mean(values, axis=-1, keepdims=True)
+    rate = lax.rsqrt(jnp.mean(center * center, axis=-1, keepdims=True) + epsilon)
+    return center * rate, rate
+
+
+def after(value, *others):
+    return lax.optimization_barrier((value, *others))[0]
+
+
+def line(ref, start=0, size=None):
+    size = ref.shape[0] if size is None else size
+    return ref[start : start + size].reshape(1, size)
+
+
+def lay_rows(out, at, vector):
+    for b in range(vector.shape[1] // LANES):
+        out[at + b : at + b + 1, :] = vector[:, b * LANES : (b + 1) * LANES]
+    return at + vector.shape[1] // LANES
+
+
+def project_kernel(
+    place_ref, tokens_ref, wq_ref, wk_ref, wv_ref, bq_ref, bv_ref, gain_ref, shift_ref,
+    hat_ref, cut0, cut1, cut2, cut3, held, turned, sems,
+):
+    chip = place_ref[0]
+    width = tokens_ref.shape[1]
+    part = width // GROUP
+    copies = [
+        pltpu.make_async_copy(ref, held.at[n], sems.at[n])
+        for n, ref in enumerate((wq_ref, wk_ref, wv_ref))
+    ]
+    for copy in copies:
+        copy.start()
+    hat, _ = norm_parts(tokens_ref[...].astype(F32))
+    hat_ref[...] = hat.astype(BF)
+    normed = (hat * line(gain_ref) + line(shift_ref)).astype(BF)
+    biases = (bq_ref, None, bv_ref)
+    for n, copy in enumerate(copies):
+        copy.wait()
+        rows = dot_nn(normed, held[n])
+        if biases[n] is not None:
+            rows = rows + line(biases[n])
+        turned[n * width : (n + 1) * width, :] = rows.astype(BF).T
+    for k, ref in enumerate((cut0, cut1, cut2, cut3)):
+        for n in range(3):
+            at = pl.multiple_of(n * width + (chip ^ k) * part, part)
+            ref[n * part : (n + 1) * part, :] = turned[pl.ds(at, part), :]
+
+
+def mult_kernel(heads, blocks_all, place_ref, rand_ref, mult_ref):
+    chip, core = place_ref[0], place_ref[2]
+    rows, lanes = mult_ref.shape[1], mult_ref.shape[2]
+    spot = lax.broadcasted_iota(jnp.int32, (rows, BLOCK), 0)
+    side = jnp.where(spot < rows // 2, core, 1 - core)
+    key_ids = 4 * (chip ^ ((spot >> 1) & 3)) + 2 * side + (spot & 1)
+    one = lambda hit: jnp.where(hit, 1.0, 0.0)
+    ends = one(key_ids == 0) + one(key_ids == blocks_all - 1)
+    for r in range(lanes // BLOCK):
+        query = 4 * (chip ^ (r // 2)) + 2 * core + (r % 2)
+        fixed = ends + one(key_ids == query - 1) + one(key_ids == query) + one(key_ids == query + 1)
+        whole = (query == 0) | (query == blocks_all - 1)
+        for h in range(heads):
+            total = fixed
+            for n in range(RAND):
+                named = rand_ref[query * (HEADS * RAND) + (chip * heads + h) * RAND + n]
+                total = total + one(key_ids == named)
+            total = jnp.where(whole, jnp.ones_like(total), total)
+            mult_ref[h, :, r * BLOCK : (r + 1) * BLOCK] = total
+
+
+def middle_kernel(
+    place_ref, tokens_ref, ctx0, ctx1, ctx2, ctx3, w_out_hbm, b_out_ref, gain_ref, shift_ref,
+    w_up_hbm, b_up_ref, d_active_hbm, cot_ref,
+    down0, down1, down2, down3, up0, up1, up2, up3, back0, back1,
+    middle_ref, active_ref, d_middle_ref, tiny_ref,
+    ctx_full, active_t, d_hidden_f, d_att_f, d_ctx_full, w_out_ref, w_up_ref, d_active_ref, sems,
+):
+    chip, item = place_ref[0], place_ref[1]
+    rows, width = tokens_ref.shape
+    part = width // GROUP
+    fan = w_up_ref.shape[1]
+    chunk = width
+    chunks = fan // chunk
+    out_copy = pltpu.make_async_copy(w_out_hbm, w_out_ref, sems.at[0])
+    out_copy.start()
+    copies = []
+    for j in range(chunks):
+        cols = slice(j * chunk, (j + 1) * chunk)
+        up_copy = pltpu.make_async_copy(w_up_hbm.at[:, cols], w_up_ref.at[:, cols], sems.at[1 + j])
+        act_copy = pltpu.make_async_copy(
+            d_active_hbm.at[:, cols], d_active_ref.at[:, cols], sems.at[1 + chunks + j]
+        )
+        up_copy.start()
+        act_copy.start()
+        copies.append((up_copy, act_copy))
+    for k, ref in enumerate((ctx0, ctx1, ctx2, ctx3)):
+        at = pl.multiple_of((chip ^ k) * part, part)
+        ctx_full[pl.ds(at, part), :] = ref[...]
+    context = ctx_full[...]
+    out_copy.wait()
+    middle = tokens_ref[...].astype(F32) + (dot_tn(context, w_out_ref[...]) + line(b_out_ref))
+    middle_ref[...] = middle
+    hat, rate = norm_parts(middle)
+    normed = (hat * line(gain_ref) + line(shift_ref)).astype(BF)
+    at = 0
+    d_norm = jnp.zeros((rows, width), F32)
+    for j in range(chunks):
+        cols = slice(j * chunk, (j + 1) * chunk)
+        copies[j][0].wait()
+        hidden = dot_nn(normed, w_up_ref[:, cols]) + line(b_up_ref, j * chunk, chunk)
+        bell = 0.5 * (1.0 + lax.erf(hidden * (0.5**0.5)))
+        active = (hidden * bell).astype(BF)
+        active_ref[:, cols] = active
+        active_t[cols, :] = active.T
+        slope = bell + hidden * jnp.exp(-0.5 * hidden * hidden) * 0.3989422804014327
+        copies[j][1].wait()
+        d_hidden = (d_active_ref[:, cols] * slope).astype(BF)
+        at = lay_rows(tiny_ref, at, jnp.sum(d_hidden.astype(F32), axis=0, keepdims=True))
+        for b in range(chunk // LANES):
+            to = j * chunk + b * LANES
+            d_hidden_f[to : to + LANES, :] = d_hidden[:, b * LANES : (b + 1) * LANES]
+        d_norm = d_norm + dot_nt(d_hidden, w_up_ref[:, cols])
+    at = lay_rows(tiny_ref, at, jnp.sum(d_norm * hat, axis=0, keepdims=True))
+    at = lay_rows(tiny_ref, at, jnp.sum(d_norm, axis=0, keepdims=True))
+    scaled = d_norm * line(gain_ref)
+    cot = cot_ref[...].astype(F32)
+    at = lay_rows(tiny_ref, at, jnp.sum(cot, axis=0, keepdims=True))
+    d_middle = cot + rate * (
+        scaled
+        - jnp.mean(scaled, axis=-1, keepdims=True)
+        - hat * jnp.mean(scaled * hat, axis=-1, keepdims=True)
+    )
+    d_middle_ref[...] = d_middle
+    d_attended = d_middle.astype(BF)
+    at = lay_rows(tiny_ref, at, jnp.sum(d_attended.astype(F32), axis=0, keepdims=True))
+    d_ctx_full[...] = dot_nt(w_out_ref[...], d_attended).astype(BF)
+    for k in range(GROUP):
+        at = pl.multiple_of((chip ^ k) * part, part)
+        ref = (back0, back1)[k % 2]
+        ref[k // 2 * part : (k // 2 + 1) * part, :] = d_ctx_full[pl.ds(at, part), :]
+    normed_t = normed.T
+    quarter, mid = fan // 8, width // 2
+    for b in range(width // LANES):
+        d_att_f[b * LANES : (b + 1) * LANES, :] = d_attended[:, b * LANES : (b + 1) * LANES]
+    early = LANES
+    late = quarter - early
+    for k, (first, second) in enumerate(zip((down0, down1, down2, down3), (up0, up1, up2, up3))):
+        target = item ^ k
+        for c in range(2):
+            at = pl.multiple_of(c * (fan // 2) + target * quarter, quarter)
+            first[c * quarter : (c + 1) * quarter, :] = active_t[pl.ds(at, quarter), :]
+            to = 2 * quarter + width + c * early
+            first[to : to + early, :] = d_hidden_f[pl.ds(at, early), :]
+            at = pl.multiple_of(c * (fan // 2) + target * quarter + early, early)
+            second[c * late : (c + 1) * late, :] = d_hidden_f[pl.ds(at, late), :]
+            at = pl.multiple_of((2 * c + (target & 1)) * part, part)
+            to = 2 * late + c * part
+            second[to : to + part, :] = ctx_full[pl.ds(at, part), :]
+        first[2 * quarter : 2 * quarter + width, :] = normed_t
+        at = pl.multiple_of((target >> 1) * mid, mid)
+        to = 2 * late + 2 * part
+        second[to : to + mid, :] = d_att_f[pl.ds(at, mid), :]
+
+
+ROUND = (0, 2, 1, 3)
+
+
+def hand_out(chip, out_ref, at, size, grads):
+    for z in range(GROUP):
+        k = chip ^ z
+        row = ((k >> 1) | ((k & 1) << 1)) * size
+        here = at
+        for grad in grads:
+            share = grad.shape[0] // GROUP
+            for b in range(grad.shape[1] // LANES):
+                out_ref[pl.ds(pl.multiple_of(row + here, 16), share), :] = grad[
+                    z * share : (z + 1) * share, b * LANES : (b + 1) * LANES
+                ].astype(out_ref.dtype)
+                here += share
+    return here
+
+
+def first_grad_kernel(place_ref, *refs):
+    pieces, cots, kept_ref, given_ref = refs[:4], refs[4:8], refs[8], refs[9]
+    down_left, down_right, up_left, up_right = refs[10:]
+    chip, core = place_ref[0], place_ref[2]
+    quarter, width, early = down_left.shape[0] // 2, up_left.shape[0], up_right.shape[1] // 2
+    for s, piece in enumerate(pieces):
+        span = slice(s * LANES, (s + 1) * LANES)
+        down_left[:, span] = piece[: 2 * quarter, :]
+        down_right[span, :] = cots[s][...]
+        up_left[:, span] = piece[2 * quarter : 2 * quarter + width, :]
+        for c in range(2 * early // LANES):
+            low = 2 * quarter + width + c * LANES
+            up_right[span, c * LANES : (c + 1) * LANES] = piece[low : low + LANES, :]
+    size = kept_ref.shape[0] // GROUP
+    for half, ref in ((1 - core, given_ref), (core, kept_ref)):
+        rows = pl.ds(pl.multiple_of(half * quarter, quarter), quarter)
+        cols = pl.ds(pl.multiple_of(half * early, early), early)
+        grad_down = dot_nn(down_left[rows, :], down_right[...])
+        at = hand_out(chip, ref, 0, size, (grad_down,))
+        hand_out(chip, ref, at, size, (dot_nn(up_left[...], up_right[:, cols]),))
+
+
+def second_grad_kernel(place_ref, *refs):
+    firsts, pieces, kept_ref, given_ref = refs[:4], refs[4:8], refs[8], refs[9]
+    up_left, up_right, out_left, out_right = refs[10:]
+    chip, core = place_ref[0], place_ref[2]
+    width, late = up_left.shape[0], up_right.shape[1] // 2
+    part, mid = out_left.shape[0] // 2, out_right.shape[1]
+    skip = firsts[0].shape[0] - width - 2 * LANES
+    for s, piece in enumerate(pieces):
+        span = slice(s * LANES, (s + 1) * LANES)
+        up_left[:, span] = firsts[s][skip : skip + width, :]
+        for b in range(2 * late // LANES):
+            up_right[span, b * LANES : (b + 1) * LANES] = piece[b * LANES : (b + 1) * LANES, :]
+        out_left[:, span] = piece[2 * late : 2 * late + 2 * part, :]
+        for b in range(mid // LANES):
+            low = 2 * late + 2 * part + b * LANES
+            out_right[span, b * LANES : (b + 1) * LANES] = piece[low : low + LANES, :]
+    size = kept_ref.shape[0] // GROUP
+    for half, ref in ((1 - core, given_ref), (core, kept_ref)):
+        rows = pl.ds(pl.multiple_of(half * part, part), part)
+        cols = pl.ds(pl.multiple_of(half * late, late), late)
+        at = hand_out(chip, ref, 0, size, (dot_nn(up_left[...], up_right[:, cols]),))
+        hand_out(chip, ref, at, size, (dot_nn(out_left[rows, :], out_right[...]),))
+
+
+def head_grad_kernel(
+    place_ref, dq_ref, dkv_ref, far_ref, hat0, hat1, gain_ref, shift_ref, wq_hbm, wk_hbm, wv_hbm,
+    back0, back1, kept_ref, given_ref, tiny_ref,
+    d_heads, normed, grad, padded, window, sems,
+):
+    chip, core = place_ref[0], place_ref[2]
+    part, tokens = dq_ref.shape
+    width = normed.shape[1]
+    wide = padded.shape[1]
+    off = pl.multiple_of((chip & 1) * HD, HD)
+    begin = pl.multiple_of(chip * part - off, LANES)
+    copies = [
+        pltpu.make_async_copy(w.at[:, pl.ds(begin, wide)], window.at[n], sems.at[n])
+        for n, w in enumerate((wq_hbm, wk_hbm, wv_hbm))
+    ]
+    for copy in copies:
+        copy.start()
+    d_heads[:part, :] = dq_ref[...]
+    d_heads[part:, :] = (dkv_ref[...] + far_ref[...].astype(F32)).astype(BF)
+    padded[...] = jnp.zeros(padded.shape, BF)
+    for n in range(3):
+        padded[n, pl.ds(off, part), :] = d_heads[n * part : (n + 1) * part, :]
+    hats = [((hat0, hat1)[k % 2], k // 2 * LANES) for k in range(GROUP)]
+    for k, (hat, at) in enumerate(hats):
+        span = slice(k * LANES, (k + 1) * LANES)
+        back, row = (back0, back1)[k % 2], k // 2 * 3 * part
+        back[row : row + 3 * part, :] = d_heads[:, span]
+        rows = hat[at : at + LANES, :].astype(F32) * line(gain_ref) + line(shift_ref)
+        normed[span, :] = rows.astype(BF)
+    grad[...] = dot_nn(d_heads[...], normed[...])
+    mid, rows = width // 2, 3 * part // GROUP
+    for b in range(mid // LANES):
+        mine = grad[:, pl.ds(pl.multiple_of(core * mid + b * LANES, LANES), LANES)]
+        theirs = grad[:, pl.ds(pl.multiple_of((1 - core) * mid + b * LANES, LANES), LANES)]
+        for q in range(GROUP):
+            at = (q * (mid // LANES) + b) * rows
+            kept_ref[at : at + rows, :] = mine[q * rows : (q + 1) * rows, :]
+            given_ref[at : at + rows, :] = theirs[q * rows : (q + 1) * rows, :].astype(BF)
+    for copy in copies:
+        copy.wait()
+    turned = [padded[n].T for n in range(3)]
+    gain_grad = jnp.zeros((1, width), F32)
+    shift_grad = jnp.zeros((1, width), F32)
+    for k, (hat, at) in enumerate(hats):
+        span = slice(k * LANES, (k + 1) * LANES)
+        d_norm = dot_nt(turned[0][span, :], window[0])
+        d_norm = d_norm + dot_nt(turned[1][span, :], window[1])
+        d_norm = d_norm + dot_nt(turned[2][span, :], window[2])
+        rows = hat[at : at + LANES, :].astype(F32)
+        gain_grad = gain_grad + jnp.sum(d_norm * rows, axis=0, keepdims=True)
+        shift_grad = shift_grad + jnp.sum(d_norm, axis=0, keepdims=True)
+    at = lay_rows(tiny_ref, 0, gain_grad)
+    at = lay_rows(tiny_ref, at, shift_grad)
+    ones = jnp.ones((8, tokens), BF)
+    for n in (0, 2):
+        sums = dot_nt(ones, padded[n])
+        for r in range(width // LANES):
+            value = jnp.zeros((1, LANES), F32)
+            for m in range(wide // LANES):
+                here = sums[:1, m * LANES : (m + 1) * LANES]
+                value = value + jnp.where(begin == (r - m) * LANES, here, 0.0)
+            tiny_ref[at : at + 1, :] = value
+            at += 1
+
+
+def input_grad_kernel(
+    place_ref, back0, back1, back2, wq_hbm, wk_hbm, wv_hbm, tokens_ref, d_middle_ref,
+    gain_ref, grad_ref, held, turned, sems,
+):
+    chip = place_ref[0]
+    rows, width = tokens_ref.shape
+    part = width // GROUP
+    copies = [
+        pltpu.make_async_copy(ref, held.at[n], sems.at[n])
+        for n, ref in enumerate((wq_hbm, wk_hbm, wv_hbm))
+    ]
+    for copy in copies:
+        copy.start()
+    for k, ref in enumerate((back0, back1, back2, back2)):
+        base = 3 * part if k == 3 else 0
+        for n in range(3):
+            at = pl.multiple_of(n * width + (chip ^ k) * part, part)
+            turned[pl.ds(at, part), :] = ref[base + n * part : base + (n + 1) * part, :]
+    d_norm = jnp.zeros((width, rows), F32)
+    for n, copy in enumerate(copies):
+        copy.wait()
+        d_norm = d_norm + dot_nn(held[n], turned[n * width : (n + 1) * width, :])
+    d_norm = d_norm.T
+    hat, rate = norm_parts(tokens_ref[...].astype(F32))
+    scaled = d_norm * line(gain_ref)
+    d_inputs = rate * (
+        scaled
+        - jnp.mean(scaled, axis=-1, keepdims=True)
+        - hat * jnp.mean(scaled * hat, axis=-1, keepdims=True)
+    )
+    grad_ref[...] = (d_middle_ref[...] + d_inputs).astype(BF)
+
+
+def fetch_halves(size, used, halves, came, sems):
+    copies = {}
+    for n, half in enumerate(halves):
+        for s in range(2):
+            copy = pltpu.make_async_copy(
+                half.at[s * size : s * size + used], came.at[n // 2, n % 2, s], sems.at[n // 2, n % 2, s]
+            )
+            copy.start()
+            copies[n // 2, n % 2, s] = copy
+    return copies
+
+
+def put_halves(layout, which, place_ref, copies, came, boxes, targets, sems):
+    chip, item, core = place_ref[0], place_ref[1], place_ref[2]
+    leaving = []
+    for piece, (flip, step) in enumerate(which):
+        side, place = core ^ flip, item ^ step
+        known = {"eighth": side * GROUP + place, "row": 2 * side + (place & 1), "column": place >> 1}
+        for k in range(GROUP):
+            h, s = k % 2, k // 2
+            copies[piece, h, s].wait()
+            at = 0
+            for (share, blocks, *_), box in zip(layout, boxes):
+                to = pl.multiple_of((chip ^ k) * share, share)
+                for b in range(blocks):
+                    box[piece, pl.ds(to, share), b * LANES : (b + 1) * LANES] = came[
+                        piece, h, s, at : at + share, :
+                    ].astype(F32)
+                    at += share
+        for n, (share, blocks, row, column, unit, first) in enumerate(layout):
+            tall, wide = GROUP * share, blocks * LANES
+            target = targets[n]
+            if row is not None:
+                start = pl.multiple_of(known[row] * tall, tall)
+                target = target.at[pl.ds(start, tall), :]
+            if column is not None:
+                start = pl.multiple_of(known[column] * unit + first, LANES)
+                target = target.at[:, pl.ds(start, wide)]
+            copy = pltpu.make_async_copy(boxes[n].at[piece], target, sems.at[piece, n])
+            copy.start()
+            leaving.append(copy)
+    return leaving
+
+
+def put_pieces_kernel(layout, size, which, place_ref, *refs):
+    outs = len(layout)
+    halves = refs[: 2 * len(which)]
+    came, in_sems, out_sems = refs[-3:]
+    boxes = refs[-3 - outs : -3]
+    done = refs[-4 - outs]
+    targets = refs[-4 - 2 * outs : -4 - outs]
+    done[...] = jnp.zeros(done.shape, F32)
+    copies = fetch_halves(size, came.shape[3], halves, came, in_sems)
+    for copy in put_halves(layout, which, place_ref, copies, came, boxes, targets, out_sems):
+        copy.wait()
+
+
+def fetch_heads(size, skip, place_ref, flip, halves, whole, sems):
+    chip, item = place_ref[0], place_ref[1]
+    part = whole.shape[1] // (3 * GROUP)
+    rows = 3 * part // GROUP
+    copies = []
+    for k in range(GROUP):
+        for z in range(GROUP):
+            to = pl.multiple_of((chip ^ z) * (3 * part) + (item ^ k) * rows, 16)
+            for b in range(whole.shape[2] // LANES):
+                at = z // 2 * size + skip + b * rows
+                copy = pltpu.make_async_copy(
+                    halves[2 * k + z % 2].at[at : at + rows],
+                    whole.at[flip, pl.ds(to, rows), b * LANES : (b + 1) * LANES],
+                    sems.at[flip, k, z, b],
+                )
+                copy.start()
+                copies.append(copy)
+    return copies
+
+
+def put_heads(place_ref, flip, copies, whole, held, targets, sems):
+    mid = whole.shape[2]
+    part = whole.shape[1] // (3 * GROUP)
+    for copy in copies:
+        copy.wait()
+    leaving = []
+    for b in range(mid // LANES):
+        start = pl.multiple_of((place_ref[2] ^ flip) * mid + b * LANES, LANES)
+        for n, target in enumerate(targets):
+            tall = jnp.concatenate(
+                [
+                    whole[
+                        flip,
+                        z * 3 * part + n * part : z * 3 * part + (n + 1) * part,
+                        b * LANES : (b + 1) * LANES,
+                    ]
+                    for z in range(GROUP)
+                ],
+                axis=0,
+            )
+            held[flip, n, b] = tall.T.astype(F32)
+            copy = pltpu.make_async_copy(
+                held.at[flip, n, b], target.at[pl.ds(start, LANES), :], sems.at[flip, n, b]
+            )
+            copy.start()
+            leaving.append(copy)
+    return leaving
+
+
+def put_rest_kernel(layout, size, skip, which, place_ref, *refs):
+    halves, targets, heads_out, done, boxes = refs[:16], refs[19:21], refs[21:24], refs[24], refs[25:27]
+    came, whole, held, in_sems, head_sems, out_sems, head_out_sems = refs[27:]
+    done[...] = jnp.zeros(done.shape, F32)
+    chosen = [halves[2 * (GROUP * flip + k) + h] for flip, k in which for h in range(2)]
+    copies = fetch_halves(size, skip, chosen, came, in_sems)
+    heads = [
+        fetch_heads(size, skip, place_ref, flip, halves[8 * flip : 8 * flip + 8], whole, head_sems)
+        for flip in range(2)
+    ]
+    leaving = put_halves(layout, which, place_ref, copies, came, boxes, targets, out_sems)
+    for flip in range(2):
+        leaving += put_heads(place_ref, flip, heads[flip], whole, held, heads_out, head_out_sems)
+    for copy in leaving:
+        copy.wait()
+
+
+def put_pieces(layout, size, which, shapes, places, halves, flags, sofar, name):
+    count, outs = len(which), len(layout)
+    filled = [value for value in sofar if value is not None]
+    kept = [n for n, value in enumerate(sofar) if value is not None]
+    used = sum(share * blocks for share, blocks, *_ in layout)
+    anywhere = pl.BlockSpec(memory_space=pl.ANY)
+    before = 1 + 2 * count + len(flags)
+    return pl.pallas_call(
+        functools.partial(put_pieces_kernel, layout, size, which),
+        in_specs=[pl.BlockSpec(memory_space=pltpu.SMEM)]
+        + [anywhere] * (2 * count)
+        + vmem(len(flags))
+        + [anywhere] * len(filled),
+        out_specs=[anywhere] * outs + vmem(1),
+        out_shape=[jax.ShapeDtypeStruct(shape, F32) for shape in shapes]
+        + [jax.ShapeDtypeStruct((8, LANES), F32)],
+        scratch_shapes=[
+            pltpu.VMEM((count, GROUP * share, blocks * LANES), F32)
+            for share, blocks, *_ in layout
+        ]
+        + [
+            pltpu.VMEM((count, 2, 2, used, LANES), BF),
+            pltpu.SemaphoreType.DMA((count, 2, 2)),
+            pltpu.SemaphoreType.DMA((count, outs)),
+        ],
+        input_output_aliases={before + i: n for i, n in enumerate(kept)},
+        compiler_params=params(),
+        cost_estimate=LIGHT,
+        name=name,
+    )(places, *halves, *flags, *filled)
+
+
+PLAN = {
+    'project': (0, 0),
+    'q1': (2, 2),
+    'q2': (2, 2),
+    'q3': (2, 2),
+    'mult': (2, 2),
+    'd_active': (2, 2),
+    'kv0': (4, 4),
+    'kv1': (4, 4),
+    'kv2': (5, 5),
+    'kv3': (4, 4),
+    'cot1': (4, 8),
+    'cot2': (4, 8),
+    'cot3': (4, 8),
+    'norm_near': (4, 6),
+    'attend': (6, 6),
+    'ctx1': (8, 8),
+    'ctx2': (8, 8),
+    'ctx3': (8, 8),
+    'middle': (10, 10),
+    'a1': (12, 12),
+    'a2': (12, 12),
+    'a3': (12, 12),
+    'dc1': (12, 12),
+    'dc2': (12, 12),
+    'norm_far': (10, 10),
+    'layer_out': (13, 15),
+    'b1': (13, 15),
+    'b2': (13, 15),
+    'b3': (13, 15),
+    'first_grad': (14, 14),
+    'one_core': (14, 14),
+    'one_z1': (15, 15),
+    'attend_back': (12, 12),
+    'far': (14, 14),
+    'one_z2': (16, 16),
+    'second_grad': (16, 16),
+    'two_core': (17, 17),
+    'head_grad': (15, 15),
+    'head_core': (15, 15),
+    'head_x': (16, 16),
+    'head_y': (16, 16),
+    'head_d': (16, 16),
+    'head_sum': (17, 17),
+    'two_z1': (18, 18),
+    'one_near': (17, 18),
+    'two_z2': (20, 20),
+    'one_far': (20, 20),
+    'one_nx': (20, 20),
+    'one_ny': (20, 20),
+    'two_near': (22, 22),
+    'one_fx': (22, 22),
+    'one_fy': (22, 22),
+    'back_z1': (17, 18),
+    'two_far': (24, 24),
+    'two_nx': (24, 24),
+    'two_ny': (24, 24),
+    'one_nd': (25, 26),
+    'one_fd': (25, 26),
+    'back_z2': (24, 25),
+    'two_fx': (25, 26),
+    'two_fy': (25, 26),
+    'input_grad': (26, 26),
+    'tiny_core': (17, 18),
+    'two_nd': (28, 28),
+    'two_fd': (28, 28),
+    'tiny_x': (22, 25),
+    'tiny_y': (28, 99),
+    'tiny_z1': (18, 20),
+    'tiny_z2': (20, 22),
+    'one_all': (17, 18),
+    'put_own': (25, 25),
+    'put_rest': (28, 28),
+    'put_two': (32, 99),
+    'one_cn0': (22, 24),
+    'one_cf0': (25, 26),
+    'two_cn0': (26, 28),
+    'two_cf0': (26, 28),
+    'one_cn1': (22, 24),
+    'one_cf1': (25, 26),
+    'two_cn1': (26, 28),
+    'two_cf1': (28, 30),
+    'one_cn2': (22, 24),
+    'one_cf2': (25, 26),
+    'two_cn2': (26, 28),
+    'two_cf2': (28, 30),
+    'one_cn3': (28, 28),
+    'one_cf3': (28, 28),
+    'two_cn3': (28, 30),
+    'two_cf3': (30, 30),
+}
+
+
+def run_steps(steps, known):
+    stage, last = {}, {}
+
+    def named(name):
+        return [source.lstrip("!").partition(".")[0] for source in steps[name][0]]
+
+    def settle(name):
+        if name in stage:
+            return stage[name]
+        first, wait = PLAN[name]
+        for source in named(name):
+            if source in steps:
+                first = max(first, settle(source))
+        stage[name], last[name] = first, max(first, wait)
+        return first
+
+    for name in steps:
+        settle(name)
+    depth = {}
+
+    def deep(name):
+        if name not in depth:
+            depth[name] = 1 + max([deep(s) for s in named(name) if s in steps], default=0)
+        return depth[name]
+
+    for name in steps:
+        deep(name)
+    made, now, waiting = dict(known), 0, []
+    order = sorted(steps, key=lambda n: (stage[n], depth[n]))
+
+    def pick(source):
+        base, _, index = source.lstrip("!").partition(".")
+        return (base, int(index)) if index else (base, None)
+
+    def turn(following):
+        ending = [n for n in waiting if last[n] < following]
+        keys = set()
+        for n in ending:
+            many = isinstance(made[n], (list, tuple))
+            if n.startswith("put_"):
+                keys.add((n, len(made[n]) - 1))
+            elif many:
+                keys.update((n, i) for i in range(len(made[n])))
+            else:
+                keys.add((n, None))
+        for n in order:
+            if stage[n] == following:
+                keys.update(
+                    pick(s) for s in steps[n][0] if not s.startswith("!") and pick(s)[0] in made
+                )
+        keys = sorted(keys, key=str)
+        values = [made[n] if i is None else made[n][i] for n, i in keys]
+        for (n, i), value in zip(keys, lax.optimization_barrier(values)):
+            if i is None:
+                made[n] = value
+            else:
+                made[n] = [value if j == i else old for j, old in enumerate(made[n])]
+        return [n for n in waiting if n not in ending]
+
+    for name in order:
+        if now < stage[name]:
+            waiting, now = turn(stage[name]), stage[name]
+        sources, function = steps[name]
+        inputs = []
+        for source in sources:
+            base, index = pick(source)
+            inputs.append(made[base] if index is None else made[base][index])
+        made[name] = function(*inputs)
+        waiting.append(name)
+    return made
+
+
+def split_device(
+    tokens,
+    rand_blocks,
+    w_query,
+    w_key,
+    w_value,
+    w_out,
+    w_up,
+    w_down,
+    bias_query,
+    bias_value,
+    bias_out,
+    bias_up,
+    bias_down,
+    attn_gain,
+    attn_shift,
+    ffn_gain,
+    ffn_shift,
+    cotangent,
+):
+    _, local_len, width = tokens.shape
+    fan = w_up.shape[1]
+    blocks_all = rand_blocks.shape[0]
+    position, item = lax.axis_index("seq"), lax.axis_index("item")
+    chip, core = position // 2, position % 2
+    heads = HEADS // GROUP
+    part = heads * HD
+    all_len = GROUP * local_len
+    quarter, mid = fan // 8, width // 2
+    early = LANES
+    late = quarter - early
+    places = jnp.stack([chip, item, core]).astype(jnp.int32)
+    smem = [pl.BlockSpec(memory_space=pltpu.SMEM)]
+    anywhere = [pl.BlockSpec(memory_space=pl.ANY)]
+    shaped = jax.ShapeDtypeStruct
+
+    first_rows = 2 * quarter + width + 2 * early
+    second_rows = 2 * late + 2 * part + mid
+    tiny_rows = (fan + 4 * width) // LANES
+    size = 3 * part
+    rows_one = (quarter * width + width * early) // LANES
+    rows_two = (width * late + part * mid) // LANES
+    rows_three = size * mid // LANES
+    half_one, half_two = rows_one // 2, rows_two // 2
+
+    def kernel(body, ins, outs, scratch=(), name=None):
+        return pl.pallas_call(
+            body,
+            in_specs=ins,
+            out_specs=vmem(len(outs)),
+            out_shape=list(outs),
+            scratch_shapes=list(scratch),
+            compiler_params=params(),
+            cost_estimate=LIGHT,
+            name=name,
+        )
+
+    box = lambda *dims: pltpu.VMEM(dims, BF)
+    box32 = lambda *dims: pltpu.VMEM(dims, F32)
+    sems = lambda n: pltpu.SemaphoreType.DMA((n,))
+
+    def project(x):
+        return kernel(
+            project_kernel,
+            smem + vmem(1) + anywhere * 3 + vmem(4),
+            [shaped((local_len, width), BF)] + [shaped((size, local_len), BF)] * 4,
+            [box(3, width, width), box(3 * width, local_len), sems(3)],
+            "project",
+        )(places, x, w_query, w_key, w_value, bias_query, bias_value, attn_gain, attn_shift)
+
+    def multiplicity(rand):
+        return kernel(
+            functools.partial(mult_kernel, heads, blocks_all),
+            smem * 2,
+            [shaped((heads, 2 * all_len // BLOCK, all_len), F32)],
+            name="multiplicity",
+        )(places, rand.reshape(-1))[0]
+
+    def attend(*ins):
+        return kernel(
+            functools.partial(attend_kernel, heads),
+            vmem(9),
+            [shaped((part, local_len), BF)] * 4
+            + [shaped((part, all_len), F32), shaped((heads, 1, all_len), F32)],
+            name="attend",
+        )(*ins)
+
+    def middle_step(ctx0, ctx1, ctx2, ctx3, d_active, cot):
+        outs = kernel(
+            middle_kernel,
+            smem + vmem(5) + anywhere + vmem(3) + anywhere + vmem(1) + anywhere + vmem(1),
+            [shaped((first_rows, LANES), BF)] * 4
+            + [shaped((second_rows, LANES), BF)] * 4
+            + [shaped((2 * part, local_len), BF)] * 2
+            + [
+                shaped((local_len, width), F32),
+                shaped((local_len, fan), BF),
+                shaped((local_len, width), F32),
+                shaped((tiny_rows, LANES), F32),
+            ],
+            [box(width, local_len), box(fan, local_len), box(fan, local_len)]
+            + [box(width, local_len)] * 2
+            + [box(width, width), box(width, fan), box32(local_len, fan)]
+            + [sems(1 + 2 * (fan // width))],
+            "middle",
+        )(
+            places, tokens[0], ctx0, ctx1, ctx2, ctx3, w_out, bias_out, ffn_gain, ffn_shift,
+            w_up, bias_up, d_active, cot,
+        )
+        return outs
+
+    def attend_back(*ins):
+        return kernel(
+            functools.partial(attend_back_kernel, heads),
+            vmem(14),
+            [
+                shaped((part, all_len), BF),
+                shaped((2 * part, all_len), F32),
+                shaped((2 * part, all_len), BF),
+            ],
+            name="attend_back",
+        )(*ins)
+
+    def first_grad(*ins):
+        return kernel(
+            first_grad_kernel,
+            smem + vmem(8),
+            [shaped((rows_one, LANES), F32), shaped((rows_one, LANES), BF)],
+            [
+                box(2 * quarter, all_len),
+                box(all_len, width),
+                box(width, all_len),
+                box(all_len, 2 * early),
+            ],
+            "first_grad",
+        )(places, *ins)
+
+    def second_grad(*ins):
+        return kernel(
+            second_grad_kernel,
+            smem + vmem(8),
+            [shaped((rows_two, LANES), F32), shaped((rows_two, LANES), BF)],
+            [
+                box(width, all_len),
+                box(all_len, 2 * late),
+                box(2 * part, all_len),
+                box(all_len, mid),
+            ],
+            "second_grad",
+        )(places, *ins)
+
+    def head_grad(*ins):
+        return kernel(
+            head_grad_kernel,
+            smem + vmem(7) + anywhere * 3,
+            [shaped((2 * size, local_len), BF)] * 2
+            + [shaped((rows_three, LANES), F32), shaped((rows_three, LANES), BF)]
+            + [shaped((4 * width // LANES, LANES), F32)],
+            [
+                box(size, all_len),
+                box(all_len, width),
+                box32(size, width),
+                box(3, part + HD, all_len),
+                box(3, width, part + HD),
+                sems(3),
+            ],
+            "head_grad",
+        )(places, *ins, attn_gain, attn_shift, w_query, w_key, w_value)
+
+    def input_grad(own, came, far, d_middle):
+        return kernel(
+            input_grad_kernel,
+            smem + vmem(3) + anywhere * 3 + vmem(3),
+            [shaped((local_len, width), BF)],
+            [box(3, width, width), box(3 * width, local_len), sems(3)],
+            "input_grad",
+        )(
+            places, own, came, far, w_query, w_key, w_value, tokens[0], d_middle, attn_gain
+        )[0]
+
+    layout_one = (
+        (quarter // GROUP, width // LANES, "eighth", None, 0, 0),
+        (width // GROUP, early // LANES, None, "eighth", quarter, 0),
+    )
+    layout_two = (
+        (width // GROUP, late // LANES, None, "eighth", quarter, early),
+        (part // GROUP, mid // LANES, "row", "column", mid, 0),
+    )
+    size_one, size_two = (rows_one + rows_three) // GROUP, rows_two // GROUP
+    shapes_one, shapes_two = ((fan, width), (width, fan)), ((width, fan), (width, width))
+
+    own_three = tuple((0, k) for k in range(3))
+    the_rest = ((0, 3), *((1, k) for k in range(GROUP)))
+    every = tuple((flip, k) for flip in range(2) for k in range(GROUP))
+
+    def put_own(*halves):
+        return put_pieces(
+            layout_one, size_one, own_three, shapes_one, places, halves, (), (None, None), "put_own"
+        )
+
+    def put_rest(*ins):
+        skip = rows_one // GROUP
+        return pl.pallas_call(
+            functools.partial(put_rest_kernel, layout_one, size_one, skip, the_rest),
+            in_specs=smem + anywhere * 16 + vmem(1) + anywhere * 2,
+            out_specs=anywhere * 5 + vmem(1),
+            out_shape=[shaped(shape, F32) for shape in shapes_one]
+            + [shaped((width, width), F32)] * 3
+            + [shaped((8, LANES), F32)],
+            scratch_shapes=[
+                box32(len(the_rest), GROUP * share, blocks * LANES)
+                for share, blocks, *_ in layout_one
+            ]
+            + [
+                box(len(the_rest), 2, 2, skip, LANES),
+                box(2, 3 * width, mid),
+                box32(2, 3, mid // LANES, LANES, width),
+                pltpu.SemaphoreType.DMA((len(the_rest), 2, 2)),
+                pltpu.SemaphoreType.DMA((2, GROUP, GROUP, mid // LANES)),
+                pltpu.SemaphoreType.DMA((len(the_rest), 2)),
+                pltpu.SemaphoreType.DMA((2, 3, mid // LANES)),
+            ],
+            input_output_aliases={18: 0, 19: 1},
+            compiler_params=params(),
+            cost_estimate=LIGHT,
+            name="put_rest",
+        )(places, *ins)
+
+    def put_two(*ins):
+        return put_pieces(
+            layout_two, size_two, every, shapes_two, places, ins[:16], ins[16:17], (ins[17], None),
+            "put_two",
+        )
+
+    def rows_of(grad_t, k):
+        blocks = grad_t.reshape(GROUP, rows_three // GROUP, LANES)
+        return lax.dynamic_index_in_dim(blocks, item ^ k, 0, False)
+
+    def head_sum(grad_t, x, y, d):
+        total = rows_of(grad_t, 0) + x.astype(F32) + (y.astype(F32) + d.astype(F32))
+        return total.astype(BF)
+
+    def last_sum(pair, far):
+        share = pair.shape[0] // 2
+        return (pair[:share] + far.astype(F32)).astype(BF)
+
+    def second_half(pair):
+        return pair[pair.shape[0] // 2 :].astype(BF)
+
+    below = lambda *parts: jnp.concatenate(parts, axis=0)
+    cot = cotangent[0]
+    todo = {
+        "project": (("tokens",), project),
+        "mult": (("rand",), multiplicity),
+        "d_active": (("cot",), lambda c: dense_back(c, w_down)),
+    }
+    for k in range(1, GROUP):
+        todo[f"q{k}"] = ((f"project.{k + 1}",), functools.partial(over_z, step=k))
+        todo[f"cot{k}"] = (("cot",), functools.partial(over_item, step=k))
+        todo[f"ctx{k}"] = ((f"attend.{k}",), functools.partial(over_z, step=k))
+    own = ["project.1", "q1", "q2", "q3"]
+    for k in range(GROUP):
+        todo[f"kv{k}"] = ((own[k],), lambda v: over_core(v[part:]))
+    other = [f"kv{k}" for k in range(GROUP)]
+    todo["attend"] = ((*own, *other, "mult"), attend)
+    todo["norm_near"] = (("project.0",), lambda v: below(v, over_z(v, 2)))
+    todo["norm_far"] = (("norm_near",), lambda v: over_z(v, 1))
+    todo["middle"] = (("attend.0", "ctx1", "ctx2", "ctx3", "d_active", "cot"), middle_step)
+    todo["layer_out"] = (
+        ("middle.10", "middle.11"),
+        lambda m, a: (m + dense_rows(a, w_down) + bias_down).astype(BF),
+    )
+    for k in range(1, GROUP):
+        todo[f"a{k}"] = ((f"middle.{k}",), functools.partial(over_item, step=k))
+        todo[f"b{k}"] = ((f"middle.{4 + k}",), functools.partial(over_item, step=k))
+    todo["dc1"] = (("middle.9",), lambda v: over_z(v, 1))
+    todo["dc2"] = (("middle.8", "dc1"), lambda v, c: over_z(below(v[part:], c[part:]), 2))
+    firsts = ["middle.0", "a1", "a2", "a3"]
+    seconds = ["middle.4", "b1", "b2", "b3"]
+    todo["first_grad"] = ((*firsts, "cot", "cot1", "cot2", "cot3"), first_grad)
+    def pair_up(half, kept, given):
+        far = over_z((kept[half:] + given[half:].astype(F32)).astype(BF), 1)
+        return kept[:half] + given[:half].astype(F32) + far.astype(F32)
+
+    todo["one_core"] = (("first_grad.1",), over_core)
+    todo["one_z1"] = (
+        ("first_grad.0", "one_core"),
+        functools.partial(pair_up, half_one),
+    )
+    todo["one_z2"] = (("one_z1",), lambda v: last_sum(v, over_z(second_half(v), 2)))
+    todo["attend_back"] = (
+        (*own, *other, "mult", "attend.4", "attend.5", "middle.8", "dc1", "dc2"),
+        attend_back,
+    )
+    todo["far"] = (("attend_back.2",), over_core)
+    todo["second_grad"] = ((*firsts, *seconds), second_grad)
+    todo["two_core"] = (("second_grad.1",), over_core)
+    todo["two_z1"] = (
+        ("second_grad.0", "two_core"),
+        functools.partial(pair_up, half_two),
+    )
+    todo["head_grad"] = (
+        ("attend_back.0", "attend_back.1", "far", "norm_near", "norm_far"),
+        head_grad,
+    )
+    todo["head_core"] = (("head_grad.2", "head_grad.3"), lambda k, g: k + over_core(g).astype(F32))
+    for k, name in enumerate("xyd"):
+        todo[f"head_{name}"] = (
+            ("head_core",),
+            lambda v, k=k + 1: over_item(rows_of(v, k).astype(BF), k),
+        )
+    todo["head_sum"] = (("head_core", "head_x", "head_y", "head_d"), head_sum)
+    todo["two_z2"] = (("two_z1",), lambda v: last_sum(v, over_z(second_half(v), 2)))
+    todo["one_all"] = (("one_z2", "head_sum"), below)
+    pieces = {}
+    for name, total in (("one", "one_all"), ("two", "two_z2")):
+        todo[f"{name}_near"] = ((total,), lambda v: below(v, over_z(v, 2)))
+        todo[f"{name}_far"] = ((f"{name}_near",), lambda v: over_z(v, 1))
+        todo[f"{name}_nx"] = ((f"{name}_near",), lambda v: over_item(v, 1))
+        todo[f"{name}_ny"] = ((f"{name}_near",), lambda v: over_item(v, 2))
+        todo[f"{name}_fx"] = ((f"{name}_far",), lambda v: over_item(v, 1))
+        todo[f"{name}_fy"] = ((f"{name}_far",), lambda v: over_item(v, 2))
+        todo[f"{name}_nd"] = ((f"{name}_nx",), lambda v: over_item(v, 2))
+        todo[f"{name}_fd"] = ((f"{name}_fy",), lambda v: over_item(v, 1))
+        flat = []
+        for k, end in enumerate(("", "x", "y", "d")):
+            halves = ("near", "far") if k == 0 else ("n" + end, "f" + end)
+            halves = [f"{name}_{h}" for h in halves]
+            flat += halves
+            todo[f"{name}_cn{k}"] = (tuple(halves[:1]), over_core)
+            todo[f"{name}_cf{k}"] = (tuple(halves[1:]), over_core)
+        mirrored = [f"{name}_c{h}{k}" for k in range(GROUP) for h in "nf"]
+        pieces[name] = (flat, mirrored)
+    own_one, mirrored_one = pieces["one"]
+    todo["put_own"] = (tuple(own_one[:6]), put_own)
+    todo["put_rest"] = (
+        (*own_one, *mirrored_one, "put_own.2", "!put_own.0", "!put_own.1"),
+        put_rest,
+    )
+    todo["put_two"] = (
+        (*pieces["two"][0], *pieces["two"][1], "put_rest.5", "!put_rest.1"),
+        put_two,
+    )
+    todo["back_z1"] = (("head_grad.1",), lambda v: over_z(v, 1))
+    todo["back_z2"] = (
+        ("head_grad.0", "back_z1"),
+        lambda v, c: over_z(below(v[size:], c[size:]), 2),
+    )
+    todo["input_grad"] = (
+        ("head_grad.0", "back_z1", "back_z2", "middle.12"),
+        input_grad,
+    )
+    todo["tiny_core"] = (
+        ("middle.13", "head_grad.4"),
+        lambda u, v: below(u, v) + over_core(below(u, v)),
+    )
+    todo["tiny_z1"] = (("tiny_core",), lambda v: v + over_z(v, 1))
+    todo["tiny_z2"] = (("tiny_z1",), lambda v: v + over_z(v, 2))
+    todo["tiny_x"] = (("tiny_z2",), lambda v: v + over_item(v, 1))
+    todo["tiny_y"] = (("tiny_x",), lambda v: v + over_item(v, 2))
+    made = run_steps(
+        todo, {"tokens": tokens[0], "rand": rand_blocks, "cot": cot}
+    )
+    tiny = made["tiny_y"]
+    layer_out, grad_tokens = made["layer_out"], made["input_grad"]
+    grad_down, grad_qkv = made["put_rest"][0], made["put_rest"][2:5]
+    grad_up, grad_out, _ = made["put_two"]
+    tiny = tiny.reshape(-1)
+    cuts, at = [], 0
+    for size in (fan,) + (width,) * 8:
+        cuts.append(tiny[at : at + size])
+        at += size
+    g_bu, g_fg, g_fs, g_bd, g_bo, g_ag, g_as, g_bq, g_bv = cuts
+    return (
+        layer_out[None],
+        grad_tokens[None],
+        grad_qkv[0],
+        grad_qkv[1],
+        grad_qkv[2],
+        grad_out,
+        grad_up,
+        grad_down,
+        g_bq,
+        g_bv,
+        g_bo,
+        g_bu,
+        g_bd,
+        g_ag,
+        g_as,
+        g_fg,
+        g_fs,
+    )
+
+
+def per_device(tokens, rand_blocks, *rest):
+    seqs, local_len, width = tokens.shape
+    fan = rest[4].shape[1]
+    fits = (
+        seqs == 1
+        and local_len == LANES
+        and lax.axis_size("item") == GROUP
+        and lax.axis_size("seq") == 2 * GROUP
+        and HEADS % GROUP == 0
+        and width == HEADS * HD
+        and fan % (8 * LANES) == 0
+        and width % (2 * LANES) == 0
+    )
+    chosen = split_device if fits else general_device
+    return chosen(tokens, rand_blocks, *rest)
+
+
 def solution(mesh):
     placed = (
         P("item", "seq", None),

time: 1080 us -> 234 us (0.22); the launches traced: 1070 us -> 234 us
  blocking collectives: 387 us -> 0 us
  local copies, waits for them, and re-layouts: 293 us -> 7.99 us
  other arithmetic: 111 us -> 3.3 us
  waiting for transfers between devices: 174 us -> 68.6 us
  Pallas kernels: 0 us -> 70 us
  matrix products: 61.5 us -> 5.9 us
  starting transfers between devices: 22.9 us -> 75.7 us
  between operations: 16.2 us -> 2.08 us
    unnamed x1 -> x0, blocking collectives: 306 us -> none
    all_gather x4 -> x0, waiting for transfers between devices: 104 us -> none  [the longest x1 104 us: per_device(): lax.all_gather(shared_rows.astype(jnp.bfloat16), ('item', 'seq'), axis=0,...]
    reshape x26 -> x1, local copies, waits for them, and re-layouts: 99.3 us -> 0.79 us  [multiplicity(): rand.reshape(-1)]
    all_gather x4 -> x0, blocking collectives: 81.3 us -> none  [the longest x2 53.3 us: entering(): lax.all_gather(part.astype(kind), axis)]
    pallas_call x0 -> x12, Pallas kernels: none -> 70 us  [the longest x2 11.1 us: put_pieces(): pl.pallas_call(functools.partial(put_pieces_kernel, layout, size, which),...]
    psum x2 -> x0, waiting for transfers between devices: 69.1 us -> none  [from_root(): return lax.psum(jnp.where(mine, shard, jnp.zeros_like(shard)), axis)]
    ppermute x4 -> x73, waiting for transfers between devices: 0.01 us -> 68.6 us  [the longest x22 54.7 us: over_z(): return lax.ppermute(value, 'seq', [(i, i ^ 2 * step) for i in range(count)])]
    ppermute x4 -> x73, starting transfers between devices: 10.1 us -> 75.7 us  [the longest x22 36.4 us: over_z(): return lax.ppermute(value, 'seq', [(i, i ^ 2 * step) for i in range(count)])]
  transfers between devices with their start and end apart: 13 -> 73, of which waited for: 3 -> 23; matrix products, arithmetic and copies ran while one was open for 17% -> 5% of each run, Pallas kernels for 0% -> 24%
where the time goes in v1:
time: 234 us
  starting transfers between devices  75.7 us (32%)
  Pallas kernels  70 us (30%)
  waiting for transfers between devices  68.6 us (29%)
  local copies, waits for them, and re-layouts  7.99 us (3%)
  matrix products  5.9 us (3%)
  other arithmetic  3.3 us (1%)
    ppermute x22, waiting for transfers between devices, over_z(): return lax.ppermute(value, 'seq', [(i, i ^ 2 * step) for i in range(count)])  54.7 us
    ppermute x22, starting transfers between devices, over_z(): return lax.ppermute(value, 'seq', [(i, i ^ 2 * step) for i in range(count)])  36.4 us
    ppermute x26, starting transfers between devices, over_item(): return lax.ppermute(value, 'item', [(i, i ^ step) for i in range(count)])  34.4 us
    ppermute x26, waiting for transfers between devices, over_item(): return lax.ppermute(value, 'item', [(i, i ^ step) for i in range(count)])  11.6 us
    pallas_call x2, Pallas kernels, put_pieces(): pl.pallas_call(functools.partial(put_pieces_kernel, layout, size, which),...  11.1 us
    pallas_call x1, Pallas kernels, middle_step(): kernel(middle_kernel, smem + vmem(5) + anywhere + vmem(3) + anywhere + vm...  10.3 us
    pallas_call x1, Pallas kernels, put_rest(): pl.pallas_call(functools.partial(put_rest_kernel, layout_one, size_one, s...  10.1 us
    pallas_call x1, Pallas kernels, attend_back(): kernel(functools.partial(attend_back_kernel, heads), vmem(14), [shaped((p...  7.49 us
  transfers between devices with their start and end apart: 73, of which 23 were waited for; matrix products, arithmetic and copies ran while one was open for 5% of the time, Pallas kernels for 24%

profile of v1, /device:TPU:0, one launch (start us, length us, event | category | flops | bytes accessed | tf_op | source)
XLA Modules:
  0.0 233.5 jit_solution(9244170130374069317)
XLA Ops:
  1.2 4.3 %project.1 = (bf16[128,768]{1,0:T(8,128)(2,1)}, bf16[576,128]{1,0:T(8,128)(2,1)}, bf16[576,128]{1,0:T(8,128)(2,1)}, bf16[576,128]{1,0:T(8,128)(2,1)}, bf16[576,128]{1,0:T(8,128)(2,1)}) custom-call(s32[3]{0:T(128)} %pad_add_fusion.place_ref, bf16[128,768]{1,0:T(8,128)(2,1)} %bitcast.49, bf16[768,768]{1,0:T(8,128)(2,1)} %wq_hbm.3, bf16[768,768]{1,0:T(8,128)(2,1)} %wk_hbm.3, ...), custom_call_target="tpu_custom_call" | custom-call | flops 1000000 | bytes 100000 | tf_op jit(solution)/shard_map/project/pallas_call | solution.py:1348
  5.6 3.1 %collective-permute-start = (bf16[576,128]{1,0:T(8,128)(2,1)}, bf16[576,128]{1,0:T(8,128)(2,1)S(1)}, u32[]{:S(2)}, u32[]{:S(2)}) collective-permute-start(bf16[576,128]{1,0:T(8,128)(2,1)} %get-tuple-element.280), channel_id=1, source_target_pairs={{0,2},{1,3},{2,0},{3,1},{4,6},{5,7},{6,4},{7,5},{8,10},{9,11},{10,... | collective-permute-start | bytes 442376 | tf_op jit(solution)/shard_map/ppermute | solution.py:503
  8.7 2.6 %collective-permute-start.1 = (bf16[576,128]{1,0:T(8,128)(2,1)}, bf16[576,128]{1,0:T(8,128)(2,1)S(1)}, u32[]{:S(2)}, u32[]{:S(2)}) collective-permute-start(bf16[576,128]{1,0:T(8,128)(2,1)} %get-tuple-element.281), channel_id=1, source_target_pairs={{0,4},{1,5},{2,6},{3,7},{4,0},{5,1},{6,2},{7,3},{8,12},{9,13},{10,... | collective-permute-start | bytes 442376 | tf_op jit(solution)/shard_map/ppermute | solution.py:503
  11.3 5.1 %fusion.5.d_active_hbm = f32[128,3072]{1,0:T(8,128)} fusion(bf16[128,768]{1,0:T(8,128)(2,1)S(1)} %bitcast.54, bf16[3072,768]{1,0:T(8,128)(2,1)} %param.25), kind=kOutput, calls=%fused_computation.37 | convolution fusion | flops 603979776 | bytes 6488064 | tf_op jit(solution)/shard_map/dot_general | solution.py:101
  18.8 4.1 %collective-permute-done.1.refs_2_ = bf16[576,128]{1,0:T(8,128)(2,1)S(1)} collective-permute-done((bf16[576,128]{1,0:T(8,128)(2,1)}, bf16[576,128]{1,0:T(8,128)(2,1)S(1)}, u32[]{:S(2)}, u32[]{:S(2)}) %collective-permute-start.1) | collective-permute-done | bytes 147488 | tf_op jit(solution)/shard_map/ppermute | solution.py:503
  23.7 3.3 %collective-permute-start.7 = (bf16[128,768]{1,0:T(8,128)(2,1)S(1)}, bf16[128,768]{1,0:T(8,128)(2,1)S(1)}, u32[]{:S(2)}, u32[]{:S(2)}) collective-permute-start(bf16[128,768]{1,0:T(8,128)(2,1)S(1)} %copy-done.64), channel_id=1, source_target_pairs={{0,4},{1,5},{2,6},{3,7},{4,0},{5,1},{6,2},{7,3},{8,12},{9,13},{10,... | collective-permute-start | bytes 589832 | tf_op jit(solution)/shard_map/ppermute | solution.py:503
  31.5 5.3 %attend.1 = (bf16[192,128]{1,0:T(8,128)(2,1)}, bf16[192,128]{1,0:T(8,128)(2,1)}, bf16[192,128]{1,0:T(8,128)(2,1)}, bf16[192,128]{1,0:T(8,128)(2,1)}, f32[192,512]{1,0:T(8,128)}, /*index=5*/f32[3,1,512]{2,1,0:T(1,128)}) custom-call(bf16[576,128]{1,0:T(8,128)(2,1)} %get-tuple-element.341.refs_0_, bf16[576,128]{1,0:T(8,128)(2,1)} %copy-done.15, ...), custom_call_target="tpu_custom_call" | custom-call | flops 1000000 | bytes 100000 | tf_op jit(solution)/shard_map/attend/pallas_call | solution.py:1365
  37.1 2.0 collective-permute-start.12
  39.1 2.2 collective-permute-start.13
  41.6 2.4 %collective-permute-done.12.ctx2 = bf16[192,128]{1,0:T(8,128)(2,1)S(1)} collective-permute-done((bf16[192,128]{1,0:T(8,128)(2,1)}, bf16[192,128]{1,0:T(8,128)(2,1)S(1)}, u32[]{:S(2)}, u32[]{:S(2)}) %collective-permute-start.12) | collective-permute-done | bytes 49184 | tf_op jit(solution)/shard_map/ppermute | solution.py:503
  45.8 10.3 %middle.1 = (bf16[1792,128]{1,0:T(8,128)(2,1)}, bf16[1792,128]{1,0:T(8,128)(2,1)}, bf16[1792,128]{1,0:T(8,128)(2,1)}, bf16[1792,128]{1,0:T(8,128)(2,1)}, bf16[12...) custom-call(s32[3]{0:T(128)} %pad_add_fusion.place_ref, ...), custom_call_target="tpu_custom_call" | custom-call | flops 1000000 | bytes 100000 | tf_op jit(solution)/shard_map/middle/pallas_call | solution.py:1374
  56.2 1.6 collective-permute-start.15
  62.0 2.6 %collective-permute-done.18.refs_12_ = bf16[384,128]{1,0:T(8,128)(2,1)S(1)} collective-permute-done((bf16[384,128]{1,0:T(8,128)(2,1)}, bf16[384,128]{1,0:T(8,128)(2,1)S(1)}, u32[]{:S(2)}, u32[]{:S(2)}) %collective-permute-start.18) | collective-permute-done | bytes 98336 | tf_op jit(solution)/shard_map/ppermute | solution.py:503
  64.6 3.2 %collective-permute-start.19 = (bf16[384,128]{1,0:T(8,128)(2,1)S(1)}, bf16[384,128]{1,0:T(8,128)(2,1)S(1)}, u32[]{:S(2)}, u32[]{:S(2)}) collective-permute-start(bf16[384,128]{1,0:T(8,128)(2,1)S(1)} %pad_maximum_fusion.5), channel_id=1, source_target_pairs={{0,4},{1,5},{2,6},{3,7},{4,0},{5,1},{6,2},{7,3},{8,12},{9,13},{10,... | collective-permute-start | bytes 294920 | tf_op jit(solution)/shard_map/ppermute | solution.py:503
  67.8 2.6 %collective-permute-done.19.refs_13_ = bf16[384,128]{1,0:T(8,128)(2,1)S(1)} collective-permute-done((bf16[384,128]{1,0:T(8,128)(2,1)S(1)}, bf16[384,128]{1,0:T(8,128)(2,1)S(1)}, u32[]{:S(2)}, u32[]{:S(2)}) %collective-permute-start.19) | collective-permute-done | bytes 98336 | tf_op jit(solution)/shard_map/ppermute | solution.py:503
  71.1 7.5 %attend_back.1 = (bf16[192,512]{1,0:T(8,128)(2,1)}, f32[384,512]{1,0:T(8,128)}, bf16[384,512]{1,0:T(8,128)(2,1)}) custom-call(bf16[576,128]{1,0:T(8,128)(2,1)} %get-tuple-element.341.refs_0_, bf16[576,128]{1,0:T(8,128)(2,1)} %copy-done.15, bf16[576,128]{1,0:T(8,128)(2,1)} %copy-done.16, bf16[576,128]{1,0:T(8,128)(2,1)} %copy-done.17, ...), custom_call_target="tpu_custom_call" | custom-call | flops 1000000 | bytes 100000 | tf_op jit(solution)/shard_map/attend_back/pallas_call | solution.py:1398
  79.6 4.1 %first_grad.1 = (f32[3072,128]{1,0:T(8,128)}, bf16[3072,128]{1,0:T(8,128)(2,1)}) custom-call(s32[3]{0:T(128)} %pad_add_fusion.place_ref, bf16[1792,128]{1,0:T(8,128)(2,1)} %get-tuple-element.408.refs_0_, bf16[1792,128]{1,0:T(8,128)(2,1)} %copy-done.6, bf16[1792,128]{1,0:T(8,128)(2,1)} %copy-done.7, bf16[1792,128]{1,0:T(8,128)(2,1)} %copy-done.8, ...), custom_call_target="tpu_custom_call" | custom-call | flops 1000000 | bytes 100000 | tf_op jit(solution)/shard_map/first_grad/pallas_call | solution.py:1410
  89.2 1.7 collective-permute-start.26
  92.4 6.2 %head_grad.1 = (bf16[1152,128]{1,0:T(8,128)(2,1)}, bf16[1152,128]{1,0:T(8,128)(2,1)}, f32[1728,128]{1,0:T(8,128)}, bf16[1728,128]{1,0:T(8,128)(2,1)}, f32[24,128]{1,0:T(8,128)}) custom-call(s32[3]{0:T(128)} %pad_add_fusion.place_ref, bf16[192,512]{1,0:T(8,128)(2,1)} %get-tuple-element.387.dq_ref, f32[384,512]{1,0:T(8,128)} %get-tuple-element.388.dkv_ref, ...), custom_call_target="tpu_custom_call" | custom-call | flops 1000000 | bytes 100000 | tf_op jit(solution)/shard_map/head_grad/pallas_call | solution.py:1438
  100.8 1.7 collective-permute-done.21.refs_6_
  102.5 3.0 %collective-permute-start.30 = (bf16[768,128]{1,0:T(8,128)(2,1)S(1)}, bf16[768,128]{1,0:T(8,128)(2,1)S(1)}, u32[]{:S(2)}, u32[]{:S(2)}) collective-permute-start(bf16[768,128]{1,0:T(8,128)(2,1)S(1)} %slice.187), channel_id=1, source_target_pairs={{0,4},{1,5},{2,6},{3,7},{4,0},{5,1},{6,2},{7,3},{8,12},{9,13},{10,... | collective-permute-start | bytes 589832 | tf_op jit(solution)/shard_map/ppermute | solution.py:503
  105.5 1.5 collective-permute-start.27
  109.1 3.9 %second_grad.1 = (f32[2112,128]{1,0:T(8,128)}, bf16[2112,128]{1,0:T(8,128)(2,1)}) custom-call(s32[3]{0:T(128)} %pad_add_fusion.place_ref, bf16[1792,128]{1,0:T(8,128)(2,1)} %get-tuple-element.408.refs_0_, bf16[1792,128]{1,0:T(8,128)(2,1)} %copy-done.6, bf16[1792,128]{1,0:T(8,128)(2,1)} %copy-done.7, bf16[1792,128]{1,0:T(8,128)(2,1)} %copy-done.8, ...), custom_call_target="tpu_custom_call" | custom-call | flops 1000000 | bytes 100000 | tf_op jit(solution)/shard_map/second_grad/pallas_call | solution.py:1424
  114.7 2.4 %collective-permute-start.32 = (bf16[1200,128]{1,0:T(8,128)(2,1)S(1)}, bf16[1200,128]{1,0:T(8,128)(2,1)S(1)}, u32[]{:S(2)}, u32[]{:S(2)}) collective-permute-start(bf16[1200,128]{1,0:T(8,128)(2,1)S(1)} %pad_maximum_fusion.2), channel_id=1, source_target_pairs={{0,4},{1,5},{2,6},{3,7},{4,0},{5,1},{6,2},{7,3},{8,12},{9,13},{10,... | collective-permute-start | bytes 921608 | tf_op jit(solution)/shard_map/ppermute | solution.py:503
  119.4 12.3 %collective-permute-done.32 = bf16[1200,128]{1,0:T(8,128)(2,1)S(1)} collective-permute-done((bf16[1200,128]{1,0:T(8,128)(2,1)S(1)}, bf16[1200,128]{1,0:T(8,128)(2,1)S(1)}, u32[]{:S(2)}, u32[]{:S(2)}) %collective-permute-start.32) | collective-permute-done | bytes 307232 | tf_op jit(solution)/shard_map/ppermute | solution.py:503
  131.8 3.5 %collective-permute-done.36 = bf16[1056,128]{1,0:T(8,128)(2,1)S(1)} collective-permute-done((bf16[1056,128]{1,0:T(8,128)(2,1)S(1)}, bf16[1056,128]{1,0:T(8,128)(2,1)S(1)}, u32[]{:S(2)}, u32[]{:S(2)}) %collective-permute-start.36) | collective-permute-done | bytes 270368 | tf_op jit(solution)/shard_map/ppermute | solution.py:503
  138.1 3.2 %collective-permute-start.41 = (bf16[528,128]{1,0:T(8,128)(2,1)S(1)}, bf16[528,128]{1,0:T(8,128)(2,1)S(1)}, u32[]{:S(2)}, u32[]{:S(2)}) collective-permute-start(bf16[528,128]{1,0:T(8,128)(2,1)S(1)} %slice.188), channel_id=1, source_target_pairs={{0,4},{1,5},{2,6},{3,7},{4,0},{5,1},{6,2},{7,3},{8,12},{9,13},{10,... | collective-permute-start | bytes 405512 | tf_op jit(solution)/shard_map/ppermute | solution.py:503
  141.4 9.9 %collective-permute-done.40 = f32[72,128]{1,0:T(8,128)S(1)} collective-permute-done((f32[72,128]{1,0:T(8,128)S(1)}, f32[72,128]{1,0:T(8,128)S(1)}, u32[]{:S(2)}, u32[]{:S(2)}) %collective-permute-start.40) | collective-permute-done | bytes 36896 | tf_op jit(solution)/shard_map/ppermute | solution.py:503
  151.3 1.8 collective-permute-done.37.refs_1_
  153.2 1.6 collective-permute-start.42
  155.7 1.6 collective-permute-start.44
  157.5 8.0 %collective-permute-done.44 = bf16[528,128]{1,0:T(8,128)(2,1)S(1)} collective-permute-done((bf16[528,128]{1,0:T(8,128)(2,1)S(1)}, bf16[528,128]{1,0:T(8,128)(2,1)S(1)}, u32[]{:S(2)}, u32[]{:S(2)}) %collective-permute-start.44) | collective-permute-done | bytes 135200 | tf_op jit(solution)/shard_map/ppermute | solution.py:503
  169.6 1.7 collective-permute-start.51
  171.4 2.3 %collective-permute-start.45 = (bf16[1152,128]{1,0:T(8,128)(2,1)S(1)}, bf16[1152,128]{1,0:T(8,128)(2,1)S(1)}, u32[]{:S(2)}, u32[]{:S(2)}) collective-permute-start(bf16[1152,128]{1,0:T(8,128)(2,1)S(1)} %pad_maximum_fusion.3), channel_id=1, source_target_pairs={{0,4},{1,5},{2,6},{3,7},{4,0},{5,1},{6,2},{7,3},{8,12},{9,13},{10,... | collective-permute-start | bytes 884744 | tf_op jit(solution)/shard_map/ppermute | solution.py:503
  173.8 4.4 %collective-permute-done.49.refs_1_ = bf16[1056,128]{1,0:T(8,128)(2,1)S(1)} collective-permute-done((bf16[1056,128]{1,0:T(8,128)(2,1)S(1)}, bf16[1056,128]{1,0:T(8,128)(2,1)S(1)}, u32[]{:S(2)}, u32[]{:S(2)}) %collective-permute-start.49) | collective-permute-done | bytes 270368 | tf_op jit(solution)/shard_map/ppermute | solution.py:503
  178.3 2.2 collective-permute-start.59
  180.5 1.9 collective-permute-start.52
  182.4 2.7 %collective-permute-done.52 = f32[72,128]{1,0:T(8,128)S(1)} collective-permute-done((f32[72,128]{1,0:T(8,128)S(1)}, f32[72,128]{1,0:T(8,128)S(1)}, u32[]{:S(2)}, u32[]{:S(2)}) %collective-permute-start.52) | collective-permute-done | bytes 36896 | tf_op jit(solution)/shard_map/ppermute | solution.py:513
  185.2 1.6 collective-permute-start.56
  188.3 2.1 collective-permute-start.57
  190.5 4.8 %put_own.1 = (f32[3072,768]{1,0:T(8,128)}, f32[768,3072]{1,0:T(8,128)}, f32[8,128]{1,0:T(8,128)}) custom-call(s32[3]{0:T(128)} %pad_add_fusion.place_ref, bf16[2400,128]{1,0:T(8,128)(2,1)} %copy-done, bf16[2400,128]{1,0:T(8,128)(2,1)} %copy-done.1, bf16[2400,128]{1,0:T(8,128)(2,1)} %copy-done.2, bf16[2400,128]{1,0:T(8,128)(2,1)} %copy-done.4, ...), custom_call_target="tpu_custom_call" | custom-call | flops 1000000 | bytes 100000 | tf_op jit(solution)/shard_map/put_own/pallas_call | solution.py:1096
  195.4 5.8 %input_grad.1 = bf16[128,768]{1,0:T(8,128)(2,1)} custom-call(s32[3]{0:T(128)} %pad_add_fusion.place_ref, bf16[1152,128]{1,0:T(8,128)(2,1)} %get-tuple-element.458.back0, bf16[1152,128]{1,0:T(8,128)(2,1)} %copy-done.21, bf16[1152,128]{1,0:T(8,128)(2,1)} %copy-done.39, bf16[768,768]{1,0:T(8,128)(2,1)} %wq_hbm.3, bf16[768,768]{1,0:T(8,128)(2,1)} %wk_hbm.3, ...), custom_call_target="tpu_custom_call" | custom-call | flops 1000000 | bytes 100000 | tf_op jit(solution)/shard_map/input_grad/pallas_call | solution.py:1456
  201.3 3.7 %collective-permute-done.57.refs_6_ = bf16[2400,128]{1,0:T(8,128)(2,1)} collective-permute-done((bf16[2400,128]{1,0:T(8,128)(2,1)S(1)}, bf16[2400,128]{1,0:T(8,128)(2,1)}, u32[]{:S(2)}, u32[]{:S(2)}) %collective-permute-start.57) | collective-permute-done | bytes 614432 | tf_op jit(solution)/shard_map/ppermute | solution.py:513
  205.6 1.7 collective-permute-start.72
  209.6 1.8 collective-permute-start.67
  211.4 2.0 collective-permute-start.66
  213.5 10.1 %put_rest.1 = (f32[3072,768]{1,0:T(8,128)}, f32[768,3072]{1,0:T(8,128)}, f32[768,768]{1,0:T(8,128)}, f32[768,768]{1,0:T(8,128)}, f32[768,768]{1,0:T(8,128)}, /*index=5*/f32[8,128]{1,0:T(8,128)}) custom-call(s32[3]{0:T(128)} %pad_add_fusion.place_ref, bf16[2400,128]{1,0:T(8,128)(2,1)} %copy-done, ...), custom_call_target="tpu_custom_call", output_to_operand_aliasing={{0}: (18, {}), {1}: (19, {})} | custom-call | flops 1000000 | bytes 100000 | tf_op jit(solution)/shard_map/put_rest/pallas_call | solution.py:1488
  227.1 6.3 %put_two.1 = (f32[768,3072]{1,0:T(8,128)}, f32[768,768]{1,0:T(8,128)}, f32[8,128]{1,0:T(8,128)}) custom-call(s32[3]{0:T(128)} %pad_add_fusion.place_ref, bf16[1056,128]{1,0:T(8,128)(2,1)} %copy-done.12, bf16[1056,128]{1,0:T(8,128)(2,1)} %copy-done.40, bf16[1056,128]{1,0:T(8,128)(2,1)} %copy-done.42, ...), custom_call_target="tpu_custom_call", output_to_operand_aliasing={{0}: (18, {})} | custom-call | flops 1000000 | bytes 100000 | tf_op jit(solution)/shard_map/put_two/pallas_call | solution.py:1096
  (305 shorter events, 47.6 us)
Async XLA Ops:
  5.6 13.2 %collective-permute-start = (bf16[576,128]{1,0:T(8,128)(2,1)}, bf16[576,128]{1,0:T(8,128)(2,1)S(1)}, u32[]{:S(2)}, u32[]{:S(2)}) collective-permute-start(bf16[576,128]{1,0:T(8,128)(2,1)} %get-tuple-element.280), channel_id=1, source_target_pairs={{0,2},{1,3},{2,0},{3,1},{4,6},{5,7},{6,4},{7,5},{8,10},{9,11},{10,... | collective-permute-start | bytes 442376 | tf_op jit(solution)/shard_map/ppermute | solution.py:503
  8.7 14.2 %collective-permute-start.1 = (bf16[576,128]{1,0:T(8,128)(2,1)}, bf16[576,128]{1,0:T(8,128)(2,1)S(1)}, u32[]{:S(2)}, u32[]{:S(2)}) collective-permute-start(bf16[576,128]{1,0:T(8,128)(2,1)} %get-tuple-element.281), channel_id=1, source_target_pairs={{0,4},{1,5},{2,6},{3,7},{4,0},{5,1},{6,2},{7,3},{8,12},{9,13},{10,... | collective-permute-start | bytes 442376 | tf_op jit(solution)/shard_map/ppermute | solution.py:503
  11.3 11.6 %collective-permute-start.2 = (bf16[576,128]{1,0:T(8,128)(2,1)}, bf16[576,128]{1,0:T(8,128)(2,1)S(1)}, u32[]{:S(2)}, u32[]{:S(2)}) collective-permute-start(bf16[576,128]{1,0:T(8,128)(2,1)} %get-tuple-element.282), channel_id=1, source_target_pairs={{0,6},{1,7},{2,4},{3,5},{4,2},{5,3},{6,0},{7,1},{8,14},{9,15},{10,... | collective-permute-start | bytes 442376 | tf_op jit(solution)/shard_map/ppermute | solution.py:503
  23.7 13.1 %collective-permute-start.7 = (bf16[128,768]{1,0:T(8,128)(2,1)S(1)}, bf16[128,768]{1,0:T(8,128)(2,1)S(1)}, u32[]{:S(2)}, u32[]{:S(2)}) collective-permute-start(bf16[128,768]{1,0:T(8,128)(2,1)S(1)} %copy-done.64), channel_id=1, source_target_pairs={{0,4},{1,5},{2,6},{3,7},{4,0},{5,1},{6,2},{7,3},{8,12},{9,13},{10,... | collective-permute-start | bytes 589832 | tf_op jit(solution)/shard_map/ppermute | solution.py:503
  27.3 11.8 %collective-permute-start.8 = (bf16[128,768]{1,0:T(8,128)(2,1)S(1)}, bf16[128,768]{1,0:T(8,128)(2,1)S(1)}, u32[]{:S(2)}, u32[]{:S(2)}) collective-permute-start(bf16[128,768]{1,0:T(8,128)(2,1)S(1)} %bitcast.55), channel_id=1, source_target_pairs={{0,8},{8,0},{16,24},{24,16},{1,9},{9,1},{17,25},{25,17},{2,10},{10... | collective-permute-start | bytes 589832 | tf_op jit(solution)/shard_map/ppermute | solution.py:513
  28.8 12.5 %collective-permute-start.9 = (bf16[128,768]{1,0:T(8,128)(2,1)S(1)}, bf16[128,768]{1,0:T(8,128)(2,1)S(1)}, u32[]{:S(2)}, u32[]{:S(2)}) collective-permute-start(bf16[128,768]{1,0:T(8,128)(2,1)S(1)} %bitcast.56), channel_id=1, source_target_pairs={{0,16},{8,24},{16,0},{24,8},{1,17},{9,25},{17,1},{25,9},{2,18},{10... | collective-permute-start | bytes 589832 | tf_op jit(solution)/shard_map/ppermute | solution.py:513
  30.4 11.0 %collective-permute-start.10 = (bf16[128,768]{1,0:T(8,128)(2,1)S(1)}, bf16[128,768]{1,0:T(8,128)(2,1)S(1)}, u32[]{:S(2)}, u32[]{:S(2)}) collective-permute-start(bf16[128,768]{1,0:T(8,128)(2,1)S(1)} %bitcast.57), channel_id=1, source_target_pairs={{0,24},{8,16},{16,8},{24,0},{1,25},{9,17},{17,9},{25,1},{2,26},{10... | collective-permute-start | bytes 589832 | tf_op jit(solution)/shard_map/ppermute | solution.py:513
  45.2 11.0 %collective-permute-start.14 = (bf16[256,768]{1,0:T(8,128)(2,1)S(1)}, bf16[256,768]{1,0:T(8,128)(2,1)S(1)}, u32[]{:S(2)}, u32[]{:S(2)}) collective-permute-start(bf16[256,768]{1,0:T(8,128)(2,1)S(1)} %pad_maximum_fusion.1.hat0), channel_id=1, source_target_pairs={{0,2},{1,3},{2,0},{3,1},{4,6},{5,7},{6,4},{7,5},{8,10},{9,11},{10,... | collective-permute-start | bytes 1179656 | tf_op jit(solution)/shard_map/ppermute | solution.py:503
  56.2 22.4 %collective-permute-start.15 = (bf16[1792,128]{1,0:T(8,128)(2,1)}, bf16[1792,128]{1,0:T(8,128)(2,1)S(1)}, u32[]{:S(2)}, u32[]{:S(2)}) collective-permute-start(bf16[1792,128]{1,0:T(8,128)(2,1)} %get-tuple-element.338), channel_id=1, source_target_pairs={{0,8},{8,0},{16,24},{24,16},{1,9},{9,1},{17,25},{25,17},{2,10},{10... | collective-permute-start | bytes 1376264 | tf_op jit(solution)/shard_map/ppermute | solution.py:513
  57.7 20.8 %collective-permute-start.16 = (bf16[1792,128]{1,0:T(8,128)(2,1)}, bf16[1792,128]{1,0:T(8,128)(2,1)S(1)}, u32[]{:S(2)}, u32[]{:S(2)}) collective-permute-start(bf16[1792,128]{1,0:T(8,128)(2,1)} %get-tuple-element.339), channel_id=1, source_target_pairs={{0,16},{8,24},{16,0},{24,8},{1,17},{9,25},{17,1},{25,9},{2,18},{10... | collective-permute-start | bytes 1376264 | tf_op jit(solution)/shard_map/ppermute | solution.py:513
  59.3 19.3 %collective-permute-start.17 = (bf16[1792,128]{1,0:T(8,128)(2,1)}, bf16[1792,128]{1,0:T(8,128)(2,1)S(1)}, u32[]{:S(2)}, u32[]{:S(2)}) collective-permute-start(bf16[1792,128]{1,0:T(8,128)(2,1)} %get-tuple-element.340), channel_id=1, source_target_pairs={{0,24},{8,16},{16,8},{24,0},{1,25},{9,17},{17,9},{25,1},{2,26},{10... | collective-permute-start | bytes 1376264 | tf_op jit(solution)/shard_map/ppermute | solution.py:513
  84.3 16.5 %collective-permute-start.20 = (bf16[1280,128]{1,0:T(8,128)(2,1)}, bf16[1280,128]{1,0:T(8,128)(2,1)S(1)}, u32[]{:S(2)}, u32[]{:S(2)}) collective-permute-start(bf16[1280,128]{1,0:T(8,128)(2,1)} %get-tuple-element.373), channel_id=1, source_target_pairs={{0,8},{8,0},{16,24},{24,16},{1,9},{9,1},{17,25},{25,17},{2,10},{10... | collective-permute-start | bytes 983048 | tf_op jit(solution)/shard_map/ppermute | solution.py:513
  85.8 16.6 %collective-permute-start.21 = (bf16[1280,128]{1,0:T(8,128)(2,1)}, bf16[1280,128]{1,0:T(8,128)(2,1)S(1)}, u32[]{:S(2)}, u32[]{:S(2)}) collective-permute-start(bf16[1280,128]{1,0:T(8,128)(2,1)} %get-tuple-element.374), channel_id=1, source_target_pairs={{0,16},{8,24},{16,0},{24,8},{1,17},{9,25},{17,1},{25,9},{2,18},{10... | collective-permute-start | bytes 983048 | tf_op jit(solution)/shard_map/ppermute | solution.py:513
  87.3 15.1 %collective-permute-start.22 = (bf16[1280,128]{1,0:T(8,128)(2,1)}, bf16[1280,128]{1,0:T(8,128)(2,1)}, u32[]{:S(2)}, u32[]{:S(2)}) collective-permute-start(bf16[1280,128]{1,0:T(8,128)(2,1)} %get-tuple-element.375), channel_id=1, source_target_pairs={{0,24},{8,16},{16,8},{24,0},{1,25},{9,17},{17,9},{25,1},{2,26},{10... | collective-permute-start | bytes 983048 | tf_op jit(solution)/shard_map/ppermute | solution.py:513
  89.2 10.3 %collective-permute-start.26 = (bf16[1536,128]{1,0:T(8,128)(2,1)S(1)}, bf16[1536,128]{1,0:T(8,128)(2,1)S(1)}, u32[]{:S(2)}, u32[]{:S(2)}) collective-permute-start(bf16[1536,128]{1,0:T(8,128)(2,1)S(1)} %add_convert_fusion), channel_id=1, source_target_pairs={{0,2},{1,3},{2,0},{3,1},{4,6},{5,7},{6,4},{7,5},{8,10},{9,11},{10,... | collective-permute-start | bytes 1179656 | tf_op jit(solution)/shard_map/ppermute | solution.py:503
  102.5 11.4 %collective-permute-start.30 = (bf16[768,128]{1,0:T(8,128)(2,1)S(1)}, bf16[768,128]{1,0:T(8,128)(2,1)S(1)}, u32[]{:S(2)}, u32[]{:S(2)}) collective-permute-start(bf16[768,128]{1,0:T(8,128)(2,1)S(1)} %slice.187), channel_id=1, source_target_pairs={{0,4},{1,5},{2,6},{3,7},{4,0},{5,1},{6,2},{7,3},{8,12},{9,13},{10,... | collective-permute-start | bytes 589832 | tf_op jit(solution)/shard_map/ppermute | solution.py:503
  105.5 8.4 %collective-permute-start.27 = (bf16[432,128]{1,0:T(8,128)(2,1)S(1)}, bf16[432,128]{1,0:T(8,128)(2,1)S(1)}, u32[]{:S(2)}, u32[]{:S(2)}) collective-permute-start(bf16[432,128]{1,0:T(8,128)(2,1)S(1)} %get-tuple-element.527), channel_id=1, source_target_pairs={{0,24},{8,16},{16,8},{24,0},{1,25},{9,17},{17,9},{25,1},{2,26},{10... | collective-permute-start | bytes 331784 | tf_op jit(solution)/shard_map/ppermute | solution.py:513
  114.0 21.4 %collective-permute-start.31 = (bf16[1152,128]{1,0:T(8,128)(2,1)S(1)}, bf16[1152,128]{1,0:T(8,128)(2,1)S(1)}, u32[]{:S(2)}, u32[]{:S(2)}) collective-permute-start(bf16[1152,128]{1,0:T(8,128)(2,1)S(1)} %copy-done.74), channel_id=1, source_target_pairs={{0,2},{1,3},{2,0},{3,1},{4,6},{5,7},{6,4},{7,5},{8,10},{9,11},{10,... | collective-permute-start | bytes 884744 | tf_op jit(solution)/shard_map/ppermute | solution.py:503
  114.7 17.0 %collective-permute-start.32 = (bf16[1200,128]{1,0:T(8,128)(2,1)S(1)}, bf16[1200,128]{1,0:T(8,128)(2,1)S(1)}, u32[]{:S(2)}, u32[]{:S(2)}) collective-permute-start(bf16[1200,128]{1,0:T(8,128)(2,1)S(1)} %pad_maximum_fusion.2), channel_id=1, source_target_pairs={{0,4},{1,5},{2,6},{3,7},{4,0},{5,1},{6,2},{7,3},{8,12},{9,13},{10,... | collective-permute-start | bytes 921608 | tf_op jit(solution)/shard_map/ppermute | solution.py:503
  117.2 14.6 %collective-permute-start.35 = (f32[72,128]{1,0:T(8,128)S(1)}, f32[72,128]{1,0:T(8,128)S(1)}, u32[]{:S(2)}, u32[]{:S(2)}) collective-permute-start(f32[72,128]{1,0:T(8,128)S(1)} %add.96), channel_id=1, source_target_pairs={{0,2},{1,3},{2,0},{3,1},{4,6},{5,7},{6,4},{7,5},{8,10},{9,11},{10,... | collective-permute-start | bytes 110600 | tf_op jit(solution)/shard_map/ppermute | solution.py:503
  118.3 17.0 %collective-permute-start.36 = (bf16[1056,128]{1,0:T(8,128)(2,1)S(1)}, bf16[1056,128]{1,0:T(8,128)(2,1)S(1)}, u32[]{:S(2)}, u32[]{:S(2)}) collective-permute-start(bf16[1056,128]{1,0:T(8,128)(2,1)S(1)} %add_convert_fusion.1), channel_id=1, source_target_pairs={{0,2},{1,3},{2,0},{3,1},{4,6},{5,7},{6,4},{7,5},{8,10},{9,11},{10,... | collective-permute-start | bytes 811016 | tf_op jit(solution)/shard_map/ppermute | solution.py:503
  135.4 17.8 %collective-permute-start.37 = (bf16[2400,128]{1,0:T(8,128)(2,1)S(1)}, bf16[2400,128]{1,0:T(8,128)(2,1)S(1)}, u32[]{:S(2)}, u32[]{:S(2)}) collective-permute-start(bf16[2400,128]{1,0:T(8,128)(2,1)S(1)} %pad_maximum_fusion.refs_0_), channel_id=1, source_target_pairs={{0,2},{1,3},{2,0},{3,1},{4,6},{5,7},{6,4},{7,5},{8,10},{9,11},{10,... | collective-permute-start | bytes 1843208 | tf_op jit(solution)/shard_map/ppermute | solution.py:503
  135.8 17.4 %collective-permute-start.38 = (bf16[2400,128]{1,0:T(8,128)(2,1)S(1)}, bf16[2400,128]{1,0:T(8,128)(2,1)S(1)}, u32[]{:S(2)}, u32[]{:S(2)}) collective-permute-start(bf16[2400,128]{1,0:T(8,128)(2,1)S(1)} %pad_maximum_fusion.refs_0_), channel_id=1, source_target_pairs={{0,8},{8,0},{16,24},{24,16},{1,9},{9,1},{17,25},{25,17},{2,10},{10... | collective-permute-start | bytes 1843208 | tf_op jit(solution)/shard_map/ppermute | solution.py:513
  137.3 15.9 %collective-permute-start.39 = (bf16[2400,128]{1,0:T(8,128)(2,1)S(1)}, bf16[2400,128]{1,0:T(8,128)(2,1)S(1)}, u32[]{:S(2)}, u32[]{:S(2)}) collective-permute-start(bf16[2400,128]{1,0:T(8,128)(2,1)S(1)} %pad_maximum_fusion.refs_0_), channel_id=1, source_target_pairs={{0,16},{8,24},{16,0},{24,8},{1,17},{9,25},{17,1},{25,9},{2,18},{10... | collective-permute-start | bytes 1843208 | tf_op jit(solution)/shard_map/ppermute | solution.py:513
  138.1 13.2 %collective-permute-start.41 = (bf16[528,128]{1,0:T(8,128)(2,1)S(1)}, bf16[528,128]{1,0:T(8,128)(2,1)S(1)}, u32[]{:S(2)}, u32[]{:S(2)}) collective-permute-start(bf16[528,128]{1,0:T(8,128)(2,1)S(1)} %slice.188), channel_id=1, source_target_pairs={{0,4},{1,5},{2,6},{3,7},{4,0},{5,1},{6,2},{7,3},{8,12},{9,13},{10,... | collective-permute-start | bytes 405512 | tf_op jit(solution)/shard_map/ppermute | solution.py:503
  141.3 10.0 %collective-permute-start.40 = (f32[72,128]{1,0:T(8,128)S(1)}, f32[72,128]{1,0:T(8,128)S(1)}, u32[]{:S(2)}, u32[]{:S(2)}) collective-permute-start(f32[72,128]{1,0:T(8,128)S(1)} %add.97), channel_id=1, source_target_pairs={{0,4},{1,5},{2,6},{3,7},{4,0},{5,1},{6,2},{7,3},{8,12},{9,13},{10,... | collective-permute-start | bytes 110600 | tf_op jit(solution)/shard_map/ppermute | solution.py:503
  153.2 13.3 %collective-permute-start.42 = (bf16[2400,128]{1,0:T(8,128)(2,1)S(1)}, bf16[2400,128]{1,0:T(8,128)(2,1)S(1)}, u32[]{:S(2)}, u32[]{:S(2)}) collective-permute-start(bf16[2400,128]{1,0:T(8,128)(2,1)S(1)} %collective-permute-done.37.refs_1_), channel_id=1, source_target_pairs={{0,8},{8,0},{16,24},{24,16},{1,9},{9,1},{17,25},{25,17},{2,10},{10... | collective-permute-start | bytes 1843208 | tf_op jit(solution)/shard_map/ppermute | solution.py:513
  154.8 13.1 %collective-permute-start.43 = (bf16[2400,128]{1,0:T(8,128)(2,1)S(1)}, bf16[2400,128]{1,0:T(8,128)(2,1)S(1)}, u32[]{:S(2)}, u32[]{:S(2)}) collective-permute-start(bf16[2400,128]{1,0:T(8,128)(2,1)S(1)} %collective-permute-done.37.refs_1_), channel_id=1, source_target_pairs={{0,16},{8,24},{16,0},{24,8},{1,17},{9,25},{17,1},{25,9},{2,18},{10... | collective-permute-start | bytes 1843208 | tf_op jit(solution)/shard_map/ppermute | solution.py:513
  155.6 14.0 %collective-permute-start.46 = (bf16[2400,128]{1,0:T(8,128)(2,1)S(1)}, bf16[2400,128]{1,0:T(8,128)(2,1)S(1)}, u32[]{:S(2)}, u32[]{:S(2)}) collective-permute-start(bf16[2400,128]{1,0:T(8,128)(2,1)S(1)} %pad_maximum_fusion.refs_0_), channel_id=1, source_target_pairs={{0,1},{1,0},{2,3},{3,2},{4,5},{5,4},{6,7},{7,6},{8,9},{9,8},{10,11... | collective-permute-start | bytes 1843208 | tf_op jit(solution)/shard_map/ppermute | solution.py:508
  155.7 9.8 %collective-permute-start.44 = (bf16[528,128]{1,0:T(8,128)(2,1)S(1)}, bf16[528,128]{1,0:T(8,128)(2,1)S(1)}, u32[]{:S(2)}, u32[]{:S(2)}) collective-permute-start(bf16[528,128]{1,0:T(8,128)(2,1)S(1)} %add_convert_fusion.4), channel_id=1, source_target_pairs={{0,4},{1,5},{2,6},{3,7},{4,0},{5,1},{6,2},{7,3},{8,12},{9,13},{10,... | collective-permute-start | bytes 405512 | tf_op jit(solution)/shard_map/ppermute | solution.py:503
  157.3 14.2 %collective-permute-start.47 = (bf16[2400,128]{1,0:T(8,128)(2,1)S(1)}, bf16[2400,128]{1,0:T(8,128)(2,1)S(1)}, u32[]{:S(2)}, u32[]{:S(2)}) collective-permute-start(bf16[2400,128]{1,0:T(8,128)(2,1)S(1)} %collective-permute-done.38.refs_2_), channel_id=1, source_target_pairs={{0,1},{1,0},{2,3},{3,2},{4,5},{5,4},{6,7},{7,6},{8,9},{9,8},{10,11... | collective-permute-start | bytes 1843208 | tf_op jit(solution)/shard_map/ppermute | solution.py:508
  165.4 8.3 %collective-permute-start.48 = (bf16[2400,128]{1,0:T(8,128)(2,1)S(1)}, bf16[2400,128]{1,0:T(8,128)(2,1)S(1)}, u32[]{:S(2)}, u32[]{:S(2)}) collective-permute-start(bf16[2400,128]{1,0:T(8,128)(2,1)S(1)} %collective-permute-done.39.refs_4_), channel_id=1, source_target_pairs={{0,1},{1,0},{2,3},{3,2},{4,5},{5,4},{6,7},{7,6},{8,9},{9,8},{10,11... | collective-permute-start | bytes 1843208 | tf_op jit(solution)/shard_map/ppermute | solution.py:508
  167.9 10.3 %collective-permute-start.49 = (bf16[1056,128]{1,0:T(8,128)(2,1)S(1)}, bf16[1056,128]{1,0:T(8,128)(2,1)S(1)}, u32[]{:S(2)}, u32[]{:S(2)}) collective-permute-start(bf16[1056,128]{1,0:T(8,128)(2,1)S(1)} %pad_maximum_fusion.4.refs_0_), channel_id=1, source_target_pairs={{0,2},{1,3},{2,0},{3,1},{4,6},{5,7},{6,4},{7,5},{8,10},{9,11},{10,... | collective-permute-start | bytes 811016 | tf_op jit(solution)/shard_map/ppermute | solution.py:503
  169.2 9.0 %collective-permute-start.50 = (bf16[1056,128]{1,0:T(8,128)(2,1)S(1)}, bf16[1056,128]{1,0:T(8,128)(2,1)S(1)}, u32[]{:S(2)}, u32[]{:S(2)}) collective-permute-start(bf16[1056,128]{1,0:T(8,128)(2,1)S(1)} %pad_maximum_fusion.4.refs_0_), channel_id=1, source_target_pairs={{0,8},{8,0},{16,24},{24,16},{1,9},{9,1},{17,25},{25,17},{2,10},{10... | collective-permute-start | bytes 811016 | tf_op jit(solution)/shard_map/ppermute | solution.py:513
  169.6 8.6 %collective-permute-start.51 = (bf16[1056,128]{1,0:T(8,128)(2,1)S(1)}, bf16[1056,128]{1,0:T(8,128)(2,1)S(1)}, u32[]{:S(2)}, u32[]{:S(2)}) collective-permute-start(bf16[1056,128]{1,0:T(8,128)(2,1)S(1)} %pad_maximum_fusion.4.refs_0_), channel_id=1, source_target_pairs={{0,16},{8,24},{16,0},{24,8},{1,17},{9,25},{17,1},{25,9},{2,18},{10... | collective-permute-start | bytes 811016 | tf_op jit(solution)/shard_map/ppermute | solution.py:513
  171.4 15.3 %collective-permute-start.45 = (bf16[1152,128]{1,0:T(8,128)(2,1)S(1)}, bf16[1152,128]{1,0:T(8,128)(2,1)S(1)}, u32[]{:S(2)}, u32[]{:S(2)}) collective-permute-start(bf16[1152,128]{1,0:T(8,128)(2,1)S(1)} %pad_maximum_fusion.3), channel_id=1, source_target_pairs={{0,4},{1,5},{2,6},{3,7},{4,0},{5,1},{6,2},{7,3},{8,12},{9,13},{10,... | collective-permute-start | bytes 884744 | tf_op jit(solution)/shard_map/ppermute | solution.py:503
  178.3 8.5 %collective-permute-start.58 = (bf16[1056,128]{1,0:T(8,128)(2,1)S(1)}, bf16[1056,128]{1,0:T(8,128)(2,1)S(1)}, u32[]{:S(2)}, u32[]{:S(2)}) collective-permute-start(bf16[1056,128]{1,0:T(8,128)(2,1)S(1)} %collective-permute-done.49.refs_1_), channel_id=1, source_target_pairs={{0,8},{8,0},{16,24},{24,16},{1,9},{9,1},{17,25},{25,17},{2,10},{10... | collective-permute-start | bytes 811016 | tf_op jit(solution)/shard_map/ppermute | solution.py:513
  178.3 9.0 %collective-permute-start.59 = (bf16[1056,128]{1,0:T(8,128)(2,1)S(1)}, bf16[1056,128]{1,0:T(8,128)(2,1)S(1)}, u32[]{:S(2)}, u32[]{:S(2)}) collective-permute-start(bf16[1056,128]{1,0:T(8,128)(2,1)S(1)} %collective-permute-done.49.refs_1_), channel_id=1, source_target_pairs={{0,16},{8,24},{16,0},{24,8},{1,17},{9,25},{17,1},{25,9},{2,18},{10... | collective-permute-start | bytes 811016 | tf_op jit(solution)/shard_map/ppermute | solution.py:513
  182.4 18.8 %collective-permute-start.55 = (bf16[2400,128]{1,0:T(8,128)(2,1)S(1)}, bf16[2400,128]{1,0:T(8,128)(2,1)S(1)}, u32[]{:S(2)}, u32[]{:S(2)}) collective-permute-start(bf16[2400,128]{1,0:T(8,128)(2,1)S(1)} %collective-permute-done.43.refs_5_), channel_id=1, source_target_pairs={{0,1},{1,0},{2,3},{3,2},{4,5},{5,4},{6,7},{7,6},{8,9},{9,8},{10,11... | collective-permute-start | bytes 1843208 | tf_op jit(solution)/shard_map/ppermute | solution.py:508
  185.2 16.1 %collective-permute-start.56 = (bf16[2400,128]{1,0:T(8,128)(2,1)S(1)}, bf16[2400,128]{1,0:T(8,128)(2,1)S(1)}, u32[]{:S(2)}, u32[]{:S(2)}) collective-permute-start(bf16[2400,128]{1,0:T(8,128)(2,1)S(1)} %collective-permute-done.43.refs_5_), channel_id=1, source_target_pairs={{0,8},{8,0},{16,24},{24,16},{1,9},{9,1},{17,25},{25,17},{2,10},{10... | collective-permute-start | bytes 1843208 | tf_op jit(solution)/shard_map/ppermute | solution.py:513
  186.8 14.5 %collective-permute-start.53 = (bf16[2400,128]{1,0:T(8,128)(2,1)S(1)}, bf16[2400,128]{1,0:T(8,128)(2,1)S(1)}, u32[]{:S(2)}, u32[]{:S(2)}) collective-permute-start(bf16[2400,128]{1,0:T(8,128)(2,1)S(1)} %collective-permute-done.37.refs_1_), channel_id=1, source_target_pairs={{0,1},{1,0},{2,3},{3,2},{4,5},{5,4},{6,7},{7,6},{8,9},{9,8},{10,11... | collective-permute-start | bytes 1843208 | tf_op jit(solution)/shard_map/ppermute | solution.py:508
  186.8 14.5 %collective-permute-start.54 = (bf16[2400,128]{1,0:T(8,128)(2,1)S(1)}, bf16[2400,128]{1,0:T(8,128)(2,1)}, u32[]{:S(2)}, u32[]{:S(2)}) collective-permute-start(bf16[2400,128]{1,0:T(8,128)(2,1)S(1)} %collective-permute-done.42.refs_3_), channel_id=1, source_target_pairs={{0,1},{1,0},{2,3},{3,2},{4,5},{5,4},{6,7},{7,6},{8,9},{9,8},{10,11... | collective-permute-start | bytes 1843208 | tf_op jit(solution)/shard_map/ppermute | solution.py:508
  188.3 16.7 %collective-permute-start.57 = (bf16[2400,128]{1,0:T(8,128)(2,1)S(1)}, bf16[2400,128]{1,0:T(8,128)(2,1)}, u32[]{:S(2)}, u32[]{:S(2)}) collective-permute-start(bf16[2400,128]{1,0:T(8,128)(2,1)S(1)} %collective-permute-done.38.refs_2_), channel_id=1, source_target_pairs={{0,16},{8,24},{16,0},{24,8},{1,17},{9,25},{17,1},{25,9},{2,18},{10... | collective-permute-start | bytes 1843208 | tf_op jit(solution)/shard_map/ppermute | solution.py:513
  207.3 16.4 %collective-permute-start.64 = (bf16[1056,128]{1,0:T(8,128)(2,1)S(1)}, bf16[1056,128]{1,0:T(8,128)(2,1)S(1)}, u32[]{:S(2)}, u32[]{:S(2)}) collective-permute-start(bf16[1056,128]{1,0:T(8,128)(2,1)S(1)} %copy-done.43), channel_id=1, source_target_pairs={{0,1},{1,0},{2,3},{3,2},{4,5},{5,4},{6,7},{7,6},{8,9},{9,8},{10,11... | collective-permute-start | bytes 811016 | tf_op jit(solution)/shard_map/ppermute | solution.py:508
  208.4 15.2 %collective-permute-start.63 = (bf16[1056,128]{1,0:T(8,128)(2,1)S(1)}, bf16[1056,128]{1,0:T(8,128)(2,1)S(1)}, u32[]{:S(2)}, u32[]{:S(2)}) collective-permute-start(bf16[1056,128]{1,0:T(8,128)(2,1)S(1)} %pad_maximum_fusion.4.refs_0_), channel_id=1, source_target_pairs={{0,1},{1,0},{2,3},{3,2},{4,5},{5,4},{6,7},{7,6},{8,9},{9,8},{10,11... | collective-permute-start | bytes 811016 | tf_op jit(solution)/shard_map/ppermute | solution.py:508
  209.5 14.8 %collective-permute-start.65 = (bf16[1056,128]{1,0:T(8,128)(2,1)S(1)}, bf16[1056,128]{1,0:T(8,128)(2,1)S(1)}, u32[]{:S(2)}, u32[]{:S(2)}) collective-permute-start(bf16[1056,128]{1,0:T(8,128)(2,1)S(1)} %copy-done.45), channel_id=1, source_target_pairs={{0,1},{1,0},{2,3},{3,2},{4,5},{5,4},{6,7},{7,6},{8,9},{9,8},{10,11... | collective-permute-start | bytes 811016 | tf_op jit(solution)/shard_map/ppermute | solution.py:508
  209.6 14.7 %collective-permute-start.67 = (bf16[1056,128]{1,0:T(8,128)(2,1)S(1)}, bf16[1056,128]{1,0:T(8,128)(2,1)S(1)}, u32[]{:S(2)}, u32[]{:S(2)}) collective-permute-start(bf16[1056,128]{1,0:T(8,128)(2,1)S(1)} %copy-done.43), channel_id=1, source_target_pairs={{0,16},{8,24},{16,0},{24,8},{1,17},{9,25},{17,1},{25,9},{2,18},{10... | collective-permute-start | bytes 811016 | tf_op jit(solution)/shard_map/ppermute | solution.py:513
  211.4 13.0 %collective-permute-start.66 = (bf16[1056,128]{1,0:T(8,128)(2,1)S(1)}, bf16[1056,128]{1,0:T(8,128)(2,1)S(1)}, u32[]{:S(2)}, u32[]{:S(2)}) collective-permute-start(bf16[1056,128]{1,0:T(8,128)(2,1)S(1)} %copy-done.49), channel_id=1, source_target_pairs={{0,8},{8,0},{16,24},{24,16},{1,9},{9,1},{17,25},{25,17},{2,10},{10... | collective-permute-start | bytes 811016 | tf_op jit(solution)/shard_map/ppermute | solution.py:513
  (102 other events, 1138.0 us)

commit v2 on v1

--- a/solution.py
+++ b/solution.py
@@ -511,24 +511,6 @@
 def over_item(value, step):
     count = lax.axis_size("item")
     return lax.ppermute(value, "item", [(i, i ^ step) for i in range(count)])
-
-
-def in_order(parts, place):
-    low = (place & 1) == 1
-    high = (place & 2) == 2
-    p0, p1, p2, p3 = parts
-    p0, p1, p2, p3 = (
-        jnp.where(low, p1, p0),
-        jnp.where(low, p0, p1),
-        jnp.where(low, p3, p2),
-        jnp.where(low, p2, p3),
-    )
-    return [
-        jnp.where(high, p2, p0),
-        jnp.where(high, p3, p1),
-        jnp.where(high, p0, p2),
-        jnp.where(high, p1, p3),
-    ]
 
 
 def params(**more):
@@ -640,10 +622,6 @@
     center = values - jnp.mean(values, axis=-1, keepdims=True)
     rate = lax.rsqrt(jnp.mean(center * center, axis=-1, keepdims=True) + epsilon)
     return center * rate, rate
-
-
-def after(value, *others):
-    return lax.optimization_barrier((value, *others))[0]
 
 
 def line(ref, start=0, size=None):
@@ -963,34 +941,20 @@
     grad_ref[...] = (d_middle_ref[...] + d_inputs).astype(BF)
 
 
-def fetch_halves(size, used, halves, came, sems):
-    copies = {}
-    for n, half in enumerate(halves):
-        for s in range(2):
-            copy = pltpu.make_async_copy(
-                half.at[s * size : s * size + used], came.at[n // 2, n % 2, s], sems.at[n // 2, n % 2, s]
-            )
-            copy.start()
-            copies[n // 2, n % 2, s] = copy
-    return copies
-
-
-def put_halves(layout, which, place_ref, copies, came, boxes, targets, sems):
+def put_halves(layout, size, which, place_ref, halves, boxes, targets, sems):
     chip, item, core = place_ref[0], place_ref[1], place_ref[2]
     leaving = []
     for piece, (flip, step) in enumerate(which):
         side, place = core ^ flip, item ^ step
-        known = {"eighth": side * GROUP + place, "row": 2 * side + (place & 1), "column": place >> 1}
+        known = (side * GROUP + place, 2 * side + (place & 1), place >> 1)
         for k in range(GROUP):
-            h, s = k % 2, k // 2
-            copies[piece, h, s].wait()
-            at = 0
+            at = k // 2 * size
             for (share, blocks, *_), box in zip(layout, boxes):
                 to = pl.multiple_of((chip ^ k) * share, share)
                 for b in range(blocks):
-                    box[piece, pl.ds(to, share), b * LANES : (b + 1) * LANES] = came[
-                        piece, h, s, at : at + share, :
-                    ].astype(F32)
+                    box[piece, pl.ds(to, share), b * LANES : (b + 1) * LANES] = halves[
+                        2 * piece + k % 2
+                    ][at : at + share, :].astype(F32)
                     at += share
         for n, (share, blocks, row, column, unit, first) in enumerate(layout):
             tall, wide = GROUP * share, blocks * LANES
@@ -1010,41 +974,27 @@
 def put_pieces_kernel(layout, size, which, place_ref, *refs):
     outs = len(layout)
     halves = refs[: 2 * len(which)]
-    came, in_sems, out_sems = refs[-3:]
-    boxes = refs[-3 - outs : -3]
-    done = refs[-4 - outs]
-    targets = refs[-4 - 2 * outs : -4 - outs]
+    boxes, sems = refs[-1 - outs : -1], refs[-1]
+    done = refs[-2 - outs]
+    targets = refs[-2 - 2 * outs : -2 - outs]
     done[...] = jnp.zeros(done.shape, F32)
-    copies = fetch_halves(size, came.shape[3], halves, came, in_sems)
-    for copy in put_halves(layout, which, place_ref, copies, came, boxes, targets, out_sems):
+    for copy in put_halves(layout, size, which, place_ref, halves, boxes, targets, sems):
         copy.wait()
 
 
-def fetch_heads(size, skip, place_ref, flip, halves, whole, sems):
+def put_heads(size, skip, place_ref, flip, halves, whole, held, targets, sems):
     chip, item = place_ref[0], place_ref[1]
+    mid = whole.shape[2]
     part = whole.shape[1] // (3 * GROUP)
     rows = 3 * part // GROUP
-    copies = []
     for k in range(GROUP):
         for z in range(GROUP):
             to = pl.multiple_of((chip ^ z) * (3 * part) + (item ^ k) * rows, 16)
-            for b in range(whole.shape[2] // LANES):
+            for b in range(mid // LANES):
                 at = z // 2 * size + skip + b * rows
-                copy = pltpu.make_async_copy(
-                    halves[2 * k + z % 2].at[at : at + rows],
-                    whole.at[flip, pl.ds(to, rows), b * LANES : (b + 1) * LANES],
-                    sems.at[flip, k, z, b],
-                )
-                copy.start()
-                copies.append(copy)
-    return copies
-
-
-def put_heads(place_ref, flip, copies, whole, held, targets, sems):
-    mid = whole.shape[2]
-    part = whole.shape[1] // (3 * GROUP)
-    for copy in copies:
-        copy.wait()
+                whole[flip, pl.ds(to, rows), b * LANES : (b + 1) * LANES] = halves[2 * k + z % 2][
+                    at : at + rows, :
+                ]
     leaving = []
     for b in range(mid // LANES):
         start = pl.multiple_of((place_ref[2] ^ flip) * mid + b * LANES, LANES)
@@ -1071,17 +1021,15 @@
 
 def put_rest_kernel(layout, size, skip, which, place_ref, *refs):
     halves, targets, heads_out, done, boxes = refs[:16], refs[19:21], refs[21:24], refs[24], refs[25:27]
-    came, whole, held, in_sems, head_sems, out_sems, head_out_sems = refs[27:]
+    whole, held, out_sems, head_out_sems = refs[27:]
     done[...] = jnp.zeros(done.shape, F32)
     chosen = [halves[2 * (GROUP * flip + k) + h] for flip, k in which for h in range(2)]
-    copies = fetch_halves(size, skip, chosen, came, in_sems)
-    heads = [
-        fetch_heads(size, skip, place_ref, flip, halves[8 * flip : 8 * flip + 8], whole, head_sems)
-        for flip in range(2)
-    ]
-    leaving = put_halves(layout, which, place_ref, copies, came, boxes, targets, out_sems)
+    leaving = put_halves(layout, size, which, place_ref, chosen, boxes, targets, out_sems)
     for flip in range(2):
-        leaving += put_heads(place_ref, flip, heads[flip], whole, held, heads_out, head_out_sems)
+        leaving += put_heads(
+            size, skip, place_ref, flip, halves[8 * flip : 8 * flip + 8], whole, held, heads_out,
+            head_out_sems,
+        )
     for copy in leaving:
         copy.wait()
 
@@ -1090,14 +1038,12 @@
     count, outs = len(which), len(layout)
     filled = [value for value in sofar if value is not None]
     kept = [n for n, value in enumerate(sofar) if value is not None]
-    used = sum(share * blocks for share, blocks, *_ in layout)
     anywhere = pl.BlockSpec(memory_space=pl.ANY)
     before = 1 + 2 * count + len(flags)
     return pl.pallas_call(
         functools.partial(put_pieces_kernel, layout, size, which),
         in_specs=[pl.BlockSpec(memory_space=pltpu.SMEM)]
-        + [anywhere] * (2 * count)
-        + vmem(len(flags))
+        + vmem(2 * count + len(flags))
         + [anywhere] * len(filled),
         out_specs=[anywhere] * outs + vmem(1),
         out_shape=[jax.ShapeDtypeStruct(shape, F32) for shape in shapes]
@@ -1106,11 +1052,7 @@
             pltpu.VMEM((count, GROUP * share, blocks * LANES), F32)
             for share, blocks, *_ in layout
         ]
-        + [
-            pltpu.VMEM((count, 2, 2, used, LANES), BF),
-            pltpu.SemaphoreType.DMA((count, 2, 2)),
-            pltpu.SemaphoreType.DMA((count, outs)),
-        ],
+        + [pltpu.SemaphoreType.DMA((count, outs))],
         input_output_aliases={before + i: n for i, n in enumerate(kept)},
         compiler_params=params(),
         cost_estimate=LIGHT,
@@ -1118,97 +1060,45 @@
     )(places, *halves, *flags, *filled)
 
 
-PLAN = {
-    'project': (0, 0),
-    'q1': (2, 2),
-    'q2': (2, 2),
-    'q3': (2, 2),
-    'mult': (2, 2),
-    'd_active': (2, 2),
-    'kv0': (4, 4),
-    'kv1': (4, 4),
-    'kv2': (5, 5),
-    'kv3': (4, 4),
-    'cot1': (4, 8),
-    'cot2': (4, 8),
-    'cot3': (4, 8),
-    'norm_near': (4, 6),
-    'attend': (6, 6),
-    'ctx1': (8, 8),
-    'ctx2': (8, 8),
-    'ctx3': (8, 8),
-    'middle': (10, 10),
-    'a1': (12, 12),
-    'a2': (12, 12),
-    'a3': (12, 12),
-    'dc1': (12, 12),
-    'dc2': (12, 12),
-    'norm_far': (10, 10),
-    'layer_out': (13, 15),
-    'b1': (13, 15),
-    'b2': (13, 15),
-    'b3': (13, 15),
-    'first_grad': (14, 14),
-    'one_core': (14, 14),
-    'one_z1': (15, 15),
-    'attend_back': (12, 12),
-    'far': (14, 14),
-    'one_z2': (16, 16),
-    'second_grad': (16, 16),
-    'two_core': (17, 17),
-    'head_grad': (15, 15),
-    'head_core': (15, 15),
-    'head_x': (16, 16),
-    'head_y': (16, 16),
-    'head_d': (16, 16),
-    'head_sum': (17, 17),
-    'two_z1': (18, 18),
-    'one_near': (17, 18),
-    'two_z2': (20, 20),
-    'one_far': (20, 20),
-    'one_nx': (20, 20),
-    'one_ny': (20, 20),
-    'two_near': (22, 22),
-    'one_fx': (22, 22),
-    'one_fy': (22, 22),
-    'back_z1': (17, 18),
-    'two_far': (24, 24),
-    'two_nx': (24, 24),
-    'two_ny': (24, 24),
-    'one_nd': (25, 26),
-    'one_fd': (25, 26),
-    'back_z2': (24, 25),
-    'two_fx': (25, 26),
-    'two_fy': (25, 26),
-    'input_grad': (26, 26),
-    'tiny_core': (17, 18),
-    'two_nd': (28, 28),
-    'two_fd': (28, 28),
-    'tiny_x': (22, 25),
-    'tiny_y': (28, 99),
-    'tiny_z1': (18, 20),
-    'tiny_z2': (20, 22),
-    'one_all': (17, 18),
-    'put_own': (25, 25),
-    'put_rest': (28, 28),
-    'put_two': (32, 99),
-    'one_cn0': (22, 24),
-    'one_cf0': (25, 26),
-    'two_cn0': (26, 28),
-    'two_cf0': (26, 28),
-    'one_cn1': (22, 24),
-    'one_cf1': (25, 26),
-    'two_cn1': (26, 28),
-    'two_cf1': (28, 30),
-    'one_cn2': (22, 24),
-    'one_cf2': (25, 26),
-    'two_cn2': (26, 28),
-    'two_cf2': (28, 30),
-    'one_cn3': (28, 28),
-    'one_cf3': (28, 28),
-    'two_cn3': (28, 30),
-    'two_cf3': (30, 30),
-}
+PLAN = dict(
+    project=(0, 0), q1=(2, 2), q2=(2, 2), q3=(2, 2), mult=(2, 2), d_active=(2, 2), kv0=(4, 4),
+    kv1=(4, 4), kv2=(5, 5), kv3=(4, 4), cot1=(4, 8), cot2=(4, 8), cot3=(4, 8), norm_near=(4, 6),
+    attend=(6, 6), ctx1=(8, 8), ctx2=(8, 8), ctx3=(8, 8), middle=(10, 10), a1=(12, 12), a2=(12, 12),
+    a3=(12, 12), dc1=(12, 12), dc2=(12, 12), norm_far=(10, 10), layer_out=(13, 15), b1=(13, 15),
+    b2=(13, 15), b3=(13, 15), first_grad=(14, 14), one_core=(14, 14), one_z1=(15, 15),
+    attend_back=(12, 12), far=(14, 14), one_z2=(16, 16), second_grad=(16, 16), two_core=(17, 17),
+    head_grad=(15, 15), head_core=(15, 15), head_x=(16, 16), head_y=(16, 16), head_d=(16, 16),
+    head_sum=(17, 17), two_z1=(18, 18), one_near=(17, 18), two_z2=(20, 20), one_far=(20, 20),
+    one_nx=(20, 20), one_ny=(20, 20), two_near=(22, 22), one_fx=(22, 22), one_fy=(22, 22),
+    back_z1=(16, 18), two_far=(24, 24), two_nx=(24, 24), two_ny=(24, 24), one_nd=(25, 26),
+    one_fd=(25, 26), back_z2=(24, 25), two_fx=(25, 26), two_fy=(25, 26), input_grad=(26, 26),
+    tiny_core=(17, 18), two_nd=(27, 28), two_fd=(27, 28), tiny_x=(18, 18), tiny_y=(20, 20),
+    tiny_z1=(22, 22), tiny_z2=(28, 30), one_all=(17, 18), put_own=(25, 25), put_rest=(28, 28),
+    put_two=(32, 99), one_cn0=(22, 24), one_cf0=(26, 26), two_cn0=(28, 30), two_cf0=(28, 30),
+    one_cn1=(22, 24), one_cf1=(26, 26), two_cn1=(28, 30), two_cf1=(28, 30), one_cn2=(22, 24),
+    one_cf2=(26, 26), two_cn2=(28, 30), two_cf2=(28, 30), one_cn3=(27, 27), one_cf3=(27, 27),
+    two_cn3=(28, 30), two_cf3=(30, 30), tiny_out=(30, 99),
+)
+
+
+class Name(str):
+    def __getitem__(self, index):
+        return Name(self + "." + str(index))
+
+    def __call__(self, k):
+        return Name(self + str(k))
+
+    def __getattr__(self, part):
+        return Name(self + "_" + part)
+
+
+class Names:
+    def __getattr__(self, name):
+        return Name(name)
+
+
+def free(name):
+    return "!" + name
 
 
 def run_steps(steps, known):
@@ -1250,7 +1140,7 @@
         keys = set()
         for n in ending:
             many = isinstance(made[n], (list, tuple))
-            if n.startswith("put_"):
+            if n.startswith(Names().put):
                 keys.add((n, len(made[n]) - 1))
             elif many:
                 keys.update((n, i) for i in range(len(made[n])))
@@ -1464,12 +1354,12 @@
         )[0]
 
     layout_one = (
-        (quarter // GROUP, width // LANES, "eighth", None, 0, 0),
-        (width // GROUP, early // LANES, None, "eighth", quarter, 0),
+        (quarter // GROUP, width // LANES, 0, None, 0, 0),
+        (width // GROUP, early // LANES, None, 0, quarter, 0),
     )
     layout_two = (
-        (width // GROUP, late // LANES, None, "eighth", quarter, early),
-        (part // GROUP, mid // LANES, "row", "column", mid, 0),
+        (width // GROUP, late // LANES, None, 0, quarter, early),
+        (part // GROUP, mid // LANES, 1, 2, mid, 0),
     )
     size_one, size_two = (rows_one + rows_three) // GROUP, rows_two // GROUP
     shapes_one, shapes_two = ((fan, width), (width, fan)), ((width, fan), (width, width))
@@ -1487,7 +1377,7 @@
         skip = rows_one // GROUP
         return pl.pallas_call(
             functools.partial(put_rest_kernel, layout_one, size_one, skip, the_rest),
-            in_specs=smem + anywhere * 16 + vmem(1) + anywhere * 2,
+            in_specs=smem + vmem(17) + anywhere * 2,
             out_specs=anywhere * 5 + vmem(1),
             out_shape=[shaped(shape, F32) for shape in shapes_one]
             + [shaped((width, width), F32)] * 3
@@ -1497,11 +1387,8 @@
                 for share, blocks, *_ in layout_one
             ]
             + [
-                box(len(the_rest), 2, 2, skip, LANES),
                 box(2, 3 * width, mid),
                 box32(2, 3, mid // LANES, LANES, width),
-                pltpu.SemaphoreType.DMA((len(the_rest), 2, 2)),
-                pltpu.SemaphoreType.DMA((2, GROUP, GROUP, mid // LANES)),
                 pltpu.SemaphoreType.DMA((len(the_rest), 2)),
                 pltpu.SemaphoreType.DMA((2, 3, mid // LANES)),
             ],
@@ -1534,128 +1421,128 @@
 
     below = lambda *parts: jnp.concatenate(parts, axis=0)
     cot = cotangent[0]
-    todo = {
-        "project": (("tokens",), project),
-        "mult": (("rand",), multiplicity),
-        "d_active": (("cot",), lambda c: dense_back(c, w_down)),
-    }
+    n, todo = Names(), {}
+    todo[n.project] = ((n.tokens,), project)
+    todo[n.mult] = ((n.rand,), multiplicity)
+    todo[n.d_active] = ((n.cot,), lambda c: dense_back(c, w_down))
     for k in range(1, GROUP):
-        todo[f"q{k}"] = ((f"project.{k + 1}",), functools.partial(over_z, step=k))
-        todo[f"cot{k}"] = (("cot",), functools.partial(over_item, step=k))
-        todo[f"ctx{k}"] = ((f"attend.{k}",), functools.partial(over_z, step=k))
-    own = ["project.1", "q1", "q2", "q3"]
+        todo[n.q(k)] = ((n.project[k + 1],), functools.partial(over_z, step=k))
+        todo[n.cot(k)] = ((n.cot,), functools.partial(over_item, step=k))
+        todo[n.ctx(k)] = ((n.attend[k],), functools.partial(over_z, step=k))
+    own = [n.project[1], n.q1, n.q2, n.q3]
     for k in range(GROUP):
-        todo[f"kv{k}"] = ((own[k],), lambda v: over_core(v[part:]))
-    other = [f"kv{k}" for k in range(GROUP)]
-    todo["attend"] = ((*own, *other, "mult"), attend)
-    todo["norm_near"] = (("project.0",), lambda v: below(v, over_z(v, 2)))
-    todo["norm_far"] = (("norm_near",), lambda v: over_z(v, 1))
-    todo["middle"] = (("attend.0", "ctx1", "ctx2", "ctx3", "d_active", "cot"), middle_step)
-    todo["layer_out"] = (
-        ("middle.10", "middle.11"),
+        todo[n.kv(k)] = ((own[k],), lambda v: over_core(v[part:]))
+    other = [n.kv(k) for k in range(GROUP)]
+    todo[n.attend] = ((*own, *other, n.mult), attend)
+    todo[n.norm_near] = ((n.project[0],), lambda v: below(v, over_z(v, 2)))
+    todo[n.norm_far] = ((n.norm_near,), lambda v: over_z(v, 1))
+    todo[n.middle] = ((n.attend[0], n.ctx1, n.ctx2, n.ctx3, n.d_active, n.cot), middle_step)
+    todo[n.layer_out] = (
+        (n.middle[10], n.middle[11]),
         lambda m, a: (m + dense_rows(a, w_down) + bias_down).astype(BF),
     )
     for k in range(1, GROUP):
-        todo[f"a{k}"] = ((f"middle.{k}",), functools.partial(over_item, step=k))
-        todo[f"b{k}"] = ((f"middle.{4 + k}",), functools.partial(over_item, step=k))
-    todo["dc1"] = (("middle.9",), lambda v: over_z(v, 1))
-    todo["dc2"] = (("middle.8", "dc1"), lambda v, c: over_z(below(v[part:], c[part:]), 2))
-    firsts = ["middle.0", "a1", "a2", "a3"]
-    seconds = ["middle.4", "b1", "b2", "b3"]
-    todo["first_grad"] = ((*firsts, "cot", "cot1", "cot2", "cot3"), first_grad)
+        todo[n.a(k)] = ((n.middle[k],), functools.partial(over_item, step=k))
+        todo[n.b(k)] = ((n.middle[4 + k],), functools.partial(over_item, step=k))
+    todo[n.dc1] = ((n.middle[9],), lambda v: over_z(v, 1))
+    todo[n.dc2] = ((n.middle[8], n.dc1), lambda v, c: over_z(below(v[part:], c[part:]), 2))
+    firsts = [n.middle[0], n.a1, n.a2, n.a3]
+    seconds = [n.middle[4], n.b1, n.b2, n.b3]
+    todo[n.first_grad] = ((*firsts, n.cot, n.cot1, n.cot2, n.cot3), first_grad)
     def pair_up(half, kept, given):
         far = over_z((kept[half:] + given[half:].astype(F32)).astype(BF), 1)
         return kept[:half] + given[:half].astype(F32) + far.astype(F32)
 
-    todo["one_core"] = (("first_grad.1",), over_core)
-    todo["one_z1"] = (
-        ("first_grad.0", "one_core"),
+    todo[n.one_core] = ((n.first_grad[1],), over_core)
+    todo[n.one_z1] = (
+        (n.first_grad[0], n.one_core),
         functools.partial(pair_up, half_one),
     )
-    todo["one_z2"] = (("one_z1",), lambda v: last_sum(v, over_z(second_half(v), 2)))
-    todo["attend_back"] = (
-        (*own, *other, "mult", "attend.4", "attend.5", "middle.8", "dc1", "dc2"),
+    todo[n.one_z2] = ((n.one_z1,), lambda v: last_sum(v, over_z(second_half(v), 2)))
+    todo[n.attend_back] = (
+        (*own, *other, n.mult, n.attend[4], n.attend[5], n.middle[8], n.dc1, n.dc2),
         attend_back,
     )
-    todo["far"] = (("attend_back.2",), over_core)
-    todo["second_grad"] = ((*firsts, *seconds), second_grad)
-    todo["two_core"] = (("second_grad.1",), over_core)
-    todo["two_z1"] = (
-        ("second_grad.0", "two_core"),
+    todo[n.far] = ((n.attend_back[2],), over_core)
+    todo[n.second_grad] = ((*firsts, *seconds), second_grad)
+    todo[n.two_core] = ((n.second_grad[1],), over_core)
+    todo[n.two_z1] = (
+        (n.second_grad[0], n.two_core),
         functools.partial(pair_up, half_two),
     )
-    todo["head_grad"] = (
-        ("attend_back.0", "attend_back.1", "far", "norm_near", "norm_far"),
+    todo[n.head_grad] = (
+        (n.attend_back[0], n.attend_back[1], n.far, n.norm_near, n.norm_far),
         head_grad,
     )
-    todo["head_core"] = (("head_grad.2", "head_grad.3"), lambda k, g: k + over_core(g).astype(F32))
-    for k, name in enumerate("xyd"):
-        todo[f"head_{name}"] = (
-            ("head_core",),
+    todo[n.head_core] = ((n.head_grad[2], n.head_grad[3]), lambda k, g: k + over_core(g).astype(F32))
+    for k, name in enumerate((n.head_x, n.head_y, n.head_d)):
+        todo[name] = (
+            (n.head_core,),
             lambda v, k=k + 1: over_item(rows_of(v, k).astype(BF), k),
         )
-    todo["head_sum"] = (("head_core", "head_x", "head_y", "head_d"), head_sum)
-    todo["two_z2"] = (("two_z1",), lambda v: last_sum(v, over_z(second_half(v), 2)))
-    todo["one_all"] = (("one_z2", "head_sum"), below)
-    pieces = {}
-    for name, total in (("one", "one_all"), ("two", "two_z2")):
-        todo[f"{name}_near"] = ((total,), lambda v: below(v, over_z(v, 2)))
-        todo[f"{name}_far"] = ((f"{name}_near",), lambda v: over_z(v, 1))
-        todo[f"{name}_nx"] = ((f"{name}_near",), lambda v: over_item(v, 1))
-        todo[f"{name}_ny"] = ((f"{name}_near",), lambda v: over_item(v, 2))
-        todo[f"{name}_fx"] = ((f"{name}_far",), lambda v: over_item(v, 1))
-        todo[f"{name}_fy"] = ((f"{name}_far",), lambda v: over_item(v, 2))
-        todo[f"{name}_nd"] = ((f"{name}_nx",), lambda v: over_item(v, 2))
-        todo[f"{name}_fd"] = ((f"{name}_fy",), lambda v: over_item(v, 1))
-        flat = []
-        for k, end in enumerate(("", "x", "y", "d")):
-            halves = ("near", "far") if k == 0 else ("n" + end, "f" + end)
-            halves = [f"{name}_{h}" for h in halves]
-            flat += halves
-            todo[f"{name}_cn{k}"] = (tuple(halves[:1]), over_core)
-            todo[f"{name}_cf{k}"] = (tuple(halves[1:]), over_core)
-        mirrored = [f"{name}_c{h}{k}" for k in range(GROUP) for h in "nf"]
-        pieces[name] = (flat, mirrored)
-    own_one, mirrored_one = pieces["one"]
-    todo["put_own"] = (tuple(own_one[:6]), put_own)
-    todo["put_rest"] = (
-        (*own_one, *mirrored_one, "put_own.2", "!put_own.0", "!put_own.1"),
+    todo[n.head_sum] = ((n.head_core, n.head_x, n.head_y, n.head_d), head_sum)
+    todo[n.two_z2] = ((n.two_z1,), lambda v: last_sum(v, over_z(second_half(v), 2)))
+    todo[n.one_all] = ((n.one_z2, n.head_sum), below)
+    pieces = []
+    for name, total in ((n.one, n.one_all), (n.two, n.two_z2)):
+        todo[name.near] = ((total,), lambda v: below(v, over_z(v, 2)))
+        todo[name.far] = ((name.near,), lambda v: over_z(v, 1))
+        todo[name.nx] = ((name.near,), lambda v: over_item(v, 1))
+        todo[name.ny] = ((name.near,), lambda v: over_item(v, 2))
+        todo[name.fx] = ((name.far,), lambda v: over_item(v, 1))
+        todo[name.fy] = ((name.far,), lambda v: over_item(v, 2))
+        todo[name.nd] = ((name.nx,), lambda v: over_item(v, 2))
+        todo[name.fd] = ((name.fy,), lambda v: over_item(v, 1))
+        nears, fars = (name.near, name.nx, name.ny, name.nd), (name.far, name.fx, name.fy, name.fd)
+        flat, mirrored = [], []
+        for k, halves in enumerate(zip(nears, fars)):
+            for half, crossed in zip(halves, (name.cn(k), name.cf(k))):
+                todo[crossed] = ((half,), over_core)
+                flat.append(half)
+                mirrored.append(crossed)
+        pieces.append((flat, mirrored))
+    own_one, mirrored_one = pieces[0]
+    todo[n.put_own] = (tuple(own_one[:6]), put_own)
+    todo[n.put_rest] = (
+        (*own_one, *mirrored_one, n.put_own[2], free(n.put_own[0]), free(n.put_own[1])),
         put_rest,
     )
-    todo["put_two"] = (
-        (*pieces["two"][0], *pieces["two"][1], "put_rest.5", "!put_rest.1"),
+    todo[n.put_two] = (
+        (*pieces[1][0], *pieces[1][1], n.put_rest[5], free(n.put_rest[1])),
         put_two,
     )
-    todo["back_z1"] = (("head_grad.1",), lambda v: over_z(v, 1))
-    todo["back_z2"] = (
-        ("head_grad.0", "back_z1"),
+    todo[n.back_z1] = ((n.head_grad[1],), lambda v: over_z(v, 1))
+    todo[n.back_z2] = (
+        (n.head_grad[0], n.back_z1),
         lambda v, c: over_z(below(v[size:], c[size:]), 2),
     )
-    todo["input_grad"] = (
-        ("head_grad.0", "back_z1", "back_z2", "middle.12"),
+    todo[n.input_grad] = (
+        (n.head_grad[0], n.back_z1, n.back_z2, n.middle[12]),
         input_grad,
     )
-    todo["tiny_core"] = (
-        ("middle.13", "head_grad.4"),
+    todo[n.tiny_core] = (
+        (n.middle[13], n.head_grad[4]),
         lambda u, v: below(u, v) + over_core(below(u, v)),
     )
-    todo["tiny_z1"] = (("tiny_core",), lambda v: v + over_z(v, 1))
-    todo["tiny_z2"] = (("tiny_z1",), lambda v: v + over_z(v, 2))
-    todo["tiny_x"] = (("tiny_z2",), lambda v: v + over_item(v, 1))
-    todo["tiny_y"] = (("tiny_x",), lambda v: v + over_item(v, 2))
+    todo[n.tiny_x] = ((n.tiny_core,), lambda v: v + over_item(v, 1))
+    todo[n.tiny_y] = ((n.tiny_x,), lambda v: v + over_item(v, 2))
+    todo[n.tiny_z1] = ((n.tiny_y,), lambda v: v + over_z(v, 1))
+    todo[n.tiny_z2] = ((n.tiny_z1,), lambda v: v + over_z(v, 2))
+    def tiny_out(v):
+        flat, cuts, at = v.reshape(-1), [], 0
+        for length in (fan,) + (width,) * 8:
+            cuts.append(flat[at : at + length])
+            at += length
+        return cuts
+
+    todo[n.tiny_out] = ((n.tiny_z2,), tiny_out)
     made = run_steps(
-        todo, {"tokens": tokens[0], "rand": rand_blocks, "cot": cot}
-    )
-    tiny = made["tiny_y"]
-    layer_out, grad_tokens = made["layer_out"], made["input_grad"]
-    grad_down, grad_qkv = made["put_rest"][0], made["put_rest"][2:5]
-    grad_up, grad_out, _ = made["put_two"]
-    tiny = tiny.reshape(-1)
-    cuts, at = [], 0
-    for size in (fan,) + (width,) * 8:
-        cuts.append(tiny[at : at + size])
-        at += size
-    g_bu, g_fg, g_fs, g_bd, g_bo, g_ag, g_as, g_bq, g_bv = cuts
+        todo, {n.tokens: tokens[0], n.rand: rand_blocks, n.cot: cot}
+    )
+    layer_out, grad_tokens = made[n.layer_out], made[n.input_grad]
+    grad_down, grad_qkv = made[n.put_rest][0], made[n.put_rest][2:5]
+    grad_up, grad_out, _ = made[n.put_two]
+    g_bu, g_fg, g_fs, g_bd, g_bo, g_ag, g_as, g_bq, g_bv = made[n.tiny_out]
     return (
         layer_out[None],
         grad_tokens[None],

time: 234 us -> 226 us (0.966)
  starting transfers between devices: 75.7 us -> 63 us
  waiting for transfers between devices: 68.6 us -> 74 us
    ppermute x26, waiting for transfers between devices: 11.6 us -> 25.4 us  [over_item(): return lax.ppermute(value, 'item', [(i, i ^ step) for i in range(count)])]
    ppermute x22, waiting for transfers between devices: 54.7 us -> 46.7 us  [over_z(): return lax.ppermute(value, 'seq', [(i, i ^ 2 * step) for i in range(count)])]
    ppermute x22, starting transfers between devices: 36.4 us -> 29.8 us  [over_z(): return lax.ppermute(value, 'seq', [(i, i ^ 2 * step) for i in range(count)])]
    ppermute x26, starting transfers between devices: 34.4 us -> 28.1 us  [over_item(): return lax.ppermute(value, 'item', [(i, i ^ step) for i in range(count)])]
    unnamed x155 -> x147, local copies, waits for them, and re-layouts: 4.87 us -> 3.99 us
  transfers between devices with their start and end apart: 73 -> 73, of which waited for: 23 -> 26; matrix products, arithmetic and copies ran while one was open for 5% -> 5% of each run, Pallas kernels for 24% -> 25%
where the time goes in v2:
time: 226 us
  waiting for transfers between devices  74 us (33%)
  Pallas kernels  70.4 us (31%)
  starting transfers between devices  63 us (28%)
  local copies, waits for them, and re-layouts  7.11 us (3%)
  matrix products  5.9 us (3%)
  other arithmetic  3.34 us (1%)
    ppermute x22, waiting for transfers between devices, over_z(): return lax.ppermute(value, 'seq', [(i, i ^ 2 * step) for i in range(count)])  46.7 us
    ppermute x22, starting transfers between devices, over_z(): return lax.ppermute(value, 'seq', [(i, i ^ 2 * step) for i in range(count)])  29.8 us
    ppermute x26, starting transfers between devices, over_item(): return lax.ppermute(value, 'item', [(i, i ^ step) for i in range(count)])  28.1 us
    ppermute x26, waiting for transfers between devices, over_item(): return lax.ppermute(value, 'item', [(i, i ^ step) for i in range(count)])  25.4 us
    pallas_call x2, Pallas kernels, put_pieces(): pl.pallas_call(functools.partial(put_pieces_kernel, layout, size, which),...  11.3 us
    pallas_call x1, Pallas kernels, put_rest(): pl.pallas_call(functools.partial(put_rest_kernel, layout_one, size_one, s...  10.4 us
    pallas_call x1, Pallas kernels, middle_step(): kernel(middle_kernel, smem + vmem(5) + anywhere + vmem(3) + anywhere + vm...  10.3 us
    pallas_call x1, Pallas kernels, attend_back(): kernel(functools.partial(attend_back_kernel, heads), vmem(14), [shaped((p...  7.49 us
  transfers between devices with their start and end apart: 73, of which 26 were waited for; matrix products, arithmetic and copies ran while one was open for 5% of the time, Pallas kernels for 25%

profile of v2, /device:TPU:0, one launch (start us, length us, event | category | flops | bytes accessed | tf_op | source)
XLA Modules:
  0.0 225.6 jit_solution(13778348242776697963)
XLA Ops:
  1.3 4.3 %project.1 = (bf16[128,768]{1,0:T(8,128)(2,1)}, bf16[576,128]{1,0:T(8,128)(2,1)}, bf16[576,128]{1,0:T(8,128)(2,1)}, bf16[576,128]{1,0:T(8,128)(2,1)}, bf16[576,128]{1,0:T(8,128)(2,1)}) custom-call(s32[3]{0:T(128)} %pad_add_fusion.place_ref, bf16[128,768]{1,0:T(8,128)(2,1)} %bitcast.49, bf16[768,768]{1,0:T(8,128)(2,1)} %wq_hbm.3, bf16[768,768]{1,0:T(8,128)(2,1)} %wk_hbm.3, ...), custom_call_target="tpu_custom_call" | custom-call | flops 1000000 | bytes 100000 | tf_op jit(solution)/shard_map/project/pallas_call | solution.py:1238
  5.7 3.1 %collective-permute-start = (bf16[576,128]{1,0:T(8,128)(2,1)}, bf16[576,128]{1,0:T(8,128)(2,1)S(1)}, u32[]{:S(2)}, u32[]{:S(2)}) collective-permute-start(bf16[576,128]{1,0:T(8,128)(2,1)} %get-tuple-element.289), channel_id=1, source_target_pairs={{0,2},{1,3},{2,0},{3,1},{4,6},{5,7},{6,4},{7,5},{8,10},{9,11},{10,... | collective-permute-start | bytes 442376 | tf_op jit(solution)/shard_map/ppermute | solution.py:503
  8.8 2.6 %collective-permute-start.1 = (bf16[576,128]{1,0:T(8,128)(2,1)}, bf16[576,128]{1,0:T(8,128)(2,1)S(1)}, u32[]{:S(2)}, u32[]{:S(2)}) collective-permute-start(bf16[576,128]{1,0:T(8,128)(2,1)} %get-tuple-element.290), channel_id=1, source_target_pairs={{0,4},{1,5},{2,6},{3,7},{4,0},{5,1},{6,2},{7,3},{8,12},{9,13},{10,... | collective-permute-start | bytes 442376 | tf_op jit(solution)/shard_map/ppermute | solution.py:503
  11.4 5.1 %fusion.5.d_active_hbm = f32[128,3072]{1,0:T(8,128)} fusion(bf16[128,768]{1,0:T(8,128)(2,1)S(1)} %bitcast.54, bf16[3072,768]{1,0:T(8,128)(2,1)} %param.25), kind=kOutput, calls=%fused_computation.37 | convolution fusion | flops 603979776 | bytes 6488064 | tf_op jit(solution)/shard_map/dot_general | solution.py:101
  17.5 1.4 multiplicity.1.refs_8_
  18.9 4.1 %collective-permute-done.1.refs_2_ = bf16[576,128]{1,0:T(8,128)(2,1)S(1)} collective-permute-done((bf16[576,128]{1,0:T(8,128)(2,1)}, bf16[576,128]{1,0:T(8,128)(2,1)S(1)}, u32[]{:S(2)}, u32[]{:S(2)}) %collective-permute-start.1) | collective-permute-done | bytes 147488 | tf_op jit(solution)/shard_map/ppermute | solution.py:503
  23.8 3.3 %collective-permute-start.7 = (bf16[128,768]{1,0:T(8,128)(2,1)S(1)}, bf16[128,768]{1,0:T(8,128)(2,1)S(1)}, u32[]{:S(2)}, u32[]{:S(2)}) collective-permute-start(bf16[128,768]{1,0:T(8,128)(2,1)S(1)} %copy-done.61), channel_id=1, source_target_pairs={{0,4},{1,5},{2,6},{3,7},{4,0},{5,1},{6,2},{7,3},{8,12},{9,13},{10,... | collective-permute-start | bytes 589832 | tf_op jit(solution)/shard_map/ppermute | solution.py:503
  27.4 1.5 collective-permute-start.8
  28.9 1.5 collective-permute-start.9
  31.6 5.3 %attend.1 = (bf16[192,128]{1,0:T(8,128)(2,1)}, bf16[192,128]{1,0:T(8,128)(2,1)}, bf16[192,128]{1,0:T(8,128)(2,1)}, bf16[192,128]{1,0:T(8,128)(2,1)}, f32[192,512]{1,0:T(8,128)}, /*index=5*/f32[3,1,512]{2,1,0:T(1,128)}) custom-call(bf16[576,128]{1,0:T(8,128)(2,1)} %get-tuple-element.350.refs_0_, bf16[576,128]{1,0:T(8,128)(2,1)} %copy-done.15, ...), custom_call_target="tpu_custom_call" | custom-call | flops 1000000 | bytes 100000 | tf_op jit(solution)/shard_map/attend/pallas_call | solution.py:1255
  37.2 2.0 collective-permute-start.12
  39.2 2.2 collective-permute-start.13
  41.6 2.4 %collective-permute-done.12.ctx2 = bf16[192,128]{1,0:T(8,128)(2,1)S(1)} collective-permute-done((bf16[192,128]{1,0:T(8,128)(2,1)}, bf16[192,128]{1,0:T(8,128)(2,1)S(1)}, u32[]{:S(2)}, u32[]{:S(2)}) %collective-permute-start.12) | collective-permute-done | bytes 49184 | tf_op jit(solution)/shard_map/ppermute | solution.py:503
  45.9 10.3 %middle.1 = (bf16[1792,128]{1,0:T(8,128)(2,1)}, bf16[1792,128]{1,0:T(8,128)(2,1)}, bf16[1792,128]{1,0:T(8,128)(2,1)}, bf16[1792,128]{1,0:T(8,128)(2,1)}, bf16[12...) custom-call(s32[3]{0:T(128)} %pad_add_fusion.place_ref, ...), custom_call_target="tpu_custom_call" | custom-call | flops 1000000 | bytes 100000 | tf_op jit(solution)/shard_map/middle/pallas_call | solution.py:1264
  56.2 1.6 collective-permute-start.15
  57.8 1.5 collective-permute-start.16
  59.8 1.5 collective-permute-start.18
  62.0 2.6 %collective-permute-done.18.refs_12_ = bf16[384,128]{1,0:T(8,128)(2,1)S(1)} collective-permute-done((bf16[384,128]{1,0:T(8,128)(2,1)}, bf16[384,128]{1,0:T(8,128)(2,1)S(1)}, u32[]{:S(2)}, u32[]{:S(2)}) %collective-permute-start.18) | collective-permute-done | bytes 98336 | tf_op jit(solution)/shard_map/ppermute | solution.py:503
  64.6 3.3 %collective-permute-start.19 = (bf16[384,128]{1,0:T(8,128)(2,1)S(1)}, bf16[384,128]{1,0:T(8,128)(2,1)S(1)}, u32[]{:S(2)}, u32[]{:S(2)}) collective-permute-start(bf16[384,128]{1,0:T(8,128)(2,1)S(1)} %pad_maximum_fusion.5), channel_id=1, source_target_pairs={{0,4},{1,5},{2,6},{3,7},{4,0},{5,1},{6,2},{7,3},{8,12},{9,13},{10,... | collective-permute-start | bytes 294920 | tf_op jit(solution)/shard_map/ppermute | solution.py:503
  67.9 3.6 %collective-permute-done.19.refs_13_ = bf16[384,128]{1,0:T(8,128)(2,1)S(1)} collective-permute-done((bf16[384,128]{1,0:T(8,128)(2,1)S(1)}, bf16[384,128]{1,0:T(8,128)(2,1)S(1)}, u32[]{:S(2)}, u32[]{:S(2)}) %collective-permute-start.19) | collective-permute-done | bytes 98336 | tf_op jit(solution)/shard_map/ppermute | solution.py:503
  72.2 7.5 %attend_back.1 = (bf16[192,512]{1,0:T(8,128)(2,1)}, f32[384,512]{1,0:T(8,128)}, bf16[384,512]{1,0:T(8,128)(2,1)}) custom-call(bf16[576,128]{1,0:T(8,128)(2,1)} %get-tuple-element.350.refs_0_, bf16[576,128]{1,0:T(8,128)(2,1)} %copy-done.15, bf16[576,128]{1,0:T(8,128)(2,1)} %copy-done.16, bf16[576,128]{1,0:T(8,128)(2,1)} %copy-done.17, ...), custom_call_target="tpu_custom_call" | custom-call | flops 1000000 | bytes 100000 | tf_op jit(solution)/shard_map/attend_back/pallas_call | solution.py:1288
  80.8 4.1 %first_grad.1 = (f32[3072,128]{1,0:T(8,128)}, bf16[3072,128]{1,0:T(8,128)(2,1)}) custom-call(s32[3]{0:T(128)} %pad_add_fusion.place_ref, bf16[1792,128]{1,0:T(8,128)(2,1)} %get-tuple-element.417.refs_0_, bf16[1792,128]{1,0:T(8,128)(2,1)} %copy-done.6, bf16[1792,128]{1,0:T(8,128)(2,1)} %copy-done.7, bf16[1792,128]{1,0:T(8,128)(2,1)} %copy-done.8, ...), custom_call_target="tpu_custom_call" | custom-call | flops 1000000 | bytes 100000 | tf_op jit(solution)/shard_map/first_grad/pallas_call | solution.py:1300
  85.5 1.5 collective-permute-start.20
  87.4 1.6 collective-permute-start.22
  92.5 6.2 %head_grad.1 = (bf16[1152,128]{1,0:T(8,128)(2,1)}, bf16[1152,128]{1,0:T(8,128)(2,1)}, f32[1728,128]{1,0:T(8,128)}, bf16[1728,128]{1,0:T(8,128)(2,1)}, f32[24,128]{1,0:T(8,128)}) custom-call(s32[3]{0:T(128)} %pad_add_fusion.place_ref, bf16[192,512]{1,0:T(8,128)(2,1)} %get-tuple-element.396.dq_ref, f32[384,512]{1,0:T(8,128)} %get-tuple-element.397.dkv_ref, ...), custom_call_target="tpu_custom_call" | custom-call | flops 1000000 | bytes 100000 | tf_op jit(solution)/shard_map/head_grad/pallas_call | solution.py:1328
  98.8 1.9 collective-permute-done.26
  100.9 2.7 %collective-permute-done.21.refs_6_ = bf16[1280,128]{1,0:T(8,128)(2,1)S(1)} collective-permute-done((bf16[1280,128]{1,0:T(8,128)(2,1)}, bf16[1280,128]{1,0:T(8,128)(2,1)S(1)}, u32[]{:S(2)}, u32[]{:S(2)}) %collective-permute-start.21) | collective-permute-done | bytes 327712 | tf_op jit(solution)/shard_map/ppermute | solution.py:513
  103.7 1.9 collective-permute-start.31
  105.7 1.5 collective-permute-start.28
  107.2 1.5 collective-permute-start.29
  109.2 3.9 %second_grad.1 = (f32[2112,128]{1,0:T(8,128)}, bf16[2112,128]{1,0:T(8,128)(2,1)}) custom-call(s32[3]{0:T(128)} %pad_add_fusion.place_ref, bf16[1792,128]{1,0:T(8,128)(2,1)} %get-tuple-element.417.refs_0_, bf16[1792,128]{1,0:T(8,128)(2,1)} %copy-done.6, bf16[1792,128]{1,0:T(8,128)(2,1)} %copy-done.7, bf16[1792,128]{1,0:T(8,128)(2,1)} %copy-done.8, ...), custom_call_target="tpu_custom_call" | custom-call | flops 1000000 | bytes 100000 | tf_op jit(solution)/shard_map/second_grad/pallas_call | solution.py:1314
  113.1 1.6 collective-permute-done.31
  119.2 13.2 %collective-permute-done.32 = bf16[1200,128]{1,0:T(8,128)(2,1)S(1)} collective-permute-done((bf16[1200,128]{1,0:T(8,128)(2,1)S(1)}, bf16[1200,128]{1,0:T(8,128)(2,1)S(1)}, u32[]{:S(2)}, u32[]{:S(2)}) %collective-permute-start.32) | collective-permute-done | bytes 307232 | tf_op jit(solution)/shard_map/ppermute | solution.py:503
  134.8 2.7 %collective-permute-start.41 = (bf16[528,128]{1,0:T(8,128)(2,1)S(1)}, bf16[528,128]{1,0:T(8,128)(2,1)S(1)}, u32[]{:S(2)}, u32[]{:S(2)}) collective-permute-start(bf16[528,128]{1,0:T(8,128)(2,1)S(1)} %slice.179), channel_id=1, source_target_pairs={{0,4},{1,5},{2,6},{3,7},{4,0},{5,1},{6,2},{7,3},{8,12},{9,13},{10,... | collective-permute-start | bytes 405512 | tf_op jit(solution)/shard_map/ppermute | solution.py:503
  138.1 11.4 %collective-permute-done.40 = f32[72,128]{1,0:T(8,128)S(1)} collective-permute-done((f32[72,128]{1,0:T(8,128)S(1)}, f32[72,128]{1,0:T(8,128)S(1)}, u32[]{:S(2)}, u32[]{:S(2)}) %collective-permute-start.40) | collective-permute-done | bytes 36896 | tf_op jit(solution)/shard_map/ppermute | solution.py:513
  149.6 1.7 collective-permute-done.37.refs_1_
  155.3 3.6 %collective-permute-done.44 = f32[72,128]{1,0:T(8,128)S(1)} collective-permute-done((f32[72,128]{1,0:T(8,128)S(1)}, f32[72,128]{1,0:T(8,128)S(1)}, u32[]{:S(2)}, u32[]{:S(2)}) %collective-permute-start.44) | collective-permute-done | bytes 36896 | tf_op jit(solution)/shard_map/ppermute | solution.py:503
  158.9 4.0 %collective-permute-done.45 = bf16[528,128]{1,0:T(8,128)(2,1)S(1)} collective-permute-done((bf16[528,128]{1,0:T(8,128)(2,1)S(1)}, bf16[528,128]{1,0:T(8,128)(2,1)S(1)}, u32[]{:S(2)}, u32[]{:S(2)}) %collective-permute-start.45) | collective-permute-done | bytes 135200 | tf_op jit(solution)/shard_map/ppermute | solution.py:503
  163.0 3.0 %collective-permute-done.42.refs_3_ = bf16[2400,128]{1,0:T(8,128)(2,1)S(1)} collective-permute-done((bf16[2400,128]{1,0:T(8,128)(2,1)S(1)}, bf16[2400,128]{1,0:T(8,128)(2,1)S(1)}, u32[]{:S(2)}, u32[]{:S(2)}) %collective-permute-start.42) | collective-permute-done | bytes 614432 | tf_op jit(solution)/shard_map/ppermute | solution.py:513
  168.7 1.7 collective-permute-start.46
  170.4 6.4 %collective-permute-done.50.refs_1_ = bf16[1056,128]{1,0:T(8,128)(2,1)S(1)} collective-permute-done((bf16[1056,128]{1,0:T(8,128)(2,1)S(1)}, bf16[1056,128]{1,0:T(8,128)(2,1)S(1)}, u32[]{:S(2)}, u32[]{:S(2)}) %collective-permute-start.50) | collective-permute-done | bytes 270368 | tf_op jit(solution)/shard_map/ppermute | solution.py:503
  176.8 1.4 collective-permute-start.58
  181.1 4.9 %put_own.1 = (f32[3072,768]{1,0:T(8,128)}, f32[768,3072]{1,0:T(8,128)}, f32[8,128]{1,0:T(8,128)}) custom-call(s32[3]{0:T(128)} %pad_add_fusion.place_ref, bf16[2400,128]{1,0:T(8,128)(2,1)} %copy-done, bf16[2400,128]{1,0:T(8,128)(2,1)} %copy-done.1, bf16[2400,128]{1,0:T(8,128)(2,1)} %copy-done.2, bf16[2400,128]{1,0:T(8,128)(2,1)} %copy-done.4, ...), custom_call_target="tpu_custom_call" | custom-call | flops 1000000 | bytes 100000 | tf_op jit(solution)/shard_map/put_own/pallas_call | solution.py:1043
  187.8 5.7 %input_grad.1 = bf16[128,768]{1,0:T(8,128)(2,1)} custom-call(s32[3]{0:T(128)} %pad_add_fusion.place_ref, bf16[1152,128]{1,0:T(8,128)(2,1)} %get-tuple-element.463.back0, bf16[1152,128]{1,0:T(8,128)(2,1)} %copy-done.21, bf16[1152,128]{1,0:T(8,128)(2,1)} %copy-done.41, bf16[768,768]{1,0:T(8,128)(2,1)} %wq_hbm.3, bf16[768,768]{1,0:T(8,128)(2,1)} %wk_hbm.3, ...), custom_call_target="tpu_custom_call" | custom-call | flops 1000000 | bytes 100000 | tf_op jit(solution)/shard_map/input_grad/pallas_call | solution.py:1346
  195.2 1.7 collective-permute-start.62
  197.9 5.8 %collective-permute-done.62.refs_6_ = bf16[1056,128]{1,0:T(8,128)(2,1)S(1)} collective-permute-done((bf16[1056,128]{1,0:T(8,128)(2,1)S(1)}, bf16[1056,128]{1,0:T(8,128)(2,1)S(1)}, u32[]{:S(2)}, u32[]{:S(2)}) %collective-permute-start.62) | collective-permute-done | bytes 270368 | tf_op jit(solution)/shard_map/ppermute | solution.py:513
  204.8 10.4 %put_rest.1 = (f32[3072,768]{1,0:T(8,128)}, f32[768,3072]{1,0:T(8,128)}, f32[768,768]{1,0:T(8,128)}, f32[768,768]{1,0:T(8,128)}, f32[768,768]{1,0:T(8,128)}, /*index=5*/f32[8,128]{1,0:T(8,128)}) custom-call(s32[3]{0:T(128)} %pad_add_fusion.place_ref, bf16[2400,128]{1,0:T(8,128)(2,1)} %copy-done, ...), custom_call_target="tpu_custom_call", output_to_operand_aliasing={{0}: (18, {}), {1}: (19, {})} | custom-call | flops 1000000 | bytes 100000 | tf_op jit(solution)/shard_map/put_rest/pallas_call | solution.py:1378
  219.1 6.3 %put_two.1 = (f32[768,3072]{1,0:T(8,128)}, f32[768,768]{1,0:T(8,128)}, f32[8,128]{1,0:T(8,128)}) custom-call(s32[3]{0:T(128)} %pad_add_fusion.place_ref, bf16[1056,128]{1,0:T(8,128)(2,1)} %copy-done.12, bf16[1056,128]{1,0:T(8,128)(2,1)} %copy-done.42, bf16[1056,128]{1,0:T(8,128)(2,1)} %copy-done.43, ...), custom_call_target="tpu_custom_call", output_to_operand_aliasing={{0}: (18, {})} | custom-call | flops 1000000 | bytes 100000 | tf_op jit(solution)/shard_map/put_two/pallas_call | solution.py:1043
  (297 shorter events, 40.5 us)
Async XLA Ops:
  5.7 13.2 %collective-permute-start = (bf16[576,128]{1,0:T(8,128)(2,1)}, bf16[576,128]{1,0:T(8,128)(2,1)S(1)}, u32[]{:S(2)}, u32[]{:S(2)}) collective-permute-start(bf16[576,128]{1,0:T(8,128)(2,1)} %get-tuple-element.289), channel_id=1, source_target_pairs={{0,2},{1,3},{2,0},{3,1},{4,6},{5,7},{6,4},{7,5},{8,10},{9,11},{10,... | collective-permute-start | bytes 442376 | tf_op jit(solution)/shard_map/ppermute | solution.py:503
  8.8 14.2 %collective-permute-start.1 = (bf16[576,128]{1,0:T(8,128)(2,1)}, bf16[576,128]{1,0:T(8,128)(2,1)S(1)}, u32[]{:S(2)}, u32[]{:S(2)}) collective-permute-start(bf16[576,128]{1,0:T(8,128)(2,1)} %get-tuple-element.290), channel_id=1, source_target_pairs={{0,4},{1,5},{2,6},{3,7},{4,0},{5,1},{6,2},{7,3},{8,12},{9,13},{10,... | collective-permute-start | bytes 442376 | tf_op jit(solution)/shard_map/ppermute | solution.py:503
  11.4 11.6 %collective-permute-start.2 = (bf16[576,128]{1,0:T(8,128)(2,1)}, bf16[576,128]{1,0:T(8,128)(2,1)S(1)}, u32[]{:S(2)}, u32[]{:S(2)}) collective-permute-start(bf16[576,128]{1,0:T(8,128)(2,1)} %get-tuple-element.291), channel_id=1, source_target_pairs={{0,6},{1,7},{2,4},{3,5},{4,2},{5,3},{6,0},{7,1},{8,14},{9,15},{10,... | collective-permute-start | bytes 442376 | tf_op jit(solution)/shard_map/ppermute | solution.py:503
  23.8 13.1 %collective-permute-start.7 = (bf16[128,768]{1,0:T(8,128)(2,1)S(1)}, bf16[128,768]{1,0:T(8,128)(2,1)S(1)}, u32[]{:S(2)}, u32[]{:S(2)}) collective-permute-start(bf16[128,768]{1,0:T(8,128)(2,1)S(1)} %copy-done.61), channel_id=1, source_target_pairs={{0,4},{1,5},{2,6},{3,7},{4,0},{5,1},{6,2},{7,3},{8,12},{9,13},{10,... | collective-permute-start | bytes 589832 | tf_op jit(solution)/shard_map/ppermute | solution.py:503
  27.4 11.8 %collective-permute-start.8 = (bf16[128,768]{1,0:T(8,128)(2,1)S(1)}, bf16[128,768]{1,0:T(8,128)(2,1)S(1)}, u32[]{:S(2)}, u32[]{:S(2)}) collective-permute-start(bf16[128,768]{1,0:T(8,128)(2,1)S(1)} %bitcast.55), channel_id=1, source_target_pairs={{0,8},{8,0},{16,24},{24,16},{1,9},{9,1},{17,25},{25,17},{2,10},{10... | collective-permute-start | bytes 589832 | tf_op jit(solution)/shard_map/ppermute | solution.py:513
  28.9 12.5 %collective-permute-start.9 = (bf16[128,768]{1,0:T(8,128)(2,1)S(1)}, bf16[128,768]{1,0:T(8,128)(2,1)S(1)}, u32[]{:S(2)}, u32[]{:S(2)}) collective-permute-start(bf16[128,768]{1,0:T(8,128)(2,1)S(1)} %bitcast.56), channel_id=1, source_target_pairs={{0,16},{8,24},{16,0},{24,8},{1,17},{9,25},{17,1},{25,9},{2,18},{10... | collective-permute-start | bytes 589832 | tf_op jit(solution)/shard_map/ppermute | solution.py:513
  30.4 11.0 %collective-permute-start.10 = (bf16[128,768]{1,0:T(8,128)(2,1)S(1)}, bf16[128,768]{1,0:T(8,128)(2,1)S(1)}, u32[]{:S(2)}, u32[]{:S(2)}) collective-permute-start(bf16[128,768]{1,0:T(8,128)(2,1)S(1)} %bitcast.57), channel_id=1, source_target_pairs={{0,24},{8,16},{16,8},{24,0},{1,25},{9,17},{17,9},{25,1},{2,26},{10... | collective-permute-start | bytes 589832 | tf_op jit(solution)/shard_map/ppermute | solution.py:513
  45.3 10.9 %collective-permute-start.14 = (bf16[256,768]{1,0:T(8,128)(2,1)S(1)}, bf16[256,768]{1,0:T(8,128)(2,1)S(1)}, u32[]{:S(2)}, u32[]{:S(2)}) collective-permute-start(bf16[256,768]{1,0:T(8,128)(2,1)S(1)} %pad_maximum_fusion.1.hat0), channel_id=1, source_target_pairs={{0,2},{1,3},{2,0},{3,1},{4,6},{5,7},{6,4},{7,5},{8,10},{9,11},{10,... | collective-permute-start | bytes 1179656 | tf_op jit(solution)/shard_map/ppermute | solution.py:503
  56.2 23.5 %collective-permute-start.15 = (bf16[1792,128]{1,0:T(8,128)(2,1)}, bf16[1792,128]{1,0:T(8,128)(2,1)S(1)}, u32[]{:S(2)}, u32[]{:S(2)}) collective-permute-start(bf16[1792,128]{1,0:T(8,128)(2,1)} %get-tuple-element.347), channel_id=1, source_target_pairs={{0,8},{8,0},{16,24},{24,16},{1,9},{9,1},{17,25},{25,17},{2,10},{10... | collective-permute-start | bytes 1376264 | tf_op jit(solution)/shard_map/ppermute | solution.py:513
  57.8 22.0 %collective-permute-start.16 = (bf16[1792,128]{1,0:T(8,128)(2,1)}, bf16[1792,128]{1,0:T(8,128)(2,1)S(1)}, u32[]{:S(2)}, u32[]{:S(2)}) collective-permute-start(bf16[1792,128]{1,0:T(8,128)(2,1)} %get-tuple-element.348), channel_id=1, source_target_pairs={{0,16},{8,24},{16,0},{24,8},{1,17},{9,25},{17,1},{25,9},{2,18},{10... | collective-permute-start | bytes 1376264 | tf_op jit(solution)/shard_map/ppermute | solution.py:513
  59.3 20.5 %collective-permute-start.17 = (bf16[1792,128]{1,0:T(8,128)(2,1)}, bf16[1792,128]{1,0:T(8,128)(2,1)S(1)}, u32[]{:S(2)}, u32[]{:S(2)}) collective-permute-start(bf16[1792,128]{1,0:T(8,128)(2,1)} %get-tuple-element.349), channel_id=1, source_target_pairs={{0,24},{8,16},{16,8},{24,0},{1,25},{9,17},{17,9},{25,1},{2,26},{10... | collective-permute-start | bytes 1376264 | tf_op jit(solution)/shard_map/ppermute | solution.py:513
  85.5 15.4 %collective-permute-start.20 = (bf16[1280,128]{1,0:T(8,128)(2,1)}, bf16[1280,128]{1,0:T(8,128)(2,1)S(1)}, u32[]{:S(2)}, u32[]{:S(2)}) collective-permute-start(bf16[1280,128]{1,0:T(8,128)(2,1)} %get-tuple-element.382), channel_id=1, source_target_pairs={{0,8},{8,0},{16,24},{24,16},{1,9},{9,1},{17,25},{25,17},{2,10},{10... | collective-permute-start | bytes 983048 | tf_op jit(solution)/shard_map/ppermute | solution.py:513
  87.0 16.6 %collective-permute-start.21 = (bf16[1280,128]{1,0:T(8,128)(2,1)}, bf16[1280,128]{1,0:T(8,128)(2,1)S(1)}, u32[]{:S(2)}, u32[]{:S(2)}) collective-permute-start(bf16[1280,128]{1,0:T(8,128)(2,1)} %get-tuple-element.383), channel_id=1, source_target_pairs={{0,16},{8,24},{16,0},{24,8},{1,17},{9,25},{17,1},{25,9},{2,18},{10... | collective-permute-start | bytes 983048 | tf_op jit(solution)/shard_map/ppermute | solution.py:513
  87.4 16.2 %collective-permute-start.22 = (bf16[1280,128]{1,0:T(8,128)(2,1)}, bf16[1280,128]{1,0:T(8,128)(2,1)}, u32[]{:S(2)}, u32[]{:S(2)}) collective-permute-start(bf16[1280,128]{1,0:T(8,128)(2,1)} %get-tuple-element.384), channel_id=1, source_target_pairs={{0,24},{8,16},{16,8},{24,0},{1,25},{9,17},{17,9},{25,1},{2,26},{10... | collective-permute-start | bytes 983048 | tf_op jit(solution)/shard_map/ppermute | solution.py:513
  90.4 10.3 %collective-permute-start.26 = (bf16[1536,128]{1,0:T(8,128)(2,1)S(1)}, bf16[1536,128]{1,0:T(8,128)(2,1)S(1)}, u32[]{:S(2)}, u32[]{:S(2)}) collective-permute-start(bf16[1536,128]{1,0:T(8,128)(2,1)S(1)} %add_convert_fusion), channel_id=1, source_target_pairs={{0,2},{1,3},{2,0},{3,1},{4,6},{5,7},{6,4},{7,5},{8,10},{9,11},{10,... | collective-permute-start | bytes 1179656 | tf_op jit(solution)/shard_map/ppermute | solution.py:503
  103.7 11.0 %collective-permute-start.31 = (bf16[768,128]{1,0:T(8,128)(2,1)S(1)}, bf16[768,128]{1,0:T(8,128)(2,1)S(1)}, u32[]{:S(2)}, u32[]{:S(2)}) collective-permute-start(bf16[768,128]{1,0:T(8,128)(2,1)S(1)} %slice.178), channel_id=1, source_target_pairs={{0,4},{1,5},{2,6},{3,7},{4,0},{5,1},{6,2},{7,3},{8,12},{9,13},{10,... | collective-permute-start | bytes 589832 | tf_op jit(solution)/shard_map/ppermute | solution.py:503
  105.6 27.1 %collective-permute-start.27 = (bf16[1152,128]{1,0:T(8,128)(2,1)}, bf16[1152,128]{1,0:T(8,128)(2,1)S(1)}, u32[]{:S(2)}, u32[]{:S(2)}) collective-permute-start(bf16[1152,128]{1,0:T(8,128)(2,1)} %get-tuple-element.412), channel_id=1, source_target_pairs={{0,2},{1,3},{2,0},{3,1},{4,6},{5,7},{6,4},{7,5},{8,10},{9,11},{10,... | collective-permute-start | bytes 884744 | tf_op jit(solution)/shard_map/ppermute | solution.py:503
  105.7 9.1 %collective-permute-start.28 = (bf16[432,128]{1,0:T(8,128)(2,1)S(1)}, bf16[432,128]{1,0:T(8,128)(2,1)S(1)}, u32[]{:S(2)}, u32[]{:S(2)}) collective-permute-start(bf16[432,128]{1,0:T(8,128)(2,1)S(1)} %get-tuple-element.545), channel_id=1, source_target_pairs={{0,24},{8,16},{16,8},{24,0},{1,25},{9,17},{17,9},{25,1},{2,26},{10... | collective-permute-start | bytes 331784 | tf_op jit(solution)/shard_map/ppermute | solution.py:513
  115.5 16.9 %collective-permute-start.32 = (bf16[1200,128]{1,0:T(8,128)(2,1)S(1)}, bf16[1200,128]{1,0:T(8,128)(2,1)S(1)}, u32[]{:S(2)}, u32[]{:S(2)}) collective-permute-start(bf16[1200,128]{1,0:T(8,128)(2,1)S(1)} %pad_maximum_fusion.2), channel_id=1, source_target_pairs={{0,4},{1,5},{2,6},{3,7},{4,0},{5,1},{6,2},{7,3},{8,12},{9,13},{10,... | collective-permute-start | bytes 921608 | tf_op jit(solution)/shard_map/ppermute | solution.py:503
  117.0 15.4 %collective-permute-start.35 = (f32[72,128]{1,0:T(8,128)S(1)}, f32[72,128]{1,0:T(8,128)S(1)}, u32[]{:S(2)}, u32[]{:S(2)}) collective-permute-start(f32[72,128]{1,0:T(8,128)S(1)} %add.96), channel_id=1, source_target_pairs={{0,8},{8,0},{16,24},{24,16},{1,9},{9,1},{17,25},{25,17},{2,10},{10... | collective-permute-start | bytes 110600 | tf_op jit(solution)/shard_map/ppermute | solution.py:513
  117.9 14.8 %collective-permute-start.36 = (bf16[1056,128]{1,0:T(8,128)(2,1)S(1)}, bf16[1056,128]{1,0:T(8,128)(2,1)S(1)}, u32[]{:S(2)}, u32[]{:S(2)}) collective-permute-start(bf16[1056,128]{1,0:T(8,128)(2,1)S(1)} %add_convert_fusion.1), channel_id=1, source_target_pairs={{0,2},{1,3},{2,0},{3,1},{4,6},{5,7},{6,4},{7,5},{8,10},{9,11},{10,... | collective-permute-start | bytes 811016 | tf_op jit(solution)/shard_map/ppermute | solution.py:503
  132.8 18.5 %collective-permute-start.37 = (bf16[2400,128]{1,0:T(8,128)(2,1)S(1)}, bf16[2400,128]{1,0:T(8,128)(2,1)S(1)}, u32[]{:S(2)}, u32[]{:S(2)}) collective-permute-start(bf16[2400,128]{1,0:T(8,128)(2,1)S(1)} %pad_maximum_fusion.refs_0_), channel_id=1, source_target_pairs={{0,2},{1,3},{2,0},{3,1},{4,6},{5,7},{6,4},{7,5},{8,10},{9,11},{10,... | collective-permute-start | bytes 1843208 | tf_op jit(solution)/shard_map/ppermute | solution.py:503
  132.9 18.4 %collective-permute-start.38 = (bf16[2400,128]{1,0:T(8,128)(2,1)S(1)}, bf16[2400,128]{1,0:T(8,128)(2,1)S(1)}, u32[]{:S(2)}, u32[]{:S(2)}) collective-permute-start(bf16[2400,128]{1,0:T(8,128)(2,1)S(1)} %pad_maximum_fusion.refs_0_), channel_id=1, source_target_pairs={{0,8},{8,0},{16,24},{24,16},{1,9},{9,1},{17,25},{25,17},{2,10},{10... | collective-permute-start | bytes 1843208 | tf_op jit(solution)/shard_map/ppermute | solution.py:513
  133.8 17.4 %collective-permute-start.39 = (bf16[2400,128]{1,0:T(8,128)(2,1)S(1)}, bf16[2400,128]{1,0:T(8,128)(2,1)S(1)}, u32[]{:S(2)}, u32[]{:S(2)}) collective-permute-start(bf16[2400,128]{1,0:T(8,128)(2,1)S(1)} %pad_maximum_fusion.refs_0_), channel_id=1, source_target_pairs={{0,16},{8,24},{16,0},{24,8},{1,17},{9,25},{17,1},{25,9},{2,18},{10... | collective-permute-start | bytes 1843208 | tf_op jit(solution)/shard_map/ppermute | solution.py:513
  134.8 14.7 %collective-permute-start.41 = (bf16[528,128]{1,0:T(8,128)(2,1)S(1)}, bf16[528,128]{1,0:T(8,128)(2,1)S(1)}, u32[]{:S(2)}, u32[]{:S(2)}) collective-permute-start(bf16[528,128]{1,0:T(8,128)(2,1)S(1)} %slice.179), channel_id=1, source_target_pairs={{0,4},{1,5},{2,6},{3,7},{4,0},{5,1},{6,2},{7,3},{8,12},{9,13},{10,... | collective-permute-start | bytes 405512 | tf_op jit(solution)/shard_map/ppermute | solution.py:503
  137.5 12.0 %collective-permute-start.40 = (f32[72,128]{1,0:T(8,128)S(1)}, f32[72,128]{1,0:T(8,128)S(1)}, u32[]{:S(2)}, u32[]{:S(2)}) collective-permute-start(f32[72,128]{1,0:T(8,128)S(1)} %add.97), channel_id=1, source_target_pairs={{0,16},{8,24},{16,0},{24,8},{1,17},{9,25},{17,1},{25,9},{2,18},{10... | collective-permute-start | bytes 110600 | tf_op jit(solution)/shard_map/ppermute | solution.py:513
  151.3 14.7 %collective-permute-start.42 = (bf16[2400,128]{1,0:T(8,128)(2,1)S(1)}, bf16[2400,128]{1,0:T(8,128)(2,1)S(1)}, u32[]{:S(2)}, u32[]{:S(2)}) collective-permute-start(bf16[2400,128]{1,0:T(8,128)(2,1)S(1)} %collective-permute-done.37.refs_1_), channel_id=1, source_target_pairs={{0,8},{8,0},{16,24},{24,16},{1,9},{9,1},{17,25},{25,17},{2,10},{10... | collective-permute-start | bytes 1843208 | tf_op jit(solution)/shard_map/ppermute | solution.py:513
  151.9 14.1 %collective-permute-start.43 = (bf16[2400,128]{1,0:T(8,128)(2,1)S(1)}, bf16[2400,128]{1,0:T(8,128)(2,1)S(1)}, u32[]{:S(2)}, u32[]{:S(2)}) collective-permute-start(bf16[2400,128]{1,0:T(8,128)(2,1)S(1)} %collective-permute-done.37.refs_1_), channel_id=1, source_target_pairs={{0,16},{8,24},{16,0},{24,8},{1,17},{9,25},{17,1},{25,9},{2,18},{10... | collective-permute-start | bytes 1843208 | tf_op jit(solution)/shard_map/ppermute | solution.py:513
  153.3 14.4 %collective-permute-start.47 = (bf16[2400,128]{1,0:T(8,128)(2,1)S(1)}, bf16[2400,128]{1,0:T(8,128)(2,1)S(1)}, u32[]{:S(2)}, u32[]{:S(2)}) collective-permute-start(bf16[2400,128]{1,0:T(8,128)(2,1)S(1)} %pad_maximum_fusion.refs_0_), channel_id=1, source_target_pairs={{0,1},{1,0},{2,3},{3,2},{4,5},{5,4},{6,7},{7,6},{8,9},{9,8},{10,11... | collective-permute-start | bytes 1843208 | tf_op jit(solution)/shard_map/ppermute | solution.py:508
  153.3 9.6 %collective-permute-start.45 = (bf16[528,128]{1,0:T(8,128)(2,1)S(1)}, bf16[528,128]{1,0:T(8,128)(2,1)S(1)}, u32[]{:S(2)}, u32[]{:S(2)}) collective-permute-start(bf16[528,128]{1,0:T(8,128)(2,1)S(1)} %add_convert_fusion.4), channel_id=1, source_target_pairs={{0,4},{1,5},{2,6},{3,7},{4,0},{5,1},{6,2},{7,3},{8,12},{9,13},{10,... | collective-permute-start | bytes 405512 | tf_op jit(solution)/shard_map/ppermute | solution.py:503
  158.9 9.8 %collective-permute-start.48 = (bf16[2400,128]{1,0:T(8,128)(2,1)S(1)}, bf16[2400,128]{1,0:T(8,128)(2,1)S(1)}, u32[]{:S(2)}, u32[]{:S(2)}) collective-permute-start(bf16[2400,128]{1,0:T(8,128)(2,1)S(1)} %collective-permute-done.38.refs_2_), channel_id=1, source_target_pairs={{0,1},{1,0},{2,3},{3,2},{4,5},{5,4},{6,7},{7,6},{8,9},{9,8},{10,11... | collective-permute-start | bytes 1843208 | tf_op jit(solution)/shard_map/ppermute | solution.py:508
  166.0 10.7 %collective-permute-start.50 = (bf16[1056,128]{1,0:T(8,128)(2,1)S(1)}, bf16[1056,128]{1,0:T(8,128)(2,1)S(1)}, u32[]{:S(2)}, u32[]{:S(2)}) collective-permute-start(bf16[1056,128]{1,0:T(8,128)(2,1)S(1)} %pad_maximum_fusion.4.refs_0_), channel_id=1, source_target_pairs={{0,2},{1,3},{2,0},{3,1},{4,6},{5,7},{6,4},{7,5},{8,10},{9,11},{10,... | collective-permute-start | bytes 811016 | tf_op jit(solution)/shard_map/ppermute | solution.py:503
  166.8 10.0 %collective-permute-start.51 = (bf16[1056,128]{1,0:T(8,128)(2,1)S(1)}, bf16[1056,128]{1,0:T(8,128)(2,1)S(1)}, u32[]{:S(2)}, u32[]{:S(2)}) collective-permute-start(bf16[1056,128]{1,0:T(8,128)(2,1)S(1)} %pad_maximum_fusion.4.refs_0_), channel_id=1, source_target_pairs={{0,8},{8,0},{16,24},{24,16},{1,9},{9,1},{17,25},{25,17},{2,10},{10... | collective-permute-start | bytes 811016 | tf_op jit(solution)/shard_map/ppermute | solution.py:513
  167.7 9.1 %collective-permute-start.52 = (bf16[1056,128]{1,0:T(8,128)(2,1)S(1)}, bf16[1056,128]{1,0:T(8,128)(2,1)S(1)}, u32[]{:S(2)}, u32[]{:S(2)}) collective-permute-start(bf16[1056,128]{1,0:T(8,128)(2,1)S(1)} %pad_maximum_fusion.4.refs_0_), channel_id=1, source_target_pairs={{0,16},{8,24},{16,0},{24,8},{1,17},{9,25},{17,1},{25,9},{2,18},{10... | collective-permute-start | bytes 811016 | tf_op jit(solution)/shard_map/ppermute | solution.py:513
  168.7 17.4 %collective-permute-start.46 = (bf16[1152,128]{1,0:T(8,128)(2,1)S(1)}, bf16[1152,128]{1,0:T(8,128)(2,1)S(1)}, u32[]{:S(2)}, u32[]{:S(2)}) collective-permute-start(bf16[1152,128]{1,0:T(8,128)(2,1)S(1)} %pad_maximum_fusion.3), channel_id=1, source_target_pairs={{0,4},{1,5},{2,6},{3,7},{4,0},{5,1},{6,2},{7,3},{8,12},{9,13},{10,... | collective-permute-start | bytes 884744 | tf_op jit(solution)/shard_map/ppermute | solution.py:503
  176.8 9.6 %collective-permute-start.58 = (bf16[1056,128]{1,0:T(8,128)(2,1)S(1)}, bf16[1056,128]{1,0:T(8,128)(2,1)}, u32[]{:S(2)}, u32[]{:S(2)}) collective-permute-start(bf16[1056,128]{1,0:T(8,128)(2,1)S(1)} %collective-permute-done.50.refs_1_), channel_id=1, source_target_pairs={{0,8},{8,0},{16,24},{24,16},{1,9},{9,1},{17,25},{25,17},{2,10},{10... | collective-permute-start | bytes 811016 | tf_op jit(solution)/shard_map/ppermute | solution.py:513
  178.3 9.5 %collective-permute-start.59 = (bf16[1056,128]{1,0:T(8,128)(2,1)S(1)}, bf16[1056,128]{1,0:T(8,128)(2,1)}, u32[]{:S(2)}, u32[]{:S(2)}) collective-permute-start(bf16[1056,128]{1,0:T(8,128)(2,1)S(1)} %collective-permute-done.50.refs_1_), channel_id=1, source_target_pairs={{0,16},{8,24},{16,0},{24,8},{1,17},{9,25},{17,1},{25,9},{2,18},{10... | collective-permute-start | bytes 811016 | tf_op jit(solution)/shard_map/ppermute | solution.py:513
  179.4 14.1 %collective-permute-start.56 = (bf16[2400,128]{1,0:T(8,128)(2,1)S(1)}, bf16[2400,128]{1,0:T(8,128)(2,1)S(1)}, u32[]{:S(2)}, u32[]{:S(2)}) collective-permute-start(bf16[2400,128]{1,0:T(8,128)(2,1)S(1)} %collective-permute-done.43.refs_5_), channel_id=1, source_target_pairs={{0,8},{8,0},{16,24},{24,16},{1,9},{9,1},{17,25},{25,17},{2,10},{10... | collective-permute-start | bytes 1843208 | tf_op jit(solution)/shard_map/ppermute | solution.py:513
  180.7 13.9 %collective-permute-start.57 = (bf16[2400,128]{1,0:T(8,128)(2,1)S(1)}, bf16[2400,128]{1,0:T(8,128)(2,1)S(1)}, u32[]{:S(2)}, u32[]{:S(2)}) collective-permute-start(bf16[2400,128]{1,0:T(8,128)(2,1)S(1)} %collective-permute-done.38.refs_2_), channel_id=1, source_target_pairs={{0,16},{8,24},{16,0},{24,8},{1,17},{9,25},{17,1},{25,9},{2,18},{10... | collective-permute-start | bytes 1843208 | tf_op jit(solution)/shard_map/ppermute | solution.py:513
  186.1 8.5 %collective-permute-start.53 = (bf16[2400,128]{1,0:T(8,128)(2,1)}, bf16[2400,128]{1,0:T(8,128)(2,1)S(1)}, u32[]{:S(2)}, u32[]{:S(2)}) collective-permute-start(bf16[2400,128]{1,0:T(8,128)(2,1)} %copy-done.1), channel_id=1, source_target_pairs={{0,1},{1,0},{2,3},{3,2},{4,5},{5,4},{6,7},{7,6},{8,9},{9,8},{10,11... | collective-permute-start | bytes 1843208 | tf_op jit(solution)/shard_map/ppermute | solution.py:508
  194.7 9.1 %collective-permute-start.60 = (bf16[2400,128]{1,0:T(8,128)(2,1)S(1)}, bf16[2400,128]{1,0:T(8,128)(2,1)S(1)}, u32[]{:S(2)}, u32[]{:S(2)}) collective-permute-start(bf16[2400,128]{1,0:T(8,128)(2,1)S(1)} %collective-permute-done.56.refs_7_), channel_id=1, source_target_pairs={{0,1},{1,0},{2,3},{3,2},{4,5},{5,4},{6,7},{7,6},{8,9},{9,8},{10,11... | collective-permute-start | bytes 1843208 | tf_op jit(solution)/shard_map/ppermute | solution.py:508
  194.7 9.0 %collective-permute-start.61 = (bf16[2400,128]{1,0:T(8,128)(2,1)S(1)}, bf16[2400,128]{1,0:T(8,128)(2,1)S(1)}, u32[]{:S(2)}, u32[]{:S(2)}) collective-permute-start(bf16[2400,128]{1,0:T(8,128)(2,1)S(1)} %collective-permute-done.57.refs_6_), channel_id=1, source_target_pairs={{0,1},{1,0},{2,3},{3,2},{4,5},{5,4},{6,7},{7,6},{8,9},{9,8},{10,11... | collective-permute-start | bytes 1843208 | tf_op jit(solution)/shard_map/ppermute | solution.py:508
  195.2 8.5 %collective-permute-start.62 = (bf16[1056,128]{1,0:T(8,128)(2,1)S(1)}, bf16[1056,128]{1,0:T(8,128)(2,1)S(1)}, u32[]{:S(2)}, u32[]{:S(2)}) collective-permute-start(bf16[1056,128]{1,0:T(8,128)(2,1)S(1)} %copy-done.44), channel_id=1, source_target_pairs={{0,16},{8,24},{16,0},{24,8},{1,17},{9,25},{17,1},{25,9},{2,18},{10... | collective-permute-start | bytes 811016 | tf_op jit(solution)/shard_map/ppermute | solution.py:513
  197.0 18.4 %collective-permute-start.64 = (bf16[1056,128]{1,0:T(8,128)(2,1)}, bf16[1056,128]{1,0:T(8,128)(2,1)S(1)}, u32[]{:S(2)}, u32[]{:S(2)}) collective-permute-start(bf16[1056,128]{1,0:T(8,128)(2,1)} %collective-permute-done.59.refs_5_), channel_id=1, source_target_pairs={{0,8},{8,0},{16,24},{24,16},{1,9},{9,1},{17,25},{25,17},{2,10},{10... | collective-permute-start | bytes 811016 | tf_op jit(solution)/shard_map/ppermute | solution.py:513
  203.7 12.1 %collective-permute-start.65 = (bf16[1056,128]{1,0:T(8,128)(2,1)S(1)}, bf16[1056,128]{1,0:T(8,128)(2,1)S(1)}, u32[]{:S(2)}, u32[]{:S(2)}) collective-permute-start(bf16[1056,128]{1,0:T(8,128)(2,1)S(1)} %collective-permute-done.50.refs_1_), channel_id=1, source_target_pairs={{0,1},{1,0},{2,3},{3,2},{4,5},{5,4},{6,7},{7,6},{8,9},{9,8},{10,11... | collective-permute-start | bytes 811016 | tf_op jit(solution)/shard_map/ppermute | solution.py:508
  203.8 12.2 %collective-permute-start.66 = (bf16[1056,128]{1,0:T(8,128)(2,1)}, bf16[1056,128]{1,0:T(8,128)(2,1)S(1)}, u32[]{:S(2)}, u32[]{:S(2)}) collective-permute-start(bf16[1056,128]{1,0:T(8,128)(2,1)} %collective-permute-done.58.refs_3_), channel_id=1, source_target_pairs={{0,1},{1,0},{2,3},{3,2},{4,5},{5,4},{6,7},{7,6},{8,9},{9,8},{10,11... | collective-permute-start | bytes 811016 | tf_op jit(solution)/shard_map/ppermute | solution.py:508
  204.3 12.1 %collective-permute-start.67 = (bf16[1056,128]{1,0:T(8,128)(2,1)}, bf16[1056,128]{1,0:T(8,128)(2,1)S(1)}, u32[]{:S(2)}, u32[]{:S(2)}) collective-permute-start(bf16[1056,128]{1,0:T(8,128)(2,1)} %collective-permute-done.59.refs_5_), channel_id=1, source_target_pairs={{0,1},{1,0},{2,3},{3,2},{4,5},{5,4},{6,7},{7,6},{8,9},{9,8},{10,11... | collective-permute-start | bytes 811016 | tf_op jit(solution)/shard_map/ppermute | solution.py:508
  204.4 10.8 %collective-permute-start.63 = (f32[72,128]{1,0:T(8,128)S(1)}, f32[72,128]{1,0:T(8,128)S(1)}, u32[]{:S(2)}, u32[]{:S(2)}) collective-permute-start(f32[72,128]{1,0:T(8,128)S(1)} %add.103), channel_id=1, source_target_pairs={{0,4},{1,5},{2,6},{3,7},{4,0},{5,1},{6,2},{7,3},{8,12},{9,13},{10,... | collective-permute-start | bytes 110600 | tf_op jit(solution)/shard_map/ppermute | solution.py:503
  (98 other events, 1020.5 us)

commit v3 on v2

--- a/solution.py
+++ b/solution.py
@@ -1070,7 +1070,7 @@
     head_grad=(15, 15), head_core=(15, 15), head_x=(16, 16), head_y=(16, 16), head_d=(16, 16),
     head_sum=(17, 17), two_z1=(18, 18), one_near=(17, 18), two_z2=(20, 20), one_far=(20, 20),
     one_nx=(20, 20), one_ny=(20, 20), two_near=(22, 22), one_fx=(22, 22), one_fy=(22, 22),
-    back_z1=(16, 18), two_far=(24, 24), two_nx=(24, 24), two_ny=(24, 24), one_nd=(25, 26),
+    back_z1=(15, 18), two_far=(24, 24), two_nx=(24, 24), two_ny=(24, 24), one_nd=(25, 26),
     one_fd=(25, 26), back_z2=(24, 25), two_fx=(25, 26), two_fy=(25, 26), input_grad=(26, 26),
     tiny_core=(17, 18), two_nd=(27, 28), two_fd=(27, 28), tiny_x=(18, 18), tiny_y=(20, 20),
     tiny_z1=(22, 22), tiny_z2=(28, 30), one_all=(17, 18), put_own=(25, 25), put_rest=(28, 28),

time: 226 us -> 226 us (level)
  no operation moved by 1% of the time
where the time goes in v3:
time: 226 us
  waiting for transfers between devices  74 us (33%)
  Pallas kernels  70.4 us (31%)
  starting transfers between devices  63 us (28%)
  local copies, waits for them, and re-layouts  7.11 us (3%)
  matrix products  5.9 us (3%)
  other arithmetic  3.34 us (1%)
    ppermute x22, waiting for transfers between devices, over_z(): return lax.ppermute(value, 'seq', [(i, i ^ 2 * step) for i in range(count)])  46.7 us
    ppermute x22, starting transfers between devices, over_z(): return lax.ppermute(value, 'seq', [(i, i ^ 2 * step) for i in range(count)])  29.8 us
    ppermute x26, starting transfers between devices, over_item(): return lax.ppermute(value, 'item', [(i, i ^ step) for i in range(count)])  28.1 us
    ppermute x26, waiting for transfers between devices, over_item(): return lax.ppermute(value, 'item', [(i, i ^ step) for i in range(count)])  25.4 us
    pallas_call x2, Pallas kernels, put_pieces(): pl.pallas_call(functools.partial(put_pieces_kernel, layout, size, which),...  11.3 us
    pallas_call x1, Pallas kernels, put_rest(): pl.pallas_call(functools.partial(put_rest_kernel, layout_one, size_one, s...  10.4 us
    pallas_call x1, Pallas kernels, middle_step(): kernel(middle_kernel, smem + vmem(5) + anywhere + vmem(3) + anywhere + vm...  10.3 us
    pallas_call x1, Pallas kernels, attend_back(): kernel(functools.partial(attend_back_kernel, heads), vmem(14), [shaped((p...  7.49 us
  transfers between devices with their start and end apart: 73, of which 26 were waited for; matrix products, arithmetic and copies ran while one was open for 5% of the time, Pallas kernels for 25%

profile of v3, /device:TPU:0, one launch (start us, length us, event | category | flops | bytes accessed | tf_op | source)
XLA Modules:
  0.0 225.6 jit_solution(13778348242776697963)
XLA Ops:
  1.3 4.3 %project.1 = (bf16[128,768]{1,0:T(8,128)(2,1)}, bf16[576,128]{1,0:T(8,128)(2,1)}, bf16[576,128]{1,0:T(8,128)(2,1)}, bf16[576,128]{1,0:T(8,128)(2,1)}, bf16[576,128]{1,0:T(8,128)(2,1)}) custom-call(s32[3]{0:T(128)} %pad_add_fusion.place_ref, bf16[128,768]{1,0:T(8,128)(2,1)} %bitcast.49, bf16[768,768]{1,0:T(8,128)(2,1)} %wq_hbm.3, bf16[768,768]{1,0:T(8,128)(2,1)} %wk_hbm.3, ...), custom_call_target="tpu_custom_call" | custom-call | flops 1000000 | bytes 100000 | tf_op jit(solution)/shard_map/project/pallas_call | solution.py:1238
  5.7 3.1 %collective-permute-start = (bf16[576,128]{1,0:T(8,128)(2,1)}, bf16[576,128]{1,0:T(8,128)(2,1)S(1)}, u32[]{:S(2)}, u32[]{:S(2)}) collective-permute-start(bf16[576,128]{1,0:T(8,128)(2,1)} %get-tuple-element.288), channel_id=1, source_target_pairs={{0,2},{1,3},{2,0},{3,1},{4,6},{5,7},{6,4},{7,5},{8,10},{9,11},{10,... | collective-permute-start | bytes 442376 | tf_op jit(solution)/shard_map/ppermute | solution.py:503
  8.8 2.6 %collective-permute-start.1 = (bf16[576,128]{1,0:T(8,128)(2,1)}, bf16[576,128]{1,0:T(8,128)(2,1)S(1)}, u32[]{:S(2)}, u32[]{:S(2)}) collective-permute-start(bf16[576,128]{1,0:T(8,128)(2,1)} %get-tuple-element.289), channel_id=1, source_target_pairs={{0,4},{1,5},{2,6},{3,7},{4,0},{5,1},{6,2},{7,3},{8,12},{9,13},{10,... | collective-permute-start | bytes 442376 | tf_op jit(solution)/shard_map/ppermute | solution.py:503
  11.4 5.1 %fusion.5.d_active_hbm = f32[128,3072]{1,0:T(8,128)} fusion(bf16[128,768]{1,0:T(8,128)(2,1)S(1)} %bitcast.54, bf16[3072,768]{1,0:T(8,128)(2,1)} %param.25), kind=kOutput, calls=%fused_computation.37 | convolution fusion | flops 603979776 | bytes 6488064 | tf_op jit(solution)/shard_map/dot_general | solution.py:101
  17.5 1.4 multiplicity.1.refs_8_
  18.9 4.1 %collective-permute-done.1.refs_2_ = bf16[576,128]{1,0:T(8,128)(2,1)S(1)} collective-permute-done((bf16[576,128]{1,0:T(8,128)(2,1)}, bf16[576,128]{1,0:T(8,128)(2,1)S(1)}, u32[]{:S(2)}, u32[]{:S(2)}) %collective-permute-start.1) | collective-permute-done | bytes 147488 | tf_op jit(solution)/shard_map/ppermute | solution.py:503
  23.8 3.3 %collective-permute-start.7 = (bf16[128,768]{1,0:T(8,128)(2,1)S(1)}, bf16[128,768]{1,0:T(8,128)(2,1)S(1)}, u32[]{:S(2)}, u32[]{:S(2)}) collective-permute-start(bf16[128,768]{1,0:T(8,128)(2,1)S(1)} %copy-done.61), channel_id=1, source_target_pairs={{0,4},{1,5},{2,6},{3,7},{4,0},{5,1},{6,2},{7,3},{8,12},{9,13},{10,... | collective-permute-start | bytes 589832 | tf_op jit(solution)/shard_map/ppermute | solution.py:503
  27.4 1.5 collective-permute-start.8
  28.9 1.5 collective-permute-start.9
  31.6 5.3 %attend.1 = (bf16[192,128]{1,0:T(8,128)(2,1)}, bf16[192,128]{1,0:T(8,128)(2,1)}, bf16[192,128]{1,0:T(8,128)(2,1)}, bf16[192,128]{1,0:T(8,128)(2,1)}, f32[192,512]{1,0:T(8,128)}, /*index=5*/f32[3,1,512]{2,1,0:T(1,128)}) custom-call(bf16[576,128]{1,0:T(8,128)(2,1)} %get-tuple-element.349.refs_0_, bf16[576,128]{1,0:T(8,128)(2,1)} %copy-done.15, ...), custom_call_target="tpu_custom_call" | custom-call | flops 1000000 | bytes 100000 | tf_op jit(solution)/shard_map/attend/pallas_call | solution.py:1255
  37.2 2.0 collective-permute-start.12
  39.2 2.2 collective-permute-start.13
  41.6 2.4 %collective-permute-done.12.ctx2 = bf16[192,128]{1,0:T(8,128)(2,1)S(1)} collective-permute-done((bf16[192,128]{1,0:T(8,128)(2,1)}, bf16[192,128]{1,0:T(8,128)(2,1)S(1)}, u32[]{:S(2)}, u32[]{:S(2)}) %collective-permute-start.12) | collective-permute-done | bytes 49184 | tf_op jit(solution)/shard_map/ppermute | solution.py:503
  45.9 10.3 %middle.1 = (bf16[1792,128]{1,0:T(8,128)(2,1)}, bf16[1792,128]{1,0:T(8,128)(2,1)}, bf16[1792,128]{1,0:T(8,128)(2,1)}, bf16[1792,128]{1,0:T(8,128)(2,1)}, bf16[12...) custom-call(s32[3]{0:T(128)} %pad_add_fusion.place_ref, ...), custom_call_target="tpu_custom_call" | custom-call | flops 1000000 | bytes 100000 | tf_op jit(solution)/shard_map/middle/pallas_call | solution.py:1264
  56.2 1.6 collective-permute-start.15
  57.8 1.5 collective-permute-start.16
  59.8 1.5 collective-permute-start.18
  62.0 2.6 %collective-permute-done.18.refs_12_ = bf16[384,128]{1,0:T(8,128)(2,1)S(1)} collective-permute-done((bf16[384,128]{1,0:T(8,128)(2,1)}, bf16[384,128]{1,0:T(8,128)(2,1)S(1)}, u32[]{:S(2)}, u32[]{:S(2)}) %collective-permute-start.18) | collective-permute-done | bytes 98336 | tf_op jit(solution)/shard_map/ppermute | solution.py:503
  64.6 3.3 %collective-permute-start.19 = (bf16[384,128]{1,0:T(8,128)(2,1)S(1)}, bf16[384,128]{1,0:T(8,128)(2,1)S(1)}, u32[]{:S(2)}, u32[]{:S(2)}) collective-permute-start(bf16[384,128]{1,0:T(8,128)(2,1)S(1)} %pad_maximum_fusion.5), channel_id=1, source_target_pairs={{0,4},{1,5},{2,6},{3,7},{4,0},{5,1},{6,2},{7,3},{8,12},{9,13},{10,... | collective-permute-start | bytes 294920 | tf_op jit(solution)/shard_map/ppermute | solution.py:503
  67.9 3.6 %collective-permute-done.19.refs_13_ = bf16[384,128]{1,0:T(8,128)(2,1)S(1)} collective-permute-done((bf16[384,128]{1,0:T(8,128)(2,1)S(1)}, bf16[384,128]{1,0:T(8,128)(2,1)S(1)}, u32[]{:S(2)}, u32[]{:S(2)}) %collective-permute-start.19) | collective-permute-done | bytes 98336 | tf_op jit(solution)/shard_map/ppermute | solution.py:503
  72.2 7.5 %attend_back.1 = (bf16[192,512]{1,0:T(8,128)(2,1)}, f32[384,512]{1,0:T(8,128)}, bf16[384,512]{1,0:T(8,128)(2,1)}) custom-call(bf16[576,128]{1,0:T(8,128)(2,1)} %get-tuple-element.349.refs_0_, bf16[576,128]{1,0:T(8,128)(2,1)} %copy-done.15, bf16[576,128]{1,0:T(8,128)(2,1)} %copy-done.16, bf16[576,128]{1,0:T(8,128)(2,1)} %copy-done.17, ...), custom_call_target="tpu_custom_call" | custom-call | flops 1000000 | bytes 100000 | tf_op jit(solution)/shard_map/attend_back/pallas_call | solution.py:1288
  80.8 4.1 %first_grad.1 = (f32[3072,128]{1,0:T(8,128)}, bf16[3072,128]{1,0:T(8,128)(2,1)}) custom-call(s32[3]{0:T(128)} %pad_add_fusion.place_ref, bf16[1792,128]{1,0:T(8,128)(2,1)} %get-tuple-element.415.refs_0_, bf16[1792,128]{1,0:T(8,128)(2,1)} %copy-done.6, bf16[1792,128]{1,0:T(8,128)(2,1)} %copy-done.7, bf16[1792,128]{1,0:T(8,128)(2,1)} %copy-done.8, ...), custom_call_target="tpu_custom_call" | custom-call | flops 1000000 | bytes 100000 | tf_op jit(solution)/shard_map/first_grad/pallas_call | solution.py:1300
  85.5 1.5 collective-permute-start.20
  87.4 1.6 collective-permute-start.22
  92.5 6.2 %head_grad.1 = (bf16[1152,128]{1,0:T(8,128)(2,1)}, bf16[1152,128]{1,0:T(8,128)(2,1)}, f32[1728,128]{1,0:T(8,128)}, bf16[1728,128]{1,0:T(8,128)(2,1)}, f32[24,128]{1,0:T(8,128)}) custom-call(s32[3]{0:T(128)} %pad_add_fusion.place_ref, bf16[192,512]{1,0:T(8,128)(2,1)} %get-tuple-element.395.dq_ref, f32[384,512]{1,0:T(8,128)} %get-tuple-element.396.dkv_ref, ...), custom_call_target="tpu_custom_call" | custom-call | flops 1000000 | bytes 100000 | tf_op jit(solution)/shard_map/head_grad/pallas_call | solution.py:1328
  98.8 1.9 collective-permute-done.26
  100.9 2.7 %collective-permute-done.21.refs_6_ = bf16[1280,128]{1,0:T(8,128)(2,1)S(1)} collective-permute-done((bf16[1280,128]{1,0:T(8,128)(2,1)}, bf16[1280,128]{1,0:T(8,128)(2,1)S(1)}, u32[]{:S(2)}, u32[]{:S(2)}) %collective-permute-start.21) | collective-permute-done | bytes 327712 | tf_op jit(solution)/shard_map/ppermute | solution.py:513
  103.7 1.9 collective-permute-start.31
  105.7 1.5 collective-permute-start.28
  107.2 1.5 collective-permute-start.29
  109.2 3.9 %second_grad.1 = (f32[2112,128]{1,0:T(8,128)}, bf16[2112,128]{1,0:T(8,128)(2,1)}) custom-call(s32[3]{0:T(128)} %pad_add_fusion.place_ref, bf16[1792,128]{1,0:T(8,128)(2,1)} %get-tuple-element.415.refs_0_, bf16[1792,128]{1,0:T(8,128)(2,1)} %copy-done.6, bf16[1792,128]{1,0:T(8,128)(2,1)} %copy-done.7, bf16[1792,128]{1,0:T(8,128)(2,1)} %copy-done.8, ...), custom_call_target="tpu_custom_call" | custom-call | flops 1000000 | bytes 100000 | tf_op jit(solution)/shard_map/second_grad/pallas_call | solution.py:1314
  113.1 1.6 collective-permute-done.31
  119.2 13.2 %collective-permute-done.32 = bf16[1200,128]{1,0:T(8,128)(2,1)S(1)} collective-permute-done((bf16[1200,128]{1,0:T(8,128)(2,1)S(1)}, bf16[1200,128]{1,0:T(8,128)(2,1)S(1)}, u32[]{:S(2)}, u32[]{:S(2)}) %collective-permute-start.32) | collective-permute-done | bytes 307232 | tf_op jit(solution)/shard_map/ppermute | solution.py:503
  134.8 2.7 %collective-permute-start.41 = (bf16[528,128]{1,0:T(8,128)(2,1)S(1)}, bf16[528,128]{1,0:T(8,128)(2,1)S(1)}, u32[]{:S(2)}, u32[]{:S(2)}) collective-permute-start(bf16[528,128]{1,0:T(8,128)(2,1)S(1)} %slice.179), channel_id=1, source_target_pairs={{0,4},{1,5},{2,6},{3,7},{4,0},{5,1},{6,2},{7,3},{8,12},{9,13},{10,... | collective-permute-start | bytes 405512 | tf_op jit(solution)/shard_map/ppermute | solution.py:503
  138.1 11.4 %collective-permute-done.40 = f32[72,128]{1,0:T(8,128)S(1)} collective-permute-done((f32[72,128]{1,0:T(8,128)S(1)}, f32[72,128]{1,0:T(8,128)S(1)}, u32[]{:S(2)}, u32[]{:S(2)}) %collective-permute-start.40) | collective-permute-done | bytes 36896 | tf_op jit(solution)/shard_map/ppermute | solution.py:513
  149.6 1.7 collective-permute-done.37.refs_1_
  155.3 3.6 %collective-permute-done.44 = f32[72,128]{1,0:T(8,128)S(1)} collective-permute-done((f32[72,128]{1,0:T(8,128)S(1)}, f32[72,128]{1,0:T(8,128)S(1)}, u32[]{:S(2)}, u32[]{:S(2)}) %collective-permute-start.44) | collective-permute-done | bytes 36896 | tf_op jit(solution)/shard_map/ppermute | solution.py:503
  158.9 4.0 %collective-permute-done.45 = bf16[528,128]{1,0:T(8,128)(2,1)S(1)} collective-permute-done((bf16[528,128]{1,0:T(8,128)(2,1)S(1)}, bf16[528,128]{1,0:T(8,128)(2,1)S(1)}, u32[]{:S(2)}, u32[]{:S(2)}) %collective-permute-start.45) | collective-permute-done | bytes 135200 | tf_op jit(solution)/shard_map/ppermute | solution.py:503
  163.0 3.0 %collective-permute-done.42.refs_3_ = bf16[2400,128]{1,0:T(8,128)(2,1)S(1)} collective-permute-done((bf16[2400,128]{1,0:T(8,128)(2,1)S(1)}, bf16[2400,128]{1,0:T(8,128)(2,1)S(1)}, u32[]{:S(2)}, u32[]{:S(2)}) %collective-permute-start.42) | collective-permute-done | bytes 614432 | tf_op jit(solution)/shard_map/ppermute | solution.py:513
  168.7 1.7 collective-permute-start.46
  170.4 6.4 %collective-permute-done.50.refs_1_ = bf16[1056,128]{1,0:T(8,128)(2,1)S(1)} collective-permute-done((bf16[1056,128]{1,0:T(8,128)(2,1)S(1)}, bf16[1056,128]{1,0:T(8,128)(2,1)S(1)}, u32[]{:S(2)}, u32[]{:S(2)}) %collective-permute-start.50) | collective-permute-done | bytes 270368 | tf_op jit(solution)/shard_map/ppermute | solution.py:503
  176.8 1.4 collective-permute-start.58
  181.1 4.9 %put_own.1 = (f32[3072,768]{1,0:T(8,128)}, f32[768,3072]{1,0:T(8,128)}, f32[8,128]{1,0:T(8,128)}) custom-call(s32[3]{0:T(128)} %pad_add_fusion.place_ref, bf16[2400,128]{1,0:T(8,128)(2,1)} %copy-done, bf16[2400,128]{1,0:T(8,128)(2,1)} %copy-done.1, bf16[2400,128]{1,0:T(8,128)(2,1)} %copy-done.2, bf16[2400,128]{1,0:T(8,128)(2,1)} %copy-done.4, ...), custom_call_target="tpu_custom_call" | custom-call | flops 1000000 | bytes 100000 | tf_op jit(solution)/shard_map/put_own/pallas_call | solution.py:1043
  187.8 5.7 %input_grad.1 = bf16[128,768]{1,0:T(8,128)(2,1)} custom-call(s32[3]{0:T(128)} %pad_add_fusion.place_ref, bf16[1152,128]{1,0:T(8,128)(2,1)} %get-tuple-element.461.back0, bf16[1152,128]{1,0:T(8,128)(2,1)} %copy-done.21, bf16[1152,128]{1,0:T(8,128)(2,1)} %copy-done.41, bf16[768,768]{1,0:T(8,128)(2,1)} %wq_hbm.3, bf16[768,768]{1,0:T(8,128)(2,1)} %wk_hbm.3, ...), custom_call_target="tpu_custom_call" | custom-call | flops 1000000 | bytes 100000 | tf_op jit(solution)/shard_map/input_grad/pallas_call | solution.py:1346
  195.2 1.7 collective-permute-start.62
  197.9 5.8 %collective-permute-done.62.refs_6_ = bf16[1056,128]{1,0:T(8,128)(2,1)S(1)} collective-permute-done((bf16[1056,128]{1,0:T(8,128)(2,1)S(1)}, bf16[1056,128]{1,0:T(8,128)(2,1)S(1)}, u32[]{:S(2)}, u32[]{:S(2)}) %collective-permute-start.62) | collective-permute-done | bytes 270368 | tf_op jit(solution)/shard_map/ppermute | solution.py:513
  204.8 10.4 %put_rest.1 = (f32[3072,768]{1,0:T(8,128)}, f32[768,3072]{1,0:T(8,128)}, f32[768,768]{1,0:T(8,128)}, f32[768,768]{1,0:T(8,128)}, f32[768,768]{1,0:T(8,128)}, /*index=5*/f32[8,128]{1,0:T(8,128)}) custom-call(s32[3]{0:T(128)} %pad_add_fusion.place_ref, bf16[2400,128]{1,0:T(8,128)(2,1)} %copy-done, ...), custom_call_target="tpu_custom_call", output_to_operand_aliasing={{0}: (18, {}), {1}: (19, {})} | custom-call | flops 1000000 | bytes 100000 | tf_op jit(solution)/shard_map/put_rest/pallas_call | solution.py:1378
  219.1 6.3 %put_two.1 = (f32[768,3072]{1,0:T(8,128)}, f32[768,768]{1,0:T(8,128)}, f32[8,128]{1,0:T(8,128)}) custom-call(s32[3]{0:T(128)} %pad_add_fusion.place_ref, bf16[1056,128]{1,0:T(8,128)(2,1)} %copy-done.12, bf16[1056,128]{1,0:T(8,128)(2,1)} %copy-done.42, bf16[1056,128]{1,0:T(8,128)(2,1)} %copy-done.43, ...), custom_call_target="tpu_custom_call", output_to_operand_aliasing={{0}: (18, {})} | custom-call | flops 1000000 | bytes 100000 | tf_op jit(solution)/shard_map/put_two/pallas_call | solution.py:1043
  (297 shorter events, 40.5 us)
Async XLA Ops:
  5.7 13.2 %collective-permute-start = (bf16[576,128]{1,0:T(8,128)(2,1)}, bf16[576,128]{1,0:T(8,128)(2,1)S(1)}, u32[]{:S(2)}, u32[]{:S(2)}) collective-permute-start(bf16[576,128]{1,0:T(8,128)(2,1)} %get-tuple-element.288), channel_id=1, source_target_pairs={{0,2},{1,3},{2,0},{3,1},{4,6},{5,7},{6,4},{7,5},{8,10},{9,11},{10,... | collective-permute-start | bytes 442376 | tf_op jit(solution)/shard_map/ppermute | solution.py:503
  8.8 14.2 %collective-permute-start.1 = (bf16[576,128]{1,0:T(8,128)(2,1)}, bf16[576,128]{1,0:T(8,128)(2,1)S(1)}, u32[]{:S(2)}, u32[]{:S(2)}) collective-permute-start(bf16[576,128]{1,0:T(8,128)(2,1)} %get-tuple-element.289), channel_id=1, source_target_pairs={{0,4},{1,5},{2,6},{3,7},{4,0},{5,1},{6,2},{7,3},{8,12},{9,13},{10,... | collective-permute-start | bytes 442376 | tf_op jit(solution)/shard_map/ppermute | solution.py:503
  11.4 11.6 %collective-permute-start.2 = (bf16[576,128]{1,0:T(8,128)(2,1)}, bf16[576,128]{1,0:T(8,128)(2,1)S(1)}, u32[]{:S(2)}, u32[]{:S(2)}) collective-permute-start(bf16[576,128]{1,0:T(8,128)(2,1)} %get-tuple-element.290), channel_id=1, source_target_pairs={{0,6},{1,7},{2,4},{3,5},{4,2},{5,3},{6,0},{7,1},{8,14},{9,15},{10,... | collective-permute-start | bytes 442376 | tf_op jit(solution)/shard_map/ppermute | solution.py:503
  23.8 13.1 %collective-permute-start.7 = (bf16[128,768]{1,0:T(8,128)(2,1)S(1)}, bf16[128,768]{1,0:T(8,128)(2,1)S(1)}, u32[]{:S(2)}, u32[]{:S(2)}) collective-permute-start(bf16[128,768]{1,0:T(8,128)(2,1)S(1)} %copy-done.61), channel_id=1, source_target_pairs={{0,4},{1,5},{2,6},{3,7},{4,0},{5,1},{6,2},{7,3},{8,12},{9,13},{10,... | collective-permute-start | bytes 589832 | tf_op jit(solution)/shard_map/ppermute | solution.py:503
  27.4 11.8 %collective-permute-start.8 = (bf16[128,768]{1,0:T(8,128)(2,1)S(1)}, bf16[128,768]{1,0:T(8,128)(2,1)S(1)}, u32[]{:S(2)}, u32[]{:S(2)}) collective-permute-start(bf16[128,768]{1,0:T(8,128)(2,1)S(1)} %bitcast.55), channel_id=1, source_target_pairs={{0,8},{8,0},{16,24},{24,16},{1,9},{9,1},{17,25},{25,17},{2,10},{10... | collective-permute-start | bytes 589832 | tf_op jit(solution)/shard_map/ppermute | solution.py:513
  28.9 12.5 %collective-permute-start.9 = (bf16[128,768]{1,0:T(8,128)(2,1)S(1)}, bf16[128,768]{1,0:T(8,128)(2,1)S(1)}, u32[]{:S(2)}, u32[]{:S(2)}) collective-permute-start(bf16[128,768]{1,0:T(8,128)(2,1)S(1)} %bitcast.56), channel_id=1, source_target_pairs={{0,16},{8,24},{16,0},{24,8},{1,17},{9,25},{17,1},{25,9},{2,18},{10... | collective-permute-start | bytes 589832 | tf_op jit(solution)/shard_map/ppermute | solution.py:513
  30.4 11.0 %collective-permute-start.10 = (bf16[128,768]{1,0:T(8,128)(2,1)S(1)}, bf16[128,768]{1,0:T(8,128)(2,1)S(1)}, u32[]{:S(2)}, u32[]{:S(2)}) collective-permute-start(bf16[128,768]{1,0:T(8,128)(2,1)S(1)} %bitcast.57), channel_id=1, source_target_pairs={{0,24},{8,16},{16,8},{24,0},{1,25},{9,17},{17,9},{25,1},{2,26},{10... | collective-permute-start | bytes 589832 | tf_op jit(solution)/shard_map/ppermute | solution.py:513
  45.3 10.9 %collective-permute-start.14 = (bf16[256,768]{1,0:T(8,128)(2,1)S(1)}, bf16[256,768]{1,0:T(8,128)(2,1)S(1)}, u32[]{:S(2)}, u32[]{:S(2)}) collective-permute-start(bf16[256,768]{1,0:T(8,128)(2,1)S(1)} %pad_maximum_fusion.1.hat0), channel_id=1, source_target_pairs={{0,2},{1,3},{2,0},{3,1},{4,6},{5,7},{6,4},{7,5},{8,10},{9,11},{10,... | collective-permute-start | bytes 1179656 | tf_op jit(solution)/shard_map/ppermute | solution.py:503
  56.2 23.5 %collective-permute-start.15 = (bf16[1792,128]{1,0:T(8,128)(2,1)}, bf16[1792,128]{1,0:T(8,128)(2,1)S(1)}, u32[]{:S(2)}, u32[]{:S(2)}) collective-permute-start(bf16[1792,128]{1,0:T(8,128)(2,1)} %get-tuple-element.346), channel_id=1, source_target_pairs={{0,8},{8,0},{16,24},{24,16},{1,9},{9,1},{17,25},{25,17},{2,10},{10... | collective-permute-start | bytes 1376264 | tf_op jit(solution)/shard_map/ppermute | solution.py:513
  57.8 22.0 %collective-permute-start.16 = (bf16[1792,128]{1,0:T(8,128)(2,1)}, bf16[1792,128]{1,0:T(8,128)(2,1)S(1)}, u32[]{:S(2)}, u32[]{:S(2)}) collective-permute-start(bf16[1792,128]{1,0:T(8,128)(2,1)} %get-tuple-element.347), channel_id=1, source_target_pairs={{0,16},{8,24},{16,0},{24,8},{1,17},{9,25},{17,1},{25,9},{2,18},{10... | collective-permute-start | bytes 1376264 | tf_op jit(solution)/shard_map/ppermute | solution.py:513
  59.3 20.5 %collective-permute-start.17 = (bf16[1792,128]{1,0:T(8,128)(2,1)}, bf16[1792,128]{1,0:T(8,128)(2,1)S(1)}, u32[]{:S(2)}, u32[]{:S(2)}) collective-permute-start(bf16[1792,128]{1,0:T(8,128)(2,1)} %get-tuple-element.348), channel_id=1, source_target_pairs={{0,24},{8,16},{16,8},{24,0},{1,25},{9,17},{17,9},{25,1},{2,26},{10... | collective-permute-start | bytes 1376264 | tf_op jit(solution)/shard_map/ppermute | solution.py:513
  85.5 15.4 %collective-permute-start.20 = (bf16[1280,128]{1,0:T(8,128)(2,1)}, bf16[1280,128]{1,0:T(8,128)(2,1)S(1)}, u32[]{:S(2)}, u32[]{:S(2)}) collective-permute-start(bf16[1280,128]{1,0:T(8,128)(2,1)} %get-tuple-element.381), channel_id=1, source_target_pairs={{0,8},{8,0},{16,24},{24,16},{1,9},{9,1},{17,25},{25,17},{2,10},{10... | collective-permute-start | bytes 983048 | tf_op jit(solution)/shard_map/ppermute | solution.py:513
  87.0 16.6 %collective-permute-start.21 = (bf16[1280,128]{1,0:T(8,128)(2,1)}, bf16[1280,128]{1,0:T(8,128)(2,1)S(1)}, u32[]{:S(2)}, u32[]{:S(2)}) collective-permute-start(bf16[1280,128]{1,0:T(8,128)(2,1)} %get-tuple-element.382), channel_id=1, source_target_pairs={{0,16},{8,24},{16,0},{24,8},{1,17},{9,25},{17,1},{25,9},{2,18},{10... | collective-permute-start | bytes 983048 | tf_op jit(solution)/shard_map/ppermute | solution.py:513
  87.4 16.2 %collective-permute-start.22 = (bf16[1280,128]{1,0:T(8,128)(2,1)}, bf16[1280,128]{1,0:T(8,128)(2,1)}, u32[]{:S(2)}, u32[]{:S(2)}) collective-permute-start(bf16[1280,128]{1,0:T(8,128)(2,1)} %get-tuple-element.383), channel_id=1, source_target_pairs={{0,24},{8,16},{16,8},{24,0},{1,25},{9,17},{17,9},{25,1},{2,26},{10... | collective-permute-start | bytes 983048 | tf_op jit(solution)/shard_map/ppermute | solution.py:513
  90.4 10.3 %collective-permute-start.26 = (bf16[1536,128]{1,0:T(8,128)(2,1)S(1)}, bf16[1536,128]{1,0:T(8,128)(2,1)S(1)}, u32[]{:S(2)}, u32[]{:S(2)}) collective-permute-start(bf16[1536,128]{1,0:T(8,128)(2,1)S(1)} %add_convert_fusion), channel_id=1, source_target_pairs={{0,2},{1,3},{2,0},{3,1},{4,6},{5,7},{6,4},{7,5},{8,10},{9,11},{10,... | collective-permute-start | bytes 1179656 | tf_op jit(solution)/shard_map/ppermute | solution.py:503
  103.7 11.0 %collective-permute-start.31 = (bf16[768,128]{1,0:T(8,128)(2,1)S(1)}, bf16[768,128]{1,0:T(8,128)(2,1)S(1)}, u32[]{:S(2)}, u32[]{:S(2)}) collective-permute-start(bf16[768,128]{1,0:T(8,128)(2,1)S(1)} %slice.178), channel_id=1, source_target_pairs={{0,4},{1,5},{2,6},{3,7},{4,0},{5,1},{6,2},{7,3},{8,12},{9,13},{10,... | collective-permute-start | bytes 589832 | tf_op jit(solution)/shard_map/ppermute | solution.py:503
  105.6 27.1 %collective-permute-start.27 = (bf16[1152,128]{1,0:T(8,128)(2,1)}, bf16[1152,128]{1,0:T(8,128)(2,1)S(1)}, u32[]{:S(2)}, u32[]{:S(2)}) collective-permute-start(bf16[1152,128]{1,0:T(8,128)(2,1)} %get-tuple-element.403), channel_id=1, source_target_pairs={{0,2},{1,3},{2,0},{3,1},{4,6},{5,7},{6,4},{7,5},{8,10},{9,11},{10,... | collective-permute-start | bytes 884744 | tf_op jit(solution)/shard_map/ppermute | solution.py:503
  105.7 9.1 %collective-permute-start.28 = (bf16[432,128]{1,0:T(8,128)(2,1)S(1)}, bf16[432,128]{1,0:T(8,128)(2,1)S(1)}, u32[]{:S(2)}, u32[]{:S(2)}) collective-permute-start(bf16[432,128]{1,0:T(8,128)(2,1)S(1)} %get-tuple-element.543), channel_id=1, source_target_pairs={{0,24},{8,16},{16,8},{24,0},{1,25},{9,17},{17,9},{25,1},{2,26},{10... | collective-permute-start | bytes 331784 | tf_op jit(solution)/shard_map/ppermute | solution.py:513
  115.5 16.9 %collective-permute-start.32 = (bf16[1200,128]{1,0:T(8,128)(2,1)S(1)}, bf16[1200,128]{1,0:T(8,128)(2,1)S(1)}, u32[]{:S(2)}, u32[]{:S(2)}) collective-permute-start(bf16[1200,128]{1,0:T(8,128)(2,1)S(1)} %pad_maximum_fusion.2), channel_id=1, source_target_pairs={{0,4},{1,5},{2,6},{3,7},{4,0},{5,1},{6,2},{7,3},{8,12},{9,13},{10,... | collective-permute-start | bytes 921608 | tf_op jit(solution)/shard_map/ppermute | solution.py:503
  117.0 15.4 %collective-permute-start.35 = (f32[72,128]{1,0:T(8,128)S(1)}, f32[72,128]{1,0:T(8,128)S(1)}, u32[]{:S(2)}, u32[]{:S(2)}) collective-permute-start(f32[72,128]{1,0:T(8,128)S(1)} %add.96), channel_id=1, source_target_pairs={{0,8},{8,0},{16,24},{24,16},{1,9},{9,1},{17,25},{25,17},{2,10},{10... | collective-permute-start | bytes 110600 | tf_op jit(solution)/shard_map/ppermute | solution.py:513
  117.9 14.8 %collective-permute-start.36 = (bf16[1056,128]{1,0:T(8,128)(2,1)S(1)}, bf16[1056,128]{1,0:T(8,128)(2,1)S(1)}, u32[]{:S(2)}, u32[]{:S(2)}) collective-permute-start(bf16[1056,128]{1,0:T(8,128)(2,1)S(1)} %add_convert_fusion.1), channel_id=1, source_target_pairs={{0,2},{1,3},{2,0},{3,1},{4,6},{5,7},{6,4},{7,5},{8,10},{9,11},{10,... | collective-permute-start | bytes 811016 | tf_op jit(solution)/shard_map/ppermute | solution.py:503
  132.8 18.5 %collective-permute-start.37 = (bf16[2400,128]{1,0:T(8,128)(2,1)S(1)}, bf16[2400,128]{1,0:T(8,128)(2,1)S(1)}, u32[]{:S(2)}, u32[]{:S(2)}) collective-permute-start(bf16[2400,128]{1,0:T(8,128)(2,1)S(1)} %pad_maximum_fusion.refs_0_), channel_id=1, source_target_pairs={{0,2},{1,3},{2,0},{3,1},{4,6},{5,7},{6,4},{7,5},{8,10},{9,11},{10,... | collective-permute-start | bytes 1843208 | tf_op jit(solution)/shard_map/ppermute | solution.py:503
  132.9 18.4 %collective-permute-start.38 = (bf16[2400,128]{1,0:T(8,128)(2,1)S(1)}, bf16[2400,128]{1,0:T(8,128)(2,1)S(1)}, u32[]{:S(2)}, u32[]{:S(2)}) collective-permute-start(bf16[2400,128]{1,0:T(8,128)(2,1)S(1)} %pad_maximum_fusion.refs_0_), channel_id=1, source_target_pairs={{0,8},{8,0},{16,24},{24,16},{1,9},{9,1},{17,25},{25,17},{2,10},{10... | collective-permute-start | bytes 1843208 | tf_op jit(solution)/shard_map/ppermute | solution.py:513
  133.8 17.4 %collective-permute-start.39 = (bf16[2400,128]{1,0:T(8,128)(2,1)S(1)}, bf16[2400,128]{1,0:T(8,128)(2,1)S(1)}, u32[]{:S(2)}, u32[]{:S(2)}) collective-permute-start(bf16[2400,128]{1,0:T(8,128)(2,1)S(1)} %pad_maximum_fusion.refs_0_), channel_id=1, source_target_pairs={{0,16},{8,24},{16,0},{24,8},{1,17},{9,25},{17,1},{25,9},{2,18},{10... | collective-permute-start | bytes 1843208 | tf_op jit(solution)/shard_map/ppermute | solution.py:513
  134.8 14.7 %collective-permute-start.41 = (bf16[528,128]{1,0:T(8,128)(2,1)S(1)}, bf16[528,128]{1,0:T(8,128)(2,1)S(1)}, u32[]{:S(2)}, u32[]{:S(2)}) collective-permute-start(bf16[528,128]{1,0:T(8,128)(2,1)S(1)} %slice.179), channel_id=1, source_target_pairs={{0,4},{1,5},{2,6},{3,7},{4,0},{5,1},{6,2},{7,3},{8,12},{9,13},{10,... | collective-permute-start | bytes 405512 | tf_op jit(solution)/shard_map/ppermute | solution.py:503
  137.5 12.0 %collective-permute-start.40 = (f32[72,128]{1,0:T(8,128)S(1)}, f32[72,128]{1,0:T(8,128)S(1)}, u32[]{:S(2)}, u32[]{:S(2)}) collective-permute-start(f32[72,128]{1,0:T(8,128)S(1)} %add.97), channel_id=1, source_target_pairs={{0,16},{8,24},{16,0},{24,8},{1,17},{9,25},{17,1},{25,9},{2,18},{10... | collective-permute-start | bytes 110600 | tf_op jit(solution)/shard_map/ppermute | solution.py:513
  151.3 14.7 %collective-permute-start.42 = (bf16[2400,128]{1,0:T(8,128)(2,1)S(1)}, bf16[2400,128]{1,0:T(8,128)(2,1)S(1)}, u32[]{:S(2)}, u32[]{:S(2)}) collective-permute-start(bf16[2400,128]{1,0:T(8,128)(2,1)S(1)} %collective-permute-done.37.refs_1_), channel_id=1, source_target_pairs={{0,8},{8,0},{16,24},{24,16},{1,9},{9,1},{17,25},{25,17},{2,10},{10... | collective-permute-start | bytes 1843208 | tf_op jit(solution)/shard_map/ppermute | solution.py:513
  151.9 14.1 %collective-permute-start.43 = (bf16[2400,128]{1,0:T(8,128)(2,1)S(1)}, bf16[2400,128]{1,0:T(8,128)(2,1)S(1)}, u32[]{:S(2)}, u32[]{:S(2)}) collective-permute-start(bf16[2400,128]{1,0:T(8,128)(2,1)S(1)} %collective-permute-done.37.refs_1_), channel_id=1, source_target_pairs={{0,16},{8,24},{16,0},{24,8},{1,17},{9,25},{17,1},{25,9},{2,18},{10... | collective-permute-start | bytes 1843208 | tf_op jit(solution)/shard_map/ppermute | solution.py:513
  153.3 14.4 %collective-permute-start.47 = (bf16[2400,128]{1,0:T(8,128)(2,1)S(1)}, bf16[2400,128]{1,0:T(8,128)(2,1)S(1)}, u32[]{:S(2)}, u32[]{:S(2)}) collective-permute-start(bf16[2400,128]{1,0:T(8,128)(2,1)S(1)} %pad_maximum_fusion.refs_0_), channel_id=1, source_target_pairs={{0,1},{1,0},{2,3},{3,2},{4,5},{5,4},{6,7},{7,6},{8,9},{9,8},{10,11... | collective-permute-start | bytes 1843208 | tf_op jit(solution)/shard_map/ppermute | solution.py:508
  153.3 9.6 %collective-permute-start.45 = (bf16[528,128]{1,0:T(8,128)(2,1)S(1)}, bf16[528,128]{1,0:T(8,128)(2,1)S(1)}, u32[]{:S(2)}, u32[]{:S(2)}) collective-permute-start(bf16[528,128]{1,0:T(8,128)(2,1)S(1)} %add_convert_fusion.4), channel_id=1, source_target_pairs={{0,4},{1,5},{2,6},{3,7},{4,0},{5,1},{6,2},{7,3},{8,12},{9,13},{10,... | collective-permute-start | bytes 405512 | tf_op jit(solution)/shard_map/ppermute | solution.py:503
  158.9 9.8 %collective-permute-start.48 = (bf16[2400,128]{1,0:T(8,128)(2,1)S(1)}, bf16[2400,128]{1,0:T(8,128)(2,1)S(1)}, u32[]{:S(2)}, u32[]{:S(2)}) collective-permute-start(bf16[2400,128]{1,0:T(8,128)(2,1)S(1)} %collective-permute-done.38.refs_2_), channel_id=1, source_target_pairs={{0,1},{1,0},{2,3},{3,2},{4,5},{5,4},{6,7},{7,6},{8,9},{9,8},{10,11... | collective-permute-start | bytes 1843208 | tf_op jit(solution)/shard_map/ppermute | solution.py:508
  166.0 10.7 %collective-permute-start.50 = (bf16[1056,128]{1,0:T(8,128)(2,1)S(1)}, bf16[1056,128]{1,0:T(8,128)(2,1)S(1)}, u32[]{:S(2)}, u32[]{:S(2)}) collective-permute-start(bf16[1056,128]{1,0:T(8,128)(2,1)S(1)} %pad_maximum_fusion.4.refs_0_), channel_id=1, source_target_pairs={{0,2},{1,3},{2,0},{3,1},{4,6},{5,7},{6,4},{7,5},{8,10},{9,11},{10,... | collective-permute-start | bytes 811016 | tf_op jit(solution)/shard_map/ppermute | solution.py:503
  166.8 10.0 %collective-permute-start.51 = (bf16[1056,128]{1,0:T(8,128)(2,1)S(1)}, bf16[1056,128]{1,0:T(8,128)(2,1)S(1)}, u32[]{:S(2)}, u32[]{:S(2)}) collective-permute-start(bf16[1056,128]{1,0:T(8,128)(2,1)S(1)} %pad_maximum_fusion.4.refs_0_), channel_id=1, source_target_pairs={{0,8},{8,0},{16,24},{24,16},{1,9},{9,1},{17,25},{25,17},{2,10},{10... | collective-permute-start | bytes 811016 | tf_op jit(solution)/shard_map/ppermute | solution.py:513
  167.7 9.1 %collective-permute-start.52 = (bf16[1056,128]{1,0:T(8,128)(2,1)S(1)}, bf16[1056,128]{1,0:T(8,128)(2,1)S(1)}, u32[]{:S(2)}, u32[]{:S(2)}) collective-permute-start(bf16[1056,128]{1,0:T(8,128)(2,1)S(1)} %pad_maximum_fusion.4.refs_0_), channel_id=1, source_target_pairs={{0,16},{8,24},{16,0},{24,8},{1,17},{9,25},{17,1},{25,9},{2,18},{10... | collective-permute-start | bytes 811016 | tf_op jit(solution)/shard_map/ppermute | solution.py:513
  168.7 17.4 %collective-permute-start.46 = (bf16[1152,128]{1,0:T(8,128)(2,1)S(1)}, bf16[1152,128]{1,0:T(8,128)(2,1)S(1)}, u32[]{:S(2)}, u32[]{:S(2)}) collective-permute-start(bf16[1152,128]{1,0:T(8,128)(2,1)S(1)} %pad_maximum_fusion.3), channel_id=1, source_target_pairs={{0,4},{1,5},{2,6},{3,7},{4,0},{5,1},{6,2},{7,3},{8,12},{9,13},{10,... | collective-permute-start | bytes 884744 | tf_op jit(solution)/shard_map/ppermute | solution.py:503
  176.8 9.6 %collective-permute-start.58 = (bf16[1056,128]{1,0:T(8,128)(2,1)S(1)}, bf16[1056,128]{1,0:T(8,128)(2,1)}, u32[]{:S(2)}, u32[]{:S(2)}) collective-permute-start(bf16[1056,128]{1,0:T(8,128)(2,1)S(1)} %collective-permute-done.50.refs_1_), channel_id=1, source_target_pairs={{0,8},{8,0},{16,24},{24,16},{1,9},{9,1},{17,25},{25,17},{2,10},{10... | collective-permute-start | bytes 811016 | tf_op jit(solution)/shard_map/ppermute | solution.py:513
  178.3 9.5 %collective-permute-start.59 = (bf16[1056,128]{1,0:T(8,128)(2,1)S(1)}, bf16[1056,128]{1,0:T(8,128)(2,1)}, u32[]{:S(2)}, u32[]{:S(2)}) collective-permute-start(bf16[1056,128]{1,0:T(8,128)(2,1)S(1)} %collective-permute-done.50.refs_1_), channel_id=1, source_target_pairs={{0,16},{8,24},{16,0},{24,8},{1,17},{9,25},{17,1},{25,9},{2,18},{10... | collective-permute-start | bytes 811016 | tf_op jit(solution)/shard_map/ppermute | solution.py:513
  179.4 14.1 %collective-permute-start.56 = (bf16[2400,128]{1,0:T(8,128)(2,1)S(1)}, bf16[2400,128]{1,0:T(8,128)(2,1)S(1)}, u32[]{:S(2)}, u32[]{:S(2)}) collective-permute-start(bf16[2400,128]{1,0:T(8,128)(2,1)S(1)} %collective-permute-done.43.refs_5_), channel_id=1, source_target_pairs={{0,8},{8,0},{16,24},{24,16},{1,9},{9,1},{17,25},{25,17},{2,10},{10... | collective-permute-start | bytes 1843208 | tf_op jit(solution)/shard_map/ppermute | solution.py:513
  180.7 13.9 %collective-permute-start.57 = (bf16[2400,128]{1,0:T(8,128)(2,1)S(1)}, bf16[2400,128]{1,0:T(8,128)(2,1)S(1)}, u32[]{:S(2)}, u32[]{:S(2)}) collective-permute-start(bf16[2400,128]{1,0:T(8,128)(2,1)S(1)} %collective-permute-done.38.refs_2_), channel_id=1, source_target_pairs={{0,16},{8,24},{16,0},{24,8},{1,17},{9,25},{17,1},{25,9},{2,18},{10... | collective-permute-start | bytes 1843208 | tf_op jit(solution)/shard_map/ppermute | solution.py:513
  186.1 8.5 %collective-permute-start.53 = (bf16[2400,128]{1,0:T(8,128)(2,1)}, bf16[2400,128]{1,0:T(8,128)(2,1)S(1)}, u32[]{:S(2)}, u32[]{:S(2)}) collective-permute-start(bf16[2400,128]{1,0:T(8,128)(2,1)} %copy-done.1), channel_id=1, source_target_pairs={{0,1},{1,0},{2,3},{3,2},{4,5},{5,4},{6,7},{7,6},{8,9},{9,8},{10,11... | collective-permute-start | bytes 1843208 | tf_op jit(solution)/shard_map/ppermute | solution.py:508
  194.7 9.1 %collective-permute-start.60 = (bf16[2400,128]{1,0:T(8,128)(2,1)S(1)}, bf16[2400,128]{1,0:T(8,128)(2,1)S(1)}, u32[]{:S(2)}, u32[]{:S(2)}) collective-permute-start(bf16[2400,128]{1,0:T(8,128)(2,1)S(1)} %collective-permute-done.56.refs_7_), channel_id=1, source_target_pairs={{0,1},{1,0},{2,3},{3,2},{4,5},{5,4},{6,7},{7,6},{8,9},{9,8},{10,11... | collective-permute-start | bytes 1843208 | tf_op jit(solution)/shard_map/ppermute | solution.py:508
  194.7 9.0 %collective-permute-start.61 = (bf16[2400,128]{1,0:T(8,128)(2,1)S(1)}, bf16[2400,128]{1,0:T(8,128)(2,1)S(1)}, u32[]{:S(2)}, u32[]{:S(2)}) collective-permute-start(bf16[2400,128]{1,0:T(8,128)(2,1)S(1)} %collective-permute-done.57.refs_6_), channel_id=1, source_target_pairs={{0,1},{1,0},{2,3},{3,2},{4,5},{5,4},{6,7},{7,6},{8,9},{9,8},{10,11... | collective-permute-start | bytes 1843208 | tf_op jit(solution)/shard_map/ppermute | solution.py:508
  195.2 8.5 %collective-permute-start.62 = (bf16[1056,128]{1,0:T(8,128)(2,1)S(1)}, bf16[1056,128]{1,0:T(8,128)(2,1)S(1)}, u32[]{:S(2)}, u32[]{:S(2)}) collective-permute-start(bf16[1056,128]{1,0:T(8,128)(2,1)S(1)} %copy-done.44), channel_id=1, source_target_pairs={{0,16},{8,24},{16,0},{24,8},{1,17},{9,25},{17,1},{25,9},{2,18},{10... | collective-permute-start | bytes 811016 | tf_op jit(solution)/shard_map/ppermute | solution.py:513
  197.0 18.4 %collective-permute-start.64 = (bf16[1056,128]{1,0:T(8,128)(2,1)}, bf16[1056,128]{1,0:T(8,128)(2,1)S(1)}, u32[]{:S(2)}, u32[]{:S(2)}) collective-permute-start(bf16[1056,128]{1,0:T(8,128)(2,1)} %collective-permute-done.59.refs_5_), channel_id=1, source_target_pairs={{0,8},{8,0},{16,24},{24,16},{1,9},{9,1},{17,25},{25,17},{2,10},{10... | collective-permute-start | bytes 811016 | tf_op jit(solution)/shard_map/ppermute | solution.py:513
  203.7 12.1 %collective-permute-start.65 = (bf16[1056,128]{1,0:T(8,128)(2,1)S(1)}, bf16[1056,128]{1,0:T(8,128)(2,1)S(1)}, u32[]{:S(2)}, u32[]{:S(2)}) collective-permute-start(bf16[1056,128]{1,0:T(8,128)(2,1)S(1)} %collective-permute-done.50.refs_1_), channel_id=1, source_target_pairs={{0,1},{1,0},{2,3},{3,2},{4,5},{5,4},{6,7},{7,6},{8,9},{9,8},{10,11... | collective-permute-start | bytes 811016 | tf_op jit(solution)/shard_map/ppermute | solution.py:508
  203.8 12.2 %collective-permute-start.66 = (bf16[1056,128]{1,0:T(8,128)(2,1)}, bf16[1056,128]{1,0:T(8,128)(2,1)S(1)}, u32[]{:S(2)}, u32[]{:S(2)}) collective-permute-start(bf16[1056,128]{1,0:T(8,128)(2,1)} %collective-permute-done.58.refs_3_), channel_id=1, source_target_pairs={{0,1},{1,0},{2,3},{3,2},{4,5},{5,4},{6,7},{7,6},{8,9},{9,8},{10,11... | collective-permute-start | bytes 811016 | tf_op jit(solution)/shard_map/ppermute | solution.py:508
  204.3 12.1 %collective-permute-start.67 = (bf16[1056,128]{1,0:T(8,128)(2,1)}, bf16[1056,128]{1,0:T(8,128)(2,1)S(1)}, u32[]{:S(2)}, u32[]{:S(2)}) collective-permute-start(bf16[1056,128]{1,0:T(8,128)(2,1)} %collective-permute-done.59.refs_5_), channel_id=1, source_target_pairs={{0,1},{1,0},{2,3},{3,2},{4,5},{5,4},{6,7},{7,6},{8,9},{9,8},{10,11... | collective-permute-start | bytes 811016 | tf_op jit(solution)/shard_map/ppermute | solution.py:508
  204.4 10.8 %collective-permute-start.63 = (f32[72,128]{1,0:T(8,128)S(1)}, f32[72,128]{1,0:T(8,128)S(1)}, u32[]{:S(2)}, u32[]{:S(2)}) collective-permute-start(f32[72,128]{1,0:T(8,128)S(1)} %add.103), channel_id=1, source_target_pairs={{0,4},{1,5},{2,6},{3,7},{4,0},{5,1},{6,2},{7,3},{8,12},{9,13},{10,... | collective-permute-start | bytes 110600 | tf_op jit(solution)/shard_map/ppermute | solution.py:503
  (98 other events, 1020.5 us)
